TPU v7x, 32 devices: a whole 2x2x4 slice. The times are simulated.
32 devices in a mesh: row: 4 (over x, core), sector: 8 (over z, y).
Axes of the slice: x: 2, y: 2, z: 4, core: 2. Of those that a mesh axis runs over, the one named last changes fastest.
Arguments:
- state: float32 [6, 256, 128, 128], P(None, 'row', 'sector'), may hold values from -6 to 6
- interp_blocks: float32 [16, 16, 32], replicated, may hold values from -0.1 to 0.8
- rotor_offset: int32 [4, 3], replicated, may hold values from 0 to 127
- axial_speed: float32 [6], replicated, may hold values from 0.3 to 1.5
- row_swirl: float32 [4], P('row'), may hold values from -1.5 to 1.5
- diffusivity: float32 [6], replicated, may hold values from 0.05 to 0.3
- coupling: float32 [6, 6], replicated, may hold values from -1.5 to 1.5
Outputs:
- advanced: float32 [6, 256, 128, 128], P(None, 'row', 'sector')
All inputs are finite; a program needn't handle non-finite values.
Results may differ from a plain program's by a relative error of at most 0.0001.
Values sent between devices are 32-bit elements; how exact they have to be, the bound alone decides.
No kernel may reach another device: no remote copies, remote signals or barrier semaphores. Data moves between devices by JAX's collectives and lax.ppermute only.
A program may use at most 128 MiB of HBM per device.

v0:
```python
import functools

import jax
import jax.numpy as jnp
from jax import lax
from jax.experimental import pallas as pl
from jax.experimental.pallas import tpu as pltpu
from jax.sharding import PartitionSpec as P

time_step = 0.4
highest = lax.Precision.HIGHEST
VMEM = pltpu.VMEM
SMEM = pltpu.SMEM
LOW = 8


def whole(space):
    return pl.BlockSpec(memory_space=space)


def held(shape):
    return pltpu.VMEM(tuple(shape), jnp.float32)


def near(value):
    return pltpu.with_memory_space_constraint(value, pltpu.VMEM)


def params():
    return pltpu.CompilerParams(vmem_limit_bytes=16 * 1024 * 1024)


class Plan:
    def __init__(self, state, sectors):
        self.fields, self.axial, self.cycle, self.radial = state.shape
        self.sectors = sectors
        strip = self.axial // 4
        self.outer = ((0, strip), (self.axial - strip, self.axial))
        self.inner = ((strip, self.axial - strip),)
        self.half = sectors // 2
        self.per = -(-2 * self.fields // self.half)
        self.dealt = (sectors, self.per, self.cycle, self.radial)

    def combo(self, side, field, plane):
        place = side * self.per * self.half + field * 2 + plane
        return place // self.per, place % self.per


def count(ranges):
    return sum(high - low for low, high in ranges)


def write_edges(plan, value, field, place, low_ref, high_ref):
    tile, row = place
    low_ref[field, tile, row : row + 2, :] = value[:2]
    high_ref[field, tile, row : row + 2, :] = value[plan.cycle - 2 :]


def gather_planes(plan, buffer, upper, lower):
    for field in range(plan.fields):
        for plane in range(2):
            piece, slot = plan.combo(0, field, plane)
            buffer[piece, slot] = upper(field, plane)
            piece, slot = plan.combo(1, field, plane)
            buffer[piece, slot] = lower(field, plane)


def clear_spare(plan, buffer):
    used = {plan.combo(side, field, plane) for side in range(2) for field in range(plan.fields) for plane in range(2)}
    for piece in range(plan.sectors):
        for slot in range(plan.per):
            if (piece, slot) not in used:
                buffer[piece, slot] = jnp.zeros((plan.cycle, plan.radial), jnp.float32)


def planes_kernel(plan, state, dealt, planes, sems):
    copies = [
        pltpu.make_async_copy(state.at[:, plan.axial - 2 : plan.axial], planes.at[0], sems.at[0]),
        pltpu.make_async_copy(state.at[:, 0:2], planes.at[1], sems.at[1]),
    ]
    for item in copies:
        item.start()
    clear_spare(plan, dealt)
    for item in copies:
        item.wait()
    gather_planes(plan, dealt, lambda f, p: planes[0, f, p], lambda f, p: planes[1, f, p])


def first_planes(plan, state):
    return pl.pallas_call(
        functools.partial(planes_kernel, plan),
        in_specs=[whole(pl.ANY)],
        out_specs=whole(VMEM),
        out_shape=held(plan.dealt),
        scratch_shapes=[
            held((2, plan.fields, 2, plan.cycle, plan.radial)),
            pltpu.SemaphoreType.DMA((2,)),
        ],
        compiler_params=params(),
        name="first_planes",
    )(state)


def first_kernel(plan, state, lo_o, hi_o, lo_i, hi_i):
    for ranges, low_ref, high_ref in ((plan.outer, lo_o, hi_o), (plan.inner, lo_i, hi_i)):
        start = 0
        for low, high in ranges:

            def body(tile, carry, low=low, start=start, low_ref=low_ref, high_ref=high_ref):
                for field in range(plan.fields):
                    for step in range(4):
                        at = low + tile * 4 + step
                        low_ref[field, start + tile, 2 * step : 2 * step + 2, :] = state[field, at, 0:2, :]
                        high_ref[field, start + tile, 2 * step : 2 * step + 2, :] = state[
                            field, at, plan.cycle - 2 : plan.cycle, :
                        ]
                return carry

            lax.fori_loop(0, (high - low) // 4, body, 0)
            start += (high - low) // 4


def edge_shape(plan, ranges):
    return held((plan.fields, count(ranges) // 4, 8, plan.radial))


def first_edges(plan, state):
    return pl.pallas_call(
        functools.partial(first_kernel, plan),
        in_specs=[whole(VMEM)],
        out_specs=[whole(VMEM)] * 4,
        out_shape=[edge_shape(plan, ranges) for ranges in (plan.outer, plan.outer, plan.inner, plan.inner)],
        compiler_params=params(),
        name="first_edges",
    )(state)


def interp_kernel(plan, section, place, offsets, weights, ring, *refs):
    *_, out, spread = refs
    full = plan.cycle * plan.sectors
    row, sector = place[0], place[1]
    up = sector < plan.half
    at = jnp.where(up, jnp.minimum(row, offsets.shape[1] - 1), jnp.maximum(row - 1, 0))
    offset = offsets[section, at]
    offset = jnp.where(up, offset, lax.rem(full - offset, full))
    turn = offset // plan.cycle
    cell = lax.rem(offset, plan.cycle)
    matrix = weights[cell]
    for k in range(2 * plan.cycle):
        spread[k] = jnp.broadcast_to(matrix[:, k : k + 1], (plan.cycle, plan.radial))
    for target in range(plan.sectors):
        here = lax.rem(target + turn, plan.sectors)
        after = lax.rem(here + 1, plan.sectors)
        for slot in range(plan.per):
            total = None
            for k in range(2 * plan.cycle):
                cell_at = k % plan.cycle
                row_value = ring[here if k < plan.cycle else after, slot, cell_at : cell_at + 1, :]
                term = spread[k] * jnp.broadcast_to(row_value, (plan.cycle, plan.radial))
                total = term if total is None else total + term
            out[target, slot] = total


def interp(plan, section, place, offsets, weights, got, after):
    operands = [place, offsets, weights, near(got), *map(near, after)]
    return pl.pallas_call(
        functools.partial(interp_kernel, plan, section),
        in_specs=[whole(SMEM), whole(SMEM)] + [whole(VMEM)] * (len(operands) - 2),
        out_specs=whole(VMEM),
        out_shape=held(plan.dealt),
        scratch_shapes=[held((2 * plan.cycle, plan.cycle, plan.radial))],
        compiler_params=params(),
        name="interpolate",
    )(*operands)


def coefficients(plan, speed, swirl, diffusion, coupling):
    twelfth = 1.0 / 12.0
    w = swirl[0]
    table = []
    for f in range(plan.fields):
        v, d = speed[f], diffusion[f]
        axial = ((-v - d) * twelfth, (8.0 * v + 16.0 * d) * twelfth, (16.0 * d - 8.0 * v) * twelfth, (v - d) * twelfth)
        cycle = ((-w - d) * twelfth, (8.0 * w + 16.0 * d) * twelfth, (16.0 * d - 8.0 * w) * twelfth, (w - d) * twelfth)
        mix = [coupling[f, e] - 7.0 * d if e == f else coupling[f, e] for e in range(plan.fields)]
        table.append((axial, cycle, d, mix))
    return table


def stage_kernel(plan, stage, outer, speed, swirl, diffusion, coupling, *refs):
    refs = list(refs)
    take = lambda number: [refs.pop(0) for _ in range(number)]
    ranges = plan.outer if outer else plan.inner
    (state,) = take(1)
    chunks = {"state": state} if stage == 0 else dict(zip(("outer", "inner"), take(2)))
    low_in, high_in = take(2)
    if outer:
        (ghosts,) = take(1)
    else:
        take(1)
    if stage == 3:
        older = take(2)
        if not outer:
            take(1)
        (out_any,) = take(1)
        if outer:
            (token,) = take(1)
        out_buf, sem = take(2)
    else:
        out, low_out, high_out, token = take(4)
        if outer:
            (dealt,) = take(1)
    work, spread = take(2)
    cycle, radial = plan.cycle, plan.radial
    terms = plan.fields + 9
    for f, (axial, around, d, mix) in enumerate(coefficients(plan, speed, swirl, diffusion, coupling)):
        for number, factor in enumerate((d, *mix, *axial, *around)):
            spread[f * terms + number] = jnp.full((8, radial), factor, jnp.float32)
    lane = lax.broadcasted_iota(jnp.int32, (8, radial), 1)
    not_first = lane > 0
    not_last = lane < radial - 1

    def source(at):
        if at < 0:
            return ghosts, 0, at + 2
        if at >= plan.axial:
            return ghosts, 1, at - plan.axial
        if stage == 0:
            return state, None, at
        start = 0
        for low, high in plan.outer:
            if low <= at < high:
                return chunks["outer"], None, start + at - low
            start += high - low
        return chunks["inner"], None, at - plan.inner[0][0]

    def fill(field, at, to):
        ref, side, place = source(at)
        if side is not None:
            piece, slot = plan.combo(side, field, place)
            work[field, to, LOW : LOW + cycle, :] = ref[piece, slot]
        else:
            work[field, to, LOW : LOW + cycle, :] = ref[field, place]

    begin = 0
    for low, high in ranges:
        size = high - low
        for field in range(plan.fields):
            for at, to in ((low - 2, 0), (low - 1, 1), (high, size + 2), (high + 1, size + 3)):
                fill(field, at, to)
        ref, _, first_place = source(low)

        def copy(tile, carry, ref=ref, first_place=first_place, begin=begin):
            for field in range(plan.fields):
                for step in range(4):
                    place = tile * 4 + step
                    work[field, place + 2, LOW : LOW + cycle, :] = ref[field, first_place + place]
                    work[field, place + 2, LOW - 2 : LOW, :] = low_in[field, begin // 4 + tile, 2 * step : 2 * step + 2, :]
                    work[field, place + 2, LOW + cycle : LOW + cycle + 2, :] = high_in[
                        field, begin // 4 + tile, 2 * step : 2 * step + 2, :
                    ]
            return carry

        lax.fori_loop(0, size // 4, copy, 0)

        def compute(tile, carry, low=low, begin=begin):
            for f in range(plan.fields):
                factors = [spread[f * terms + number] for number in range(terms)]
                values = {}
                for step in range(4):
                    at = tile * 4 + step + 2
                    for row in range(0, cycle, 8):
                        here = slice(LOW + row, LOW + row + 8)
                        center = work[f, at, here, :]
                        left = jnp.where(not_first, pltpu.roll(center, 1, 1), 0.0)
                        right = jnp.where(not_last, pltpu.roll(center, radial - 1, 1), 0.0)
                        total = factors[0] * (left + right)
                        for e in range(plan.fields):
                            total += factors[1 + e] * (center if e == f else work[e, at, here, :])
                        for number, by in enumerate((-2, -1, 1, 2)):
                            total += factors[1 + plan.fields + number] * work[f, at + by, here, :]
                            total += factors[5 + plan.fields + number] * work[f, at, LOW + row + by : LOW + row + by + 8, :]
                        place = begin + tile * 4 + step
                        base = state[f, low + tile * 4 + step, row : row + 8, :]
                        if stage == 3:
                            second, third = older
                            kept = second[f, place, row : row + 8, :] + 2.0 * third[f, place, row : row + 8, :]
                            value = (kept + center - base) * (1.0 / 3.0) + (time_step / 6.0) * total
                        else:
                            value = base + (time_step if stage == 2 else 0.5 * time_step) * total
                        values[step, row] = value
                for (step, row), value in values.items():
                    place = begin + tile * 4 + step
                    if stage == 3:
                        out_buf[f, place, row : row + 8, :] = value
                        continue
                    out[f, place, row : row + 8, :] = value
                    if row == 0:
                        low_out[f, begin // 4 + tile, 2 * step : 2 * step + 2, :] = value[:2]
                    if row == cycle - 8:
                        high_out[f, begin // 4 + tile, 2 * step : 2 * step + 2, :] = value[6:]
            return carry

        lax.fori_loop(0, size // 4, compute, 0)
        begin += size

    if stage == 3:
        begin = 0
        copies = []
        for number, (low, high) in enumerate(ranges):
            copies.append(
                pltpu.make_async_copy(
                    out_buf.at[:, begin : begin + high - low], out_any.at[:, low:high], sem.at[number]
                )
            )
            copies[-1].start()
            begin += high - low
        for item in copies:
            item.wait()
    elif outer:
        total = count(ranges)
        clear_spare(plan, dealt)
        gather_planes(plan, dealt, lambda f, p: out[f, total - 2 + p], lambda f, p: out[f, p])
    if stage < 3 or outer:
        token[...] = jnp.zeros(token.shape, jnp.float32)


def stage_call(plan, stage, outer, scalars, state, chunks, halos, extra, older=(), whole_out=None):
    ranges = plan.outer if outer else plan.inner
    chunk = (plan.fields, count(ranges), plan.cycle, plan.radial)
    longest = max(high - low for low, high in ranges)
    operands, specs = list(scalars), [whole(SMEM)] * len(scalars)

    def add(values):
        operands.extend(map(near, values))
        specs.extend([whole(VMEM)] * len(values))

    add([state, *(chunks or ()), *halos, extra])
    scratch = [
        held((plan.fields, longest + 4, plan.cycle + 16, plan.radial)),
        held((plan.fields * (plan.fields + 9), 8, plan.radial)),
    ]
    aliases = {}
    token = held((8, plan.radial))
    if stage == 3:
        add(older)
        if whole_out is not None:
            aliases = {len(operands): 0}
            operands.append(whole_out)
            specs.append(whole(pl.ANY))
        out_shape = [jax.ShapeDtypeStruct(state.shape, jnp.float32)] + [token] * outer
        out_specs = [whole(pl.ANY)] + [whole(VMEM)] * outer
        scratch = [held(chunk), pltpu.SemaphoreType.DMA((len(ranges),))] + scratch
    else:
        out_shape = [held(chunk), edge_shape(plan, ranges), edge_shape(plan, ranges), token]
        if outer:
            out_shape.append(held(plan.dealt))
        out_specs = [whole(VMEM)] * len(out_shape)
    return pl.pallas_call(
        functools.partial(stage_kernel, plan, stage, outer),
        in_specs=specs,
        out_specs=out_specs,
        out_shape=out_shape,
        scratch_shapes=scratch,
        input_output_aliases=aliases,
        compiler_params=params(),
        name=f"stage{stage}_{'outer' if outer else 'inner'}",
    )(*operands)


def exchange(edges):
    size = lax.axis_size("sector")
    ahead = [(i, (i + 1) % size) for i in range(size)]
    back = [(i, (i - 1) % size) for i in range(size)]
    low_edges, high_edges = edges
    return lax.ppermute(high_edges, "sector", ahead), lax.ppermute(low_edges, "sector", back)


def row_hop(plan, value):
    rows = lax.axis_size("row")
    route = []
    for row in range(rows):
        for sector in range(plan.sectors):
            target = row + 1 if sector < plan.half else row - 1
            if 0 <= target < rows:
                route.append((row * plan.sectors + sector, target * plan.sectors + sector))
    return lax.ppermute(value, ("row", "sector"), route)


def on_device(state, interp_blocks, rotor_offset, axial_speed, row_swirl, diffusivity, coupling):
    plan = Plan(state, lax.axis_size("sector"))
    place = jnp.stack([lax.axis_index("row"), lax.axis_index("sector")]).astype(jnp.int32)
    scalars = (axial_speed, row_swirl, diffusivity, coupling)

    dealt = first_planes(plan, state)
    lo_o, hi_o, lo_i, hi_i = first_edges(plan, state)
    outer_edges, inner_edges = (lo_o, hi_o), (lo_i, hi_i)
    chunks, waited = None, ()
    history = []
    for stage in range(4):
        got = lax.all_to_all(dealt, "sector", 0, 0, tiled=True)
        outer_halos = exchange(outer_edges)
        made = interp(plan, stage, place, rotor_offset, interp_blocks, got, waited)
        hopped = row_hop(plan, made)
        ghosts = lax.all_to_all(hopped, "sector", 0, 0, tiled=True)
        inner_edges = lax.optimization_barrier((*inner_edges, ghosts))[:2]
        inner_halos = exchange(inner_edges)
        last = stage == 3
        older = [(history[0][i], history[1][i]) if last else () for i in range(2)]
        out_o, *rest = stage_call(plan, stage, True, scalars, state, chunks, outer_halos, ghosts, older[0])
        token = rest[0] if last else rest[2]
        out_i, *rest_i = stage_call(
            plan, stage, False, scalars, state, chunks, inner_halos, token, older[1], out_o if last else None
        )
        if last:
            return out_i
        outer_edges, dealt = rest[:2], rest[3]
        inner_edges, waited = rest_i[:2], rest_i[2:]
        chunks = (out_o, out_i)
        history.append(chunks)


def solution(mesh):
    return jax.shard_map(
        on_device,
        mesh=mesh,
        in_specs=(P(None, "row", "sector", None), P(), P(), P(), P("row"), P(), P()),
        out_specs=P(None, "row", "sector", None),
        check_vma=False,
    )
```

profile of v0, /device:TPU:1, one launch (start us, length us, event | category | flops | bytes accessed | tf_op | source)
XLA Modules:
  0.0 247.0 jit_solution(9723480765590843217)
XLA Ops:
  0.0 1.9 copy-done
  2.7 6.5 %all-to-all-start = ((f32[8,3,16,128]{3,2,1,0:T(8,128)}), f32[8,3,16,128]{3,2,1,0:T(8,128)S(1)}, u32[]{:S(2)}, u32[]{:S(2)}) async-start(f32[8,3,16,128]{3,2,1,0:T(8,128)} %first_planes.1), calls=%async_computation | async-start | bytes 393216 | tf_op jit(solution)/shard_map/all_to_all | solution.py:401
  9.3 6.6 %all-to-all-done.ring = f32[8,3,16,128]{3,2,1,0:T(8,128)S(1)} async-done(((f32[8,3,16,128]{3,2,1,0:T(8,128)}), f32[8,3,16,128]{3,2,1,0:T(8,128)S(1)}, u32[]{:S(2)}, u32[]{:S(2)}) %all-to-all-start) | async-done | bytes 196640 | tf_op jit(solution)/shard_map/all_to_all | solution.py:401
  17.0 5.2 %collective-permute-start.2 = (f32[8,3,16,128]{3,2,1,0:T(8,128)S(1)}, f32[8,3,16,128]{3,2,1,0:T(8,128)}, u32[]{:S(2)}, u32[]{:S(2)}) collective-permute-start(f32[8,3,16,128]{3,2,1,0:T(8,128)S(1)} %interpolate.4), channel_id=1, source_target_pairs={{0,8},{1,9},{2,10},{3,11},{8,16},{9,17},{10,18},{11,19},{12,4},{13... | collective-permute-start | bytes 589832 | tf_op jit(solution)/shard_map/ppermute | solution.py:387
  22.3 2.6 %collective-permute-done.2 = f32[8,3,16,128]{3,2,1,0:T(8,128)} collective-permute-done((f32[8,3,16,128]{3,2,1,0:T(8,128)S(1)}, f32[8,3,16,128]{3,2,1,0:T(8,128)}, u32[]{:S(2)}, u32[]{:S(2)}) %collective-permute-start.2) | collective-permute-done | bytes 196640 | tf_op jit(solution)/shard_map/ppermute | solution.py:387
  24.9 3.7 %all-to-all-start.1 = ((f32[8,3,16,128]{3,2,1,0:T(8,128)}), f32[8,3,16,128]{3,2,1,0:T(8,128)S(1)}, u32[]{:S(2)}, u32[]{:S(2)}) async-start(f32[8,3,16,128]{3,2,1,0:T(8,128)} %collective-permute-done.2), calls=%async_computation.1 | async-start | bytes 393216 | tf_op jit(solution)/shard_map/all_to_all | solution.py:405
  31.8 2.7 %collective-permute-start.1 = (f32[6,8,8,128]{3,2,1,0:T(8,128)S(1)}, f32[6,8,8,128]{3,2,1,0:T(8,128)S(1)}, u32[]{:S(2)}, u32[]{:S(2)}) collective-permute-start(f32[6,8,8,128]{3,2,1,0:T(8,128)S(1)} %get-tuple-element.47), channel_id=1, source_target_pairs={{0,7},{1,0},{2,1},{3,2},{4,3},{5,4},{6,5},{7,6},{8,15},{9,8},{10,9... | collective-permute-start | bytes 589832 | tf_op jit(solution)/shard_map/ppermute | solution.py:376
  35.2 4.6 %collective-permute-done.refs_1_ = f32[6,8,8,128]{3,2,1,0:T(8,128)S(1)} collective-permute-done((f32[6,8,8,128]{3,2,1,0:T(8,128)S(1)}, f32[6,8,8,128]{3,2,1,0:T(8,128)S(1)}, u32[]{:S(2)}, u32[]{:S(2)}) %collective-permute-start) | collective-permute-done | bytes 196640 | tf_op jit(solution)/shard_map/ppermute | solution.py:376
  40.4 1.6 collective-permute-done.1.refs_2_
  44.6 3.5 %stage0_outer.1 = (f32[6,32,16,128]{3,2,1,0:T(8,128)S(1)}, f32[6,8,8,128]{3,2,1,0:T(8,128)S(1)}, f32[6,8,8,128]{3,2,1,0:T(8,128)S(1)}, f32[8,128]{1,0:T(8,128)S(1)}, f32[8,3,16,128]{3,2,1,0:T(8,128)S(1)}) custom-call(f32[6]{0:T(128)S(1)} %copy-done.39, f32[1]{0:T(128)S(6)} %copy.10.swirl, f32[6]{0:T(128)S(1)} %copy-done.40, f32[6,6]{1,0:T(8,128)S(1)} %copy-done.23, ...), custom_call_target="tpu_custom_call" | custom-call | tf_op jit(solution)/shard_map/stage0_outer/pallas_call | solution.py:359
  51.2 3.6 %all-to-all-start.2 = ((f32[8,3,16,128]{3,2,1,0:T(8,128)}), f32[8,3,16,128]{3,2,1,0:T(8,128)S(1)}, u32[]{:S(2)}, u32[]{:S(2)}) async-start(f32[8,3,16,128]{3,2,1,0:T(8,128)} %copy-done.24), calls=%async_computation.2 | async-start | bytes 393216 | tf_op jit(solution)/shard_map/all_to_all | solution.py:401
  54.8 1.5 collective-permute-start.3
  56.2 2.7 %collective-permute-start.4 = (f32[6,8,8,128]{3,2,1,0:T(8,128)}, f32[6,8,8,128]{3,2,1,0:T(8,128)S(1)}, u32[]{:S(2)}, u32[]{:S(2)}) collective-permute-start(f32[6,8,8,128]{3,2,1,0:T(8,128)} %copy-done.54), channel_id=1, source_target_pairs={{0,7},{1,0},{2,1},{3,2},{4,3},{5,4},{6,5},{7,6},{8,15},{9,8},{10,9... | collective-permute-start | bytes 589832 | tf_op jit(solution)/shard_map/ppermute | solution.py:376
  59.0 8.0 %collective-permute-done.3.refs_1_ = f32[6,8,8,128]{3,2,1,0:T(8,128)S(1)} collective-permute-done((f32[6,8,8,128]{3,2,1,0:T(8,128)}, f32[6,8,8,128]{3,2,1,0:T(8,128)S(1)}, u32[]{:S(2)}, u32[]{:S(2)}) %collective-permute-start.3) | collective-permute-done | bytes 196640 | tf_op jit(solution)/shard_map/ppermute | solution.py:376
  68.2 3.4 %stage0_inner.1 = (f32[6,32,16,128]{3,2,1,0:T(8,128)S(1)}, f32[6,8,8,128]{3,2,1,0:T(8,128)S(1)}, f32[6,8,8,128]{3,2,1,0:T(8,128)S(1)}, f32[8,128]{1,0:T(8,128)S(1)}) custom-call(f32[6]{0:T(128)S(1)} %copy-done.39, f32[1]{0:T(128)S(6)} %copy.10.swirl, f32[6]{0:T(128)S(1)} %copy-done.40, f32[6,6]{1,0:T(8,128)S(1)} %copy-done.23, ...), custom_call_target="tpu_custom_call" | custom-call | tf_op jit(solution)/shard_map/stage0_inner/pallas_call | solution.py:359
  75.3 1.9 collective-permute-start.7
  77.2 2.6 %collective-permute-done.7 = f32[8,3,16,128]{3,2,1,0:T(8,128)} collective-permute-done((f32[8,3,16,128]{3,2,1,0:T(8,128)S(1)}, f32[8,3,16,128]{3,2,1,0:T(8,128)}, u32[]{:S(2)}, u32[]{:S(2)}) %collective-permute-start.7) | collective-permute-done | bytes 196640 | tf_op jit(solution)/shard_map/ppermute | solution.py:387
  79.8 6.8 %all-to-all-start.3 = ((f32[8,3,16,128]{3,2,1,0:T(8,128)}), f32[8,3,16,128]{3,2,1,0:T(8,128)S(1)}, u32[]{:S(2)}, u32[]{:S(2)}) async-start(f32[8,3,16,128]{3,2,1,0:T(8,128)} %collective-permute-done.7), calls=%async_computation.3 | async-start | bytes 393216 | tf_op jit(solution)/shard_map/all_to_all | solution.py:405
  86.6 1.5 collective-permute-start.5
  88.1 2.7 %collective-permute-start.6 = (f32[6,8,8,128]{3,2,1,0:T(8,128)}, f32[6,8,8,128]{3,2,1,0:T(8,128)S(1)}, u32[]{:S(2)}, u32[]{:S(2)}) collective-permute-start(f32[6,8,8,128]{3,2,1,0:T(8,128)} %copy-done.49), channel_id=1, source_target_pairs={{0,7},{1,0},{2,1},{3,2},{4,3},{5,4},{6,5},{7,6},{8,15},{9,8},{10,9... | collective-permute-start | bytes 589832 | tf_op jit(solution)/shard_map/ppermute | solution.py:376
  90.8 6.4 %collective-permute-done.5.refs_3_ = f32[6,8,8,128]{3,2,1,0:T(8,128)S(1)} collective-permute-done((f32[6,8,8,128]{3,2,1,0:T(8,128)}, f32[6,8,8,128]{3,2,1,0:T(8,128)S(1)}, u32[]{:S(2)}, u32[]{:S(2)}) %collective-permute-start.5) | collective-permute-done | bytes 196640 | tf_op jit(solution)/shard_map/ppermute | solution.py:376
  104.2 3.5 %stage1_outer.1 = (f32[6,32,16,128]{3,2,1,0:T(8,128)S(1)}, f32[6,8,8,128]{3,2,1,0:T(8,128)S(1)}, f32[6,8,8,128]{3,2,1,0:T(8,128)S(1)}, f32[8,128]{1,0:T(8,128)S(1)}, f32[8,3,16,128]{3,2,1,0:T(8,128)S(1)}) custom-call(f32[6]{0:T(128)S(1)} %copy-done.39, f32[1]{0:T(128)S(6)} %copy.10.swirl, f32[6]{0:T(128)S(1)} %copy-done.40, f32[6,6]{1,0:T(8,128)S(1)} %copy-done.23, ...), custom_call_target="tpu_custom_call" | custom-call | tf_op jit(solution)/shard_map/stage1_outer/pallas_call | solution.py:359
  110.9 4.1 %all-to-all-start.4 = ((f32[8,3,16,128]{3,2,1,0:T(8,128)}), f32[8,3,16,128]{3,2,1,0:T(8,128)S(1)}, u32[]{:S(2)}, u32[]{:S(2)}) async-start(f32[8,3,16,128]{3,2,1,0:T(8,128)} %copy-done.25), calls=%async_computation.4 | async-start | bytes 393216 | tf_op jit(solution)/shard_map/all_to_all | solution.py:401
  115.0 1.5 collective-permute-start.8
  116.5 2.7 %collective-permute-start.9 = (f32[6,8,8,128]{3,2,1,0:T(8,128)}, f32[6,8,8,128]{3,2,1,0:T(8,128)S(1)}, u32[]{:S(2)}, u32[]{:S(2)}) collective-permute-start(f32[6,8,8,128]{3,2,1,0:T(8,128)} %copy-done.44), channel_id=1, source_target_pairs={{0,7},{1,0},{2,1},{3,2},{4,3},{5,4},{6,5},{7,6},{8,15},{9,8},{10,9... | collective-permute-start | bytes 589832 | tf_op jit(solution)/shard_map/ppermute | solution.py:376
  119.2 8.5 %collective-permute-done.8.refs_3_ = f32[6,8,8,128]{3,2,1,0:T(8,128)S(1)} collective-permute-done((f32[6,8,8,128]{3,2,1,0:T(8,128)}, f32[6,8,8,128]{3,2,1,0:T(8,128)S(1)}, u32[]{:S(2)}, u32[]{:S(2)}) %collective-permute-start.8) | collective-permute-done | bytes 196640 | tf_op jit(solution)/shard_map/ppermute | solution.py:376
  131.8 3.4 %stage1_inner.1 = (f32[6,32,16,128]{3,2,1,0:T(8,128)S(1)}, f32[6,8,8,128]{3,2,1,0:T(8,128)S(1)}, f32[6,8,8,128]{3,2,1,0:T(8,128)S(1)}, f32[8,128]{1,0:T(8,128)S(1)}) custom-call(f32[6]{0:T(128)S(1)} %copy-done.39, f32[1]{0:T(128)S(6)} %copy.10.swirl, f32[6]{0:T(128)S(1)} %copy-done.40, f32[6,6]{1,0:T(8,128)S(1)} %copy-done.23, ...), custom_call_target="tpu_custom_call" | custom-call | tf_op jit(solution)/shard_map/stage1_inner/pallas_call | solution.py:359
  138.9 1.9 collective-permute-start.12
  140.8 2.6 %collective-permute-done.12 = f32[8,3,16,128]{3,2,1,0:T(8,128)} collective-permute-done((f32[8,3,16,128]{3,2,1,0:T(8,128)S(1)}, f32[8,3,16,128]{3,2,1,0:T(8,128)}, u32[]{:S(2)}, u32[]{:S(2)}) %collective-permute-start.12) | collective-permute-done | bytes 196640 | tf_op jit(solution)/shard_map/ppermute | solution.py:387
  143.4 6.6 %all-to-all-start.5 = ((f32[8,3,16,128]{3,2,1,0:T(8,128)}), f32[8,3,16,128]{3,2,1,0:T(8,128)S(1)}, u32[]{:S(2)}, u32[]{:S(2)}) async-start(f32[8,3,16,128]{3,2,1,0:T(8,128)} %collective-permute-done.12), calls=%async_computation.5 | async-start | bytes 393216 | tf_op jit(solution)/shard_map/all_to_all | solution.py:405
  150.0 1.5 collective-permute-start.10
  151.4 2.7 %collective-permute-start.11 = (f32[6,8,8,128]{3,2,1,0:T(8,128)}, f32[6,8,8,128]{3,2,1,0:T(8,128)S(1)}, u32[]{:S(2)}, u32[]{:S(2)}) collective-permute-start(f32[6,8,8,128]{3,2,1,0:T(8,128)} %copy-done.50), channel_id=1, source_target_pairs={{0,7},{1,0},{2,1},{3,2},{4,3},{5,4},{6,5},{7,6},{8,15},{9,8},{10,9... | collective-permute-start | bytes 589832 | tf_op jit(solution)/shard_map/ppermute | solution.py:376
  154.2 6.2 %collective-permute-done.10.refs_3_ = f32[6,8,8,128]{3,2,1,0:T(8,128)S(1)} collective-permute-done((f32[6,8,8,128]{3,2,1,0:T(8,128)}, f32[6,8,8,128]{3,2,1,0:T(8,128)S(1)}, u32[]{:S(2)}, u32[]{:S(2)}) %collective-permute-start.10) | collective-permute-done | bytes 196640 | tf_op jit(solution)/shard_map/ppermute | solution.py:376
  167.4 3.5 %stage2_outer.1 = (f32[6,32,16,128]{3,2,1,0:T(8,128)S(1)}, f32[6,8,8,128]{3,2,1,0:T(8,128)S(1)}, f32[6,8,8,128]{3,2,1,0:T(8,128)S(1)}, f32[8,128]{1,0:T(8,128)S(1)}, f32[8,3,16,128]{3,2,1,0:T(8,128)S(1)}) custom-call(f32[6]{0:T(128)S(1)} %copy-done.39, f32[1]{0:T(128)S(6)} %copy.10.swirl, f32[6]{0:T(128)S(1)} %copy-done.40, f32[6,6]{1,0:T(8,128)S(1)} %copy-done.23, ...), custom_call_target="tpu_custom_call" | custom-call | tf_op jit(solution)/shard_map/stage2_outer/pallas_call | solution.py:359
  174.1 4.2 %all-to-all-start.6 = ((f32[8,3,16,128]{3,2,1,0:T(8,128)}), f32[8,3,16,128]{3,2,1,0:T(8,128)S(1)}, u32[]{:S(2)}, u32[]{:S(2)}) async-start(f32[8,3,16,128]{3,2,1,0:T(8,128)} %copy-done.26), calls=%async_computation.6 | async-start | bytes 393216 | tf_op jit(solution)/shard_map/all_to_all | solution.py:401
  179.7 2.7 %collective-permute-start.14 = (f32[6,8,8,128]{3,2,1,0:T(8,128)}, f32[6,8,8,128]{3,2,1,0:T(8,128)S(1)}, u32[]{:S(2)}, u32[]{:S(2)}) collective-permute-start(f32[6,8,8,128]{3,2,1,0:T(8,128)} %copy-done.45), channel_id=1, source_target_pairs={{0,7},{1,0},{2,1},{3,2},{4,3},{5,4},{6,5},{7,6},{8,15},{9,8},{10,9... | collective-permute-start | bytes 589832 | tf_op jit(solution)/shard_map/ppermute | solution.py:376
  182.4 8.6 %collective-permute-done.13.refs_3_ = f32[6,8,8,128]{3,2,1,0:T(8,128)S(1)} collective-permute-done((f32[6,8,8,128]{3,2,1,0:T(8,128)}, f32[6,8,8,128]{3,2,1,0:T(8,128)S(1)}, u32[]{:S(2)}, u32[]{:S(2)}) %collective-permute-start.13) | collective-permute-done | bytes 196640 | tf_op jit(solution)/shard_map/ppermute | solution.py:376
  195.1 3.4 %stage2_inner.1 = (f32[6,32,16,128]{3,2,1,0:T(8,128)S(1)}, f32[6,8,8,128]{3,2,1,0:T(8,128)S(1)}, f32[6,8,8,128]{3,2,1,0:T(8,128)S(1)}, f32[8,128]{1,0:T(8,128)S(1)}) custom-call(f32[6]{0:T(128)S(1)} %copy-done.39, f32[1]{0:T(128)S(6)} %copy.10.swirl, f32[6]{0:T(128)S(1)} %copy-done.40, f32[6,6]{1,0:T(8,128)S(1)} %copy-done.23, ...), custom_call_target="tpu_custom_call" | custom-call | tf_op jit(solution)/shard_map/stage2_inner/pallas_call | solution.py:359
  202.3 1.9 collective-permute-start.15
  204.2 2.6 %collective-permute-done.15 = f32[8,3,16,128]{3,2,1,0:T(8,128)} collective-permute-done((f32[8,3,16,128]{3,2,1,0:T(8,128)S(1)}, f32[8,3,16,128]{3,2,1,0:T(8,128)}, u32[]{:S(2)}, u32[]{:S(2)}) %collective-permute-start.15) | collective-permute-done | bytes 196640 | tf_op jit(solution)/shard_map/ppermute | solution.py:387
  206.8 6.6 %all-to-all-start.7 = ((f32[8,3,16,128]{3,2,1,0:T(8,128)}), f32[8,3,16,128]{3,2,1,0:T(8,128)S(1)}, u32[]{:S(2)}, u32[]{:S(2)}) async-start(f32[8,3,16,128]{3,2,1,0:T(8,128)} %collective-permute-done.15), calls=%async_computation.7 | async-start | bytes 393216 | tf_op jit(solution)/shard_map/all_to_all | solution.py:405
  213.3 1.5 collective-permute-start.18
  214.8 2.7 %collective-permute-start.19 = (f32[6,8,8,128]{3,2,1,0:T(8,128)}, f32[6,8,8,128]{3,2,1,0:T(8,128)}, u32[]{:S(2)}, u32[]{:S(2)}) collective-permute-start(f32[6,8,8,128]{3,2,1,0:T(8,128)} %copy-done.42), channel_id=1, source_target_pairs={{0,7},{1,0},{2,1},{3,2},{4,3},{5,4},{6,5},{7,6},{8,15},{9,8},{10,9... | collective-permute-start | bytes 589832 | tf_op jit(solution)/shard_map/ppermute | solution.py:376
  217.5 4.0 %all-to-all-done.7.refs_5_ = f32[8,3,16,128]{3,2,1,0:T(8,128)S(1)} async-done(((f32[8,3,16,128]{3,2,1,0:T(8,128)}), f32[8,3,16,128]{3,2,1,0:T(8,128)S(1)}, u32[]{:S(2)}, u32[]{:S(2)}) %all-to-all-start.7) | async-done | bytes 196640 | tf_op jit(solution)/shard_map/all_to_all | solution.py:405
  221.6 3.2 %collective-permute-start.16 = (f32[6,8,8,128]{3,2,1,0:T(8,128)}, f32[6,8,8,128]{3,2,1,0:T(8,128)S(1)}, u32[]{:S(2)}, u32[]{:S(2)}) collective-permute-start(f32[6,8,8,128]{3,2,1,0:T(8,128)} %copy-done.51), channel_id=1, source_target_pairs={{0,1},{1,2},{2,3},{3,4},{4,5},{5,6},{6,7},{7,0},{8,9},{9,10},{10,1... | collective-permute-start | bytes 589832 | tf_op jit(solution)/shard_map/ppermute | solution.py:376
  226.7 4.7 %collective-permute-done.19.refs_4_ = f32[6,8,8,128]{3,2,1,0:T(8,128)} collective-permute-done((f32[6,8,8,128]{3,2,1,0:T(8,128)}, f32[6,8,8,128]{3,2,1,0:T(8,128)}, u32[]{:S(2)}, u32[]{:S(2)}) %collective-permute-start.19) | collective-permute-done | bytes 196640 | tf_op jit(solution)/shard_map/ppermute | solution.py:376
  237.1 5.2 %stage3_outer.1 = (f32[6,64,16,128]{3,2,1,0:T(8,128)}, f32[8,128]{1,0:T(8,128)S(1)}) custom-call(f32[6]{0:T(128)S(1)} %copy-done.39, f32[1]{0:T(128)S(6)} %copy.10.swirl, f32[6]{0:T(128)S(1)} %copy-done.40, f32[6,6]{1,0:T(8,128)S(1)} %copy-done.23, f32[6,64,16,128]{3,2,1,0:T(8,128)S(1)} %copy-done.1, f32[6,32,16,128]{3,2,1,0:T(8,128)S(1)} %copy-done.19, ...), custom_call_target="tpu_custom_call" | custom-call | tf_op jit(solution)/shard_map/stage3_outer/pallas_call | solution.py:359
  242.3 4.6 %stage3_inner.1 = f32[6,64,16,128]{3,2,1,0:T(8,128)} custom-call(f32[6]{0:T(128)S(1)} %copy-done.39, f32[1]{0:T(128)S(6)} %copy.10.swirl, f32[6]{0:T(128)S(1)} %copy-done.40, f32[6,6]{1,0:T(8,128)S(1)} %copy-done.23, f32[6,64,16,128]{3,2,1,0:T(8,128)S(1)} %copy-done.1, f32[6,32,16,128]{3,2,1,0:T(8,128)S(1)} %copy-done.19, ...), custom_call_target="tpu_custom_call", output_to_operand_aliasing={{}: (12, {})} | custom-call | tf_op jit(solution)/shard_map/stage3_inner/pallas_call | solution.py:359
  (135 shorter events, 61.4 us)
Async XLA Ops:
  0.0 1.9 copy-start
  1.9 14.0 %copy-start.22 = (f32[16,16,32]{2,1,0:T(8,128)S(1)}, f32[16,16,32]{2,1,0:T(8,128)}, u32[]{:S(2)}) copy-start(f32[16,16,32]{2,1,0:T(8,128)} %weights.7) | copy-start | bytes 98308
  1.9 14.0 %copy-start.41 = (s32[4,3]{1,0:T(4,128)S(1)}, s32[4,3]{1,0:T(4,128)}, u32[]{:S(2)}) copy-start(s32[4,3]{1,0:T(4,128)} %offsets.7) | copy-start | bytes 148
  1.9 26.7 %copy-start.1 = (f32[6,64,16,128]{3,2,1,0:T(8,128)S(1)}, f32[6,64,16,128]{3,2,1,0:T(8,128)}, u32[]{:S(2)}) copy-start(f32[6,64,16,128]{3,2,1,0:T(8,128)} %refs_0_.15) | copy-start | bytes 9437188
  2.7 13.2 %all-to-all-start = ((f32[8,3,16,128]{3,2,1,0:T(8,128)}), f32[8,3,16,128]{3,2,1,0:T(8,128)S(1)}, u32[]{:S(2)}, u32[]{:S(2)}) async-start(f32[8,3,16,128]{3,2,1,0:T(8,128)} %first_planes.1), calls=%async_computation | async-start | bytes 393216 | tf_op jit(solution)/shard_map/all_to_all | solution.py:401
  17.0 7.8 %collective-permute-start.2 = (f32[8,3,16,128]{3,2,1,0:T(8,128)S(1)}, f32[8,3,16,128]{3,2,1,0:T(8,128)}, u32[]{:S(2)}, u32[]{:S(2)}) collective-permute-start(f32[8,3,16,128]{3,2,1,0:T(8,128)S(1)} %interpolate.4), channel_id=1, source_target_pairs={{0,8},{1,9},{2,10},{3,11},{8,16},{9,17},{10,18},{11,19},{12,4},{13... | collective-permute-start | bytes 589832 | tf_op jit(solution)/shard_map/ppermute | solution.py:387
  24.9 17.8 %all-to-all-start.1 = ((f32[8,3,16,128]{3,2,1,0:T(8,128)}), f32[8,3,16,128]{3,2,1,0:T(8,128)S(1)}, u32[]{:S(2)}, u32[]{:S(2)}) async-start(f32[8,3,16,128]{3,2,1,0:T(8,128)} %collective-permute-done.2), calls=%async_computation.1 | async-start | bytes 393216 | tf_op jit(solution)/shard_map/all_to_all | solution.py:405
  28.6 14.1 %copy-start.23 = (f32[6,6]{1,0:T(8,128)S(1)}, f32[6,6]{1,0:T(8,128)}, u32[]{:S(2)}) copy-start(f32[6,6]{1,0:T(8,128)} %coupling.15) | copy-start | bytes 436
  28.6 14.1 %copy-start.39 = (f32[6]{0:T(128)S(1)}, f32[6]{0:T(128)}, u32[]{:S(2)}) copy-start(f32[6]{0:T(128)} %speed.15) | copy-start | bytes 76
  28.6 14.1 %copy-start.40 = (f32[6]{0:T(128)S(1)}, f32[6]{0:T(128)}, u32[]{:S(2)}) copy-start(f32[6]{0:T(128)} %diffusion.15) | copy-start | bytes 76
  30.3 9.4 %collective-permute-start = (f32[6,8,8,128]{3,2,1,0:T(8,128)S(1)}, f32[6,8,8,128]{3,2,1,0:T(8,128)S(1)}, u32[]{:S(2)}, u32[]{:S(2)}) collective-permute-start(f32[6,8,8,128]{3,2,1,0:T(8,128)S(1)} %get-tuple-element.46), channel_id=1, source_target_pairs={{0,1},{1,2},{2,3},{3,4},{4,5},{5,6},{6,7},{7,0},{8,9},{9,10},{10,1... | collective-permute-start | bytes 589832 | tf_op jit(solution)/shard_map/ppermute | solution.py:376
  31.8 10.2 %collective-permute-start.1 = (f32[6,8,8,128]{3,2,1,0:T(8,128)S(1)}, f32[6,8,8,128]{3,2,1,0:T(8,128)S(1)}, u32[]{:S(2)}, u32[]{:S(2)}) collective-permute-start(f32[6,8,8,128]{3,2,1,0:T(8,128)S(1)} %get-tuple-element.47), channel_id=1, source_target_pairs={{0,7},{1,0},{2,1},{3,2},{4,3},{5,4},{6,5},{7,6},{8,15},{9,8},{10,9... | collective-permute-start | bytes 589832 | tf_op jit(solution)/shard_map/ppermute | solution.py:376
  51.2 23.0 %all-to-all-start.2 = ((f32[8,3,16,128]{3,2,1,0:T(8,128)}), f32[8,3,16,128]{3,2,1,0:T(8,128)S(1)}, u32[]{:S(2)}, u32[]{:S(2)}) async-start(f32[8,3,16,128]{3,2,1,0:T(8,128)} %copy-done.24), calls=%async_computation.2 | async-start | bytes 393216 | tf_op jit(solution)/shard_map/all_to_all | solution.py:401
  54.8 12.2 %collective-permute-start.3 = (f32[6,8,8,128]{3,2,1,0:T(8,128)}, f32[6,8,8,128]{3,2,1,0:T(8,128)S(1)}, u32[]{:S(2)}, u32[]{:S(2)}) collective-permute-start(f32[6,8,8,128]{3,2,1,0:T(8,128)} %copy-done.55), channel_id=1, source_target_pairs={{0,1},{1,2},{2,3},{3,4},{4,5},{5,6},{6,7},{7,0},{8,9},{9,10},{10,1... | collective-permute-start | bytes 589832 | tf_op jit(solution)/shard_map/ppermute | solution.py:376
  56.2 11.9 %collective-permute-start.4 = (f32[6,8,8,128]{3,2,1,0:T(8,128)}, f32[6,8,8,128]{3,2,1,0:T(8,128)S(1)}, u32[]{:S(2)}, u32[]{:S(2)}) collective-permute-start(f32[6,8,8,128]{3,2,1,0:T(8,128)} %copy-done.54), channel_id=1, source_target_pairs={{0,7},{1,0},{2,1},{3,2},{4,3},{5,4},{6,5},{7,6},{8,15},{9,8},{10,9... | collective-permute-start | bytes 589832 | tf_op jit(solution)/shard_map/ppermute | solution.py:376
  75.3 4.5 %collective-permute-start.7 = (f32[8,3,16,128]{3,2,1,0:T(8,128)S(1)}, f32[8,3,16,128]{3,2,1,0:T(8,128)}, u32[]{:S(2)}, u32[]{:S(2)}) collective-permute-start(f32[8,3,16,128]{3,2,1,0:T(8,128)S(1)} %interpolate.5), channel_id=1, source_target_pairs={{0,8},{1,9},{2,10},{3,11},{8,16},{9,17},{10,18},{11,19},{12,4},{13... | collective-permute-start | bytes 589832 | tf_op jit(solution)/shard_map/ppermute | solution.py:387
  79.8 19.7 %all-to-all-start.3 = ((f32[8,3,16,128]{3,2,1,0:T(8,128)}), f32[8,3,16,128]{3,2,1,0:T(8,128)S(1)}, u32[]{:S(2)}, u32[]{:S(2)}) async-start(f32[8,3,16,128]{3,2,1,0:T(8,128)} %collective-permute-done.7), calls=%async_computation.3 | async-start | bytes 393216 | tf_op jit(solution)/shard_map/all_to_all | solution.py:405
  86.6 10.6 %collective-permute-start.5 = (f32[6,8,8,128]{3,2,1,0:T(8,128)}, f32[6,8,8,128]{3,2,1,0:T(8,128)S(1)}, u32[]{:S(2)}, u32[]{:S(2)}) collective-permute-start(f32[6,8,8,128]{3,2,1,0:T(8,128)} %copy-done.52), channel_id=1, source_target_pairs={{0,1},{1,2},{2,3},{3,4},{4,5},{5,6},{6,7},{7,0},{8,9},{9,10},{10,1... | collective-permute-start | bytes 589832 | tf_op jit(solution)/shard_map/ppermute | solution.py:376
  88.1 10.8 %collective-permute-start.6 = (f32[6,8,8,128]{3,2,1,0:T(8,128)}, f32[6,8,8,128]{3,2,1,0:T(8,128)S(1)}, u32[]{:S(2)}, u32[]{:S(2)}) collective-permute-start(f32[6,8,8,128]{3,2,1,0:T(8,128)} %copy-done.49), channel_id=1, source_target_pairs={{0,7},{1,0},{2,1},{3,2},{4,3},{5,4},{6,5},{7,6},{8,15},{9,8},{10,9... | collective-permute-start | bytes 589832 | tf_op jit(solution)/shard_map/ppermute | solution.py:376
  99.6 1.4 copy-start.3
  101.0 1.4 copy-start.7
  110.9 26.9 %all-to-all-start.4 = ((f32[8,3,16,128]{3,2,1,0:T(8,128)}), f32[8,3,16,128]{3,2,1,0:T(8,128)S(1)}, u32[]{:S(2)}, u32[]{:S(2)}) async-start(f32[8,3,16,128]{3,2,1,0:T(8,128)} %copy-done.25), calls=%async_computation.4 | async-start | bytes 393216 | tf_op jit(solution)/shard_map/all_to_all | solution.py:401
  115.0 12.6 %collective-permute-start.8 = (f32[6,8,8,128]{3,2,1,0:T(8,128)}, f32[6,8,8,128]{3,2,1,0:T(8,128)S(1)}, u32[]{:S(2)}, u32[]{:S(2)}) collective-permute-start(f32[6,8,8,128]{3,2,1,0:T(8,128)} %copy-done.46), channel_id=1, source_target_pairs={{0,1},{1,2},{2,3},{3,4},{4,5},{5,6},{6,7},{7,0},{8,9},{9,10},{10,1... | collective-permute-start | bytes 589832 | tf_op jit(solution)/shard_map/ppermute | solution.py:376
  116.5 12.5 %collective-permute-start.9 = (f32[6,8,8,128]{3,2,1,0:T(8,128)}, f32[6,8,8,128]{3,2,1,0:T(8,128)S(1)}, u32[]{:S(2)}, u32[]{:S(2)}) collective-permute-start(f32[6,8,8,128]{3,2,1,0:T(8,128)} %copy-done.44), channel_id=1, source_target_pairs={{0,7},{1,0},{2,1},{3,2},{4,3},{5,4},{6,5},{7,6},{8,15},{9,8},{10,9... | collective-permute-start | bytes 589832 | tf_op jit(solution)/shard_map/ppermute | solution.py:376
  129.0 1.4 copy-start.4
  138.9 4.5 %collective-permute-start.12 = (f32[8,3,16,128]{3,2,1,0:T(8,128)S(1)}, f32[8,3,16,128]{3,2,1,0:T(8,128)}, u32[]{:S(2)}, u32[]{:S(2)}) collective-permute-start(f32[8,3,16,128]{3,2,1,0:T(8,128)S(1)} %interpolate.6), channel_id=1, source_target_pairs={{0,8},{1,9},{2,10},{3,11},{8,16},{9,17},{10,18},{11,19},{12,4},{13... | collective-permute-start | bytes 589832 | tf_op jit(solution)/shard_map/ppermute | solution.py:387
  143.4 19.3 %all-to-all-start.5 = ((f32[8,3,16,128]{3,2,1,0:T(8,128)}), f32[8,3,16,128]{3,2,1,0:T(8,128)S(1)}, u32[]{:S(2)}, u32[]{:S(2)}) async-start(f32[8,3,16,128]{3,2,1,0:T(8,128)} %collective-permute-done.12), calls=%async_computation.5 | async-start | bytes 393216 | tf_op jit(solution)/shard_map/all_to_all | solution.py:405
  150.0 10.4 %collective-permute-start.10 = (f32[6,8,8,128]{3,2,1,0:T(8,128)}, f32[6,8,8,128]{3,2,1,0:T(8,128)S(1)}, u32[]{:S(2)}, u32[]{:S(2)}) collective-permute-start(f32[6,8,8,128]{3,2,1,0:T(8,128)} %copy-done.53), channel_id=1, source_target_pairs={{0,1},{1,2},{2,3},{3,4},{4,5},{5,6},{6,7},{7,0},{8,9},{9,10},{10,1... | collective-permute-start | bytes 589832 | tf_op jit(solution)/shard_map/ppermute | solution.py:376
  151.4 10.6 %collective-permute-start.11 = (f32[6,8,8,128]{3,2,1,0:T(8,128)}, f32[6,8,8,128]{3,2,1,0:T(8,128)S(1)}, u32[]{:S(2)}, u32[]{:S(2)}) collective-permute-start(f32[6,8,8,128]{3,2,1,0:T(8,128)} %copy-done.50), channel_id=1, source_target_pairs={{0,7},{1,0},{2,1},{3,2},{4,3},{5,4},{6,5},{7,6},{8,15},{9,8},{10,9... | collective-permute-start | bytes 589832 | tf_op jit(solution)/shard_map/ppermute | solution.py:376
  162.8 1.4 copy-start.11
  164.2 1.4 copy-start.15
  174.1 27.0 %all-to-all-start.6 = ((f32[8,3,16,128]{3,2,1,0:T(8,128)}), f32[8,3,16,128]{3,2,1,0:T(8,128)S(1)}, u32[]{:S(2)}, u32[]{:S(2)}) async-start(f32[8,3,16,128]{3,2,1,0:T(8,128)} %copy-done.26), calls=%async_computation.6 | async-start | bytes 393216 | tf_op jit(solution)/shard_map/all_to_all | solution.py:401
  178.2 12.7 %collective-permute-start.13 = (f32[6,8,8,128]{3,2,1,0:T(8,128)}, f32[6,8,8,128]{3,2,1,0:T(8,128)S(1)}, u32[]{:S(2)}, u32[]{:S(2)}) collective-permute-start(f32[6,8,8,128]{3,2,1,0:T(8,128)} %copy-done.47), channel_id=1, source_target_pairs={{0,1},{1,2},{2,3},{3,4},{4,5},{5,6},{6,7},{7,0},{8,9},{9,10},{10,1... | collective-permute-start | bytes 589832 | tf_op jit(solution)/shard_map/ppermute | solution.py:376
  179.7 12.6 %collective-permute-start.14 = (f32[6,8,8,128]{3,2,1,0:T(8,128)}, f32[6,8,8,128]{3,2,1,0:T(8,128)S(1)}, u32[]{:S(2)}, u32[]{:S(2)}) collective-permute-start(f32[6,8,8,128]{3,2,1,0:T(8,128)} %copy-done.45), channel_id=1, source_target_pairs={{0,7},{1,0},{2,1},{3,2},{4,3},{5,4},{6,5},{7,6},{8,15},{9,8},{10,9... | collective-permute-start | bytes 589832 | tf_op jit(solution)/shard_map/ppermute | solution.py:376
  192.3 1.4 copy-start.12
  193.7 1.4 copy-start.16
  202.3 4.5 %collective-permute-start.15 = (f32[8,3,16,128]{3,2,1,0:T(8,128)S(1)}, f32[8,3,16,128]{3,2,1,0:T(8,128)}, u32[]{:S(2)}, u32[]{:S(2)}) collective-permute-start(f32[8,3,16,128]{3,2,1,0:T(8,128)S(1)} %interpolate.7), channel_id=1, source_target_pairs={{0,8},{1,9},{2,10},{3,11},{8,16},{9,17},{10,18},{11,19},{12,4},{13... | collective-permute-start | bytes 589832 | tf_op jit(solution)/shard_map/ppermute | solution.py:387
  206.8 14.8 %all-to-all-start.7 = ((f32[8,3,16,128]{3,2,1,0:T(8,128)}), f32[8,3,16,128]{3,2,1,0:T(8,128)S(1)}, u32[]{:S(2)}, u32[]{:S(2)}) async-start(f32[8,3,16,128]{3,2,1,0:T(8,128)} %collective-permute-done.15), calls=%async_computation.7 | async-start | bytes 393216 | tf_op jit(solution)/shard_map/all_to_all | solution.py:405
  213.3 13.4 %collective-permute-start.18 = (f32[6,8,8,128]{3,2,1,0:T(8,128)}, f32[6,8,8,128]{3,2,1,0:T(8,128)}, u32[]{:S(2)}, u32[]{:S(2)}) collective-permute-start(f32[6,8,8,128]{3,2,1,0:T(8,128)} %copy-done.43), channel_id=1, source_target_pairs={{0,1},{1,2},{2,3},{3,4},{4,5},{5,6},{6,7},{7,0},{8,9},{9,10},{10,1... | collective-permute-start | bytes 589832 | tf_op jit(solution)/shard_map/ppermute | solution.py:376
  214.8 16.7 %collective-permute-start.19 = (f32[6,8,8,128]{3,2,1,0:T(8,128)}, f32[6,8,8,128]{3,2,1,0:T(8,128)}, u32[]{:S(2)}, u32[]{:S(2)}) collective-permute-start(f32[6,8,8,128]{3,2,1,0:T(8,128)} %copy-done.42), channel_id=1, source_target_pairs={{0,7},{1,0},{2,1},{3,2},{4,3},{5,4},{6,5},{7,6},{8,15},{9,8},{10,9... | collective-permute-start | bytes 589832 | tf_op jit(solution)/shard_map/ppermute | solution.py:376
  221.6 20.7 %collective-permute-start.16 = (f32[6,8,8,128]{3,2,1,0:T(8,128)}, f32[6,8,8,128]{3,2,1,0:T(8,128)S(1)}, u32[]{:S(2)}, u32[]{:S(2)}) collective-permute-start(f32[6,8,8,128]{3,2,1,0:T(8,128)} %copy-done.51), channel_id=1, source_target_pairs={{0,1},{1,2},{2,3},{3,4},{4,5},{5,6},{6,7},{7,0},{8,9},{9,10},{10,1... | collective-permute-start | bytes 589832 | tf_op jit(solution)/shard_map/ppermute | solution.py:376
  224.7 17.6 %collective-permute-start.17 = (f32[6,8,8,128]{3,2,1,0:T(8,128)}, f32[6,8,8,128]{3,2,1,0:T(8,128)S(1)}, u32[]{:S(2)}, u32[]{:S(2)}) collective-permute-start(f32[6,8,8,128]{3,2,1,0:T(8,128)} %copy-done.48), channel_id=1, source_target_pairs={{0,7},{1,0},{2,1},{3,2},{4,3},{5,4},{6,5},{7,6},{8,15},{9,8},{10,9... | collective-permute-start | bytes 589832 | tf_op jit(solution)/shard_map/ppermute | solution.py:376
  231.5 1.4 copy-start.5
  232.9 1.4 copy-start.13
  234.3 1.4 copy-start.19
  235.7 1.4 copy-start.21
  237.1 5.2 %copy-start.9 = (f32[6,32,16,128]{3,2,1,0:T(8,128)S(1)}, f32[6,32,16,128]{3,2,1,0:T(8,128)}, u32[]{:S(2)}) copy-start(f32[6,32,16,128]{3,2,1,0:T(8,128)} %copy-done.6) | copy-start | bytes 4718596
  237.1 5.2 %copy-start.17 = (f32[6,32,16,128]{3,2,1,0:T(8,128)S(1)}, f32[6,32,16,128]{3,2,1,0:T(8,128)}, u32[]{:S(2)}) copy-start(f32[6,32,16,128]{3,2,1,0:T(8,128)} %copy-done.14) | copy-start | bytes 4718596
  (36 other events, 29.5 us)
where the time goes:
time: 248 us; the launch traced here: 247 us
  starting transfers between devices  86.6 us (35%)
  waiting for transfers between devices  76.3 us (31%)
  local copies, waits for them, and re-layouts  46.8 us (19%)
  Pallas kernels  36.2 us (15%)
    unnamed x112, local copies, waits for them, and re-layouts  46.8 us
    ppermute x8, waiting for transfers between devices, exchange(): lax.ppermute(high_edges, 'sector', ahead)  43.3 us
    pallas_call x8, Pallas kernels, stage_call(): pl.pallas_call(functools.partial(stage_kernel, plan, stage, outer), in_sp...  30.5 us
    all_to_all x4, starting transfers between devices, on_device(): ghosts = lax.all_to_all(hopped, 'sector', 0, 0, tiled=True)  23.7 us
    ppermute x8, starting transfers between devices, exchange(): lax.ppermute(low_edges, 'sector', back)  20.1 us
    all_to_all x4, starting transfers between devices, on_device(): got = lax.all_to_all(dealt, 'sector', 0, 0, tiled=True)  18.4 us
    ppermute x8, starting transfers between devices, exchange(): lax.ppermute(high_edges, 'sector', ahead)  13.4 us
    ppermute x8, waiting for transfers between devices, exchange(): lax.ppermute(low_edges, 'sector', back)  12 us
  transfers between devices with their start and end apart: 28, of which 20 were waited for; matrix products, arithmetic and copies ran while one was open for 0% of the time, Pallas kernels for 6%

commit v1 on v0

--- a/solution.py
+++ b/solution.py
@@ -39,7 +39,10 @@
         self.inner = ((strip, self.axial - strip),)
         self.half = sectors // 2
         self.per = -(-2 * self.fields // self.half)
+        self.high = sectors // 2
         self.dealt = (sectors, self.per, self.cycle, self.radial)
+        self.part = (self.high, self.per, self.cycle, self.radial)
+        self.pair = (2, self.per, self.cycle, self.radial)
 
     def combo(self, side, field, plane):
         place = side * self.per * self.half + field * 2 + plane
@@ -73,7 +76,13 @@
                 buffer[piece, slot] = jnp.zeros((plan.cycle, plan.radial), jnp.float32)
 
 
-def planes_kernel(plan, state, dealt, planes, sems):
+def split(plan, low, dealt, keep, give):
+    for high in range(plan.high):
+        keep[high] = dealt[2 * high + low]
+        give[high] = dealt[2 * high + 1 - low]
+
+
+def planes_kernel(plan, place, state, keep, give, dealt, planes, sems):
     copies = [
         pltpu.make_async_copy(state.at[:, plan.axial - 2 : plan.axial], planes.at[0], sems.at[0]),
         pltpu.make_async_copy(state.at[:, 0:2], planes.at[1], sems.at[1]),
@@ -84,40 +93,40 @@
     for item in copies:
         item.wait()
     gather_planes(plan, dealt, lambda f, p: planes[0, f, p], lambda f, p: planes[1, f, p])
-
-
-def first_planes(plan, state):
+    split(plan, place[1] % 2, dealt, keep, give)
+
+
+def first_planes(plan, place, state):
     return pl.pallas_call(
         functools.partial(planes_kernel, plan),
-        in_specs=[whole(pl.ANY)],
-        out_specs=whole(VMEM),
-        out_shape=held(plan.dealt),
+        in_specs=[whole(SMEM), whole(pl.ANY)],
+        out_specs=[whole(VMEM)] * 2,
+        out_shape=[held(plan.part)] * 2,
         scratch_shapes=[
+            held(plan.dealt),
             held((2, plan.fields, 2, plan.cycle, plan.radial)),
             pltpu.SemaphoreType.DMA((2,)),
         ],
         compiler_params=params(),
         name="first_planes",
-    )(state)
-
-
-def first_kernel(plan, state, lo_o, hi_o, lo_i, hi_i):
-    for ranges, low_ref, high_ref in ((plan.outer, lo_o, hi_o), (plan.inner, lo_i, hi_i)):
-        start = 0
-        for low, high in ranges:
-
-            def body(tile, carry, low=low, start=start, low_ref=low_ref, high_ref=high_ref):
-                for field in range(plan.fields):
-                    for step in range(4):
-                        at = low + tile * 4 + step
-                        low_ref[field, start + tile, 2 * step : 2 * step + 2, :] = state[field, at, 0:2, :]
-                        high_ref[field, start + tile, 2 * step : 2 * step + 2, :] = state[
-                            field, at, plan.cycle - 2 : plan.cycle, :
-                        ]
-                return carry
-
-            lax.fori_loop(0, (high - low) // 4, body, 0)
-            start += (high - low) // 4
+    )(place, state)
+
+
+def first_kernel(plan, state, low_ref, high_ref):
+    start = 0
+    for low, high in plan.outer + plan.inner:
+
+        def body(tile, carry, low=low, start=start):
+            for field in range(plan.fields):
+                for step in range(4):
+                    at = low + tile * 4 + step
+                    rows = slice(2 * step, 2 * step + 2)
+                    low_ref[field, start + tile, rows, :] = state[field, at, 0:2, :]
+                    high_ref[field, start + tile, rows, :] = state[field, at, plan.cycle - 2 : plan.cycle, :]
+            return carry
+
+        lax.fori_loop(0, (high - low) // 4, body, 0)
+        start += (high - low) // 4
 
 
 def edge_shape(plan, ranges):
@@ -128,15 +137,57 @@
     return pl.pallas_call(
         functools.partial(first_kernel, plan),
         in_specs=[whole(VMEM)],
-        out_specs=[whole(VMEM)] * 4,
-        out_shape=[edge_shape(plan, ranges) for ranges in (plan.outer, plan.outer, plan.inner, plan.inner)],
+        out_specs=[whole(VMEM)] * 2,
+        out_shape=[edge_shape(plan, plan.outer + plan.inner)] * 2,
         compiler_params=params(),
         name="first_edges",
-    )(state)
-
-
-def interp_kernel(plan, section, place, offsets, weights, ring, *refs):
-    *_, out, spread = refs
+    )(near(state))
+
+
+def gather_kernel(plan, place, keep, came, *refs):
+    outs = refs[-plan.high :]
+    low, high = place[1] % 2, place[1] // 2
+    for ahead, out in enumerate(outs):
+        target = lax.rem(high + ahead, plan.high)
+        out[low] = keep[target]
+        out[1 - low] = came[target]
+
+
+def gather(plan, place, keep, came, after):
+    operands = [place, *map(near, (keep, came)), *map(near, after)]
+    return pl.pallas_call(
+        functools.partial(gather_kernel, plan),
+        in_specs=[whole(SMEM)] + [whole(VMEM)] * (len(operands) - 1),
+        out_specs=[whole(VMEM)] * plan.high,
+        out_shape=[held(plan.pair)] * plan.high,
+        compiler_params=params(),
+        name="gather_low",
+    )(*operands)
+
+
+def sort_kernel(plan, place, *refs):
+    came, (keep, give) = refs[: plan.high], refs[plan.high :]
+    low, high = place[1] % 2, place[1] // 2
+    for ahead, value in enumerate(came):
+        source = lax.rem(high + plan.high - ahead, plan.high)
+        keep[source] = value[low]
+        give[source] = value[1 - low]
+
+
+def sort(plan, place, came):
+    return pl.pallas_call(
+        functools.partial(sort_kernel, plan),
+        in_specs=[whole(SMEM)] + [whole(VMEM)] * plan.high,
+        out_specs=[whole(VMEM)] * 2,
+        out_shape=[held(plan.part)] * 2,
+        compiler_params=params(),
+        name="sort_low",
+    )(place, *map(near, came))
+
+
+def interp_kernel(plan, section, place, offsets, weights, *refs):
+    *refs, ring, spread = refs
+    came, outs = refs[: plan.high], refs[plan.high :]
     full = plan.cycle * plan.sectors
     row, sector = place[0], place[1]
     up = sector < plan.half
@@ -148,30 +199,36 @@
     matrix = weights[cell]
     for k in range(2 * plan.cycle):
         spread[k] = jnp.broadcast_to(matrix[:, k : k + 1], (plan.cycle, plan.radial))
-    for target in range(plan.sectors):
-        here = lax.rem(target + turn, plan.sectors)
-        after = lax.rem(here + 1, plan.sectors)
-        for slot in range(plan.per):
-            total = None
-            for k in range(2 * plan.cycle):
-                cell_at = k % plan.cycle
-                row_value = ring[here if k < plan.cycle else after, slot, cell_at : cell_at + 1, :]
-                term = spread[k] * jnp.broadcast_to(row_value, (plan.cycle, plan.radial))
-                total = term if total is None else total + term
-            out[target, slot] = total
-
-
-def interp(plan, section, place, offsets, weights, got, after):
-    operands = [place, offsets, weights, near(got), *map(near, after)]
+    high = sector // 2
+    for ahead, value in enumerate(came):
+        source = lax.rem(high + plan.high - ahead, plan.high)
+        for low in range(2):
+            ring[2 * source + low] = value[low]
+    for ahead, out in enumerate(outs):
+        for low in range(2):
+            target = 2 * lax.rem(high + ahead, plan.high) + low
+            here = lax.rem(target + turn, plan.sectors)
+            after = lax.rem(here + 1, plan.sectors)
+            for slot in range(plan.per):
+                total = None
+                for k in range(2 * plan.cycle):
+                    cell_at = k % plan.cycle
+                    row_value = ring[here if k < plan.cycle else after, slot, cell_at : cell_at + 1, :]
+                    term = spread[k] * jnp.broadcast_to(row_value, (plan.cycle, plan.radial))
+                    total = term if total is None else total + term
+                out[low, slot] = total
+
+
+def interp(plan, section, place, offsets, weights, came):
     return pl.pallas_call(
         functools.partial(interp_kernel, plan, section),
-        in_specs=[whole(SMEM), whole(SMEM)] + [whole(VMEM)] * (len(operands) - 2),
-        out_specs=whole(VMEM),
-        out_shape=held(plan.dealt),
-        scratch_shapes=[held((2 * plan.cycle, plan.cycle, plan.radial))],
+        in_specs=[whole(SMEM), whole(SMEM)] + [whole(VMEM)] * (1 + plan.high),
+        out_specs=[whole(VMEM)] * plan.high,
+        out_shape=[held(plan.pair)] * plan.high,
+        scratch_shapes=[held(plan.dealt), held((2 * plan.cycle, plan.cycle, plan.radial))],
         compiler_params=params(),
         name="interpolate",
-    )(*operands)
+    )(place, offsets, weights, *map(near, came))
 
 
 def coefficients(plan, speed, swirl, diffusion, coupling):
@@ -195,7 +252,9 @@
     chunks = {"state": state} if stage == 0 else dict(zip(("outer", "inner"), take(2)))
     low_in, high_in = take(2)
     if outer:
-        (ghosts,) = take(1)
+        place, keep_in, came_in = take(3)
+    elif stage < 3:
+        outer_edges = take(2)
     else:
         take(1)
     if stage == 3:
@@ -207,10 +266,20 @@
             (token,) = take(1)
         out_buf, sem = take(2)
     else:
-        out, low_out, high_out, token = take(4)
+        out, low_out, high_out = take(3)
         if outer:
-            (dealt,) = take(1)
+            keep_out, give_out = take(2)
     work, spread = take(2)
+    if outer:
+        (ghosts,) = take(1)
+        low_place = place[1] % 2
+        for high in range(plan.high):
+            ghosts[2 * high + low_place] = keep_in[high]
+            ghosts[2 * high + 1 - low_place] = came_in[high]
+    tiles_ahead = 0 if outer else count(plan.outer) // 4
+    if not outer and stage < 3:
+        low_out[:, :tiles_ahead] = outer_edges[0][...]
+        high_out[:, :tiles_ahead] = outer_edges[1][...]
     cycle, radial = plan.cycle, plan.radial
     terms = plan.fields + 9
     for f, (axial, around, d, mix) in enumerate(coefficients(plan, speed, swirl, diffusion, coupling)):
@@ -255,9 +324,9 @@
                 for step in range(4):
                     place = tile * 4 + step
                     work[field, place + 2, LOW : LOW + cycle, :] = ref[field, first_place + place]
-                    work[field, place + 2, LOW - 2 : LOW, :] = low_in[field, begin // 4 + tile, 2 * step : 2 * step + 2, :]
+                    work[field, place + 2, LOW - 2 : LOW, :] = low_in[field, tiles_ahead + begin // 4 + tile, 2 * step : 2 * step + 2, :]
                     work[field, place + 2, LOW + cycle : LOW + cycle + 2, :] = high_in[
-                        field, begin // 4 + tile, 2 * step : 2 * step + 2, :
+                        field, tiles_ahead + begin // 4 + tile, 2 * step : 2 * step + 2, :
                     ]
             return carry
 
@@ -296,9 +365,9 @@
                         continue
                     out[f, place, row : row + 8, :] = value
                     if row == 0:
-                        low_out[f, begin // 4 + tile, 2 * step : 2 * step + 2, :] = value[:2]
+                        low_out[f, tiles_ahead + begin // 4 + tile, 2 * step : 2 * step + 2, :] = value[:2]
                     if row == cycle - 8:
-                        high_out[f, begin // 4 + tile, 2 * step : 2 * step + 2, :] = value[6:]
+                        high_out[f, tiles_ahead + begin // 4 + tile, 2 * step : 2 * step + 2, :] = value[6:]
             return carry
 
         lax.fori_loop(0, size // 4, compute, 0)
@@ -319,9 +388,10 @@
             item.wait()
     elif outer:
         total = count(ranges)
-        clear_spare(plan, dealt)
-        gather_planes(plan, dealt, lambda f, p: out[f, total - 2 + p], lambda f, p: out[f, p])
-    if stage < 3 or outer:
+        clear_spare(plan, ghosts)
+        gather_planes(plan, ghosts, lambda f, p: out[f, total - 2 + p], lambda f, p: out[f, p])
+        split(plan, low_place, ghosts, keep_out, give_out)
+    if stage == 3 and outer:
         token[...] = jnp.zeros(token.shape, jnp.float32)
 
 
@@ -335,11 +405,18 @@
         operands.extend(map(near, values))
         specs.extend([whole(VMEM)] * len(values))
 
-    add([state, *(chunks or ()), *halos, extra])
+    add([state, *(chunks or ()), *halos])
+    if outer:
+        operands.append(extra[0])
+        specs.append(whole(SMEM))
+        extra = extra[1:]
+    add(extra)
     scratch = [
         held((plan.fields, longest + 4, plan.cycle + 16, plan.radial)),
         held((plan.fields * (plan.fields + 9), 8, plan.radial)),
     ]
+    if outer:
+        scratch.append(held(plan.dealt))
     aliases = {}
     token = held((8, plan.radial))
     if stage == 3:
@@ -352,9 +429,10 @@
         out_specs = [whole(pl.ANY)] + [whole(VMEM)] * outer
         scratch = [held(chunk), pltpu.SemaphoreType.DMA((len(ranges),))] + scratch
     else:
-        out_shape = [held(chunk), edge_shape(plan, ranges), edge_shape(plan, ranges), token]
+        edges = edge_shape(plan, ranges if outer else plan.outer + plan.inner)
+        out_shape = [held(chunk), edges, edges]
         if outer:
-            out_shape.append(held(plan.dealt))
+            out_shape += [held(plan.part)] * 2
         out_specs = [whole(VMEM)] * len(out_shape)
     return pl.pallas_call(
         functools.partial(stage_kernel, plan, stage, outer),
@@ -376,15 +454,30 @@
     return lax.ppermute(high_edges, "sector", ahead), lax.ppermute(low_edges, "sector", back)
 
 
-def row_hop(plan, value):
-    rows = lax.axis_size("row")
-    route = []
-    for row in range(rows):
-        for sector in range(plan.sectors):
-            target = row + 1 if sector < plan.half else row - 1
-            if 0 <= target < rows:
-                route.append((row * plan.sectors + sector, target * plan.sectors + sector))
-    return lax.ppermute(value, ("row", "sector"), route)
+def swap_low(plan, value):
+    return lax.ppermute(value, "sector", [(i, i + 1 - 2 * (i % 2)) for i in range(plan.sectors)])
+
+
+def along_high(plan, values):
+    sent = [values[0]]
+    for ahead in range(1, plan.high):
+        route = [(i, (i + 2 * ahead) % plan.sectors) for i in range(plan.sectors)]
+        sent.append(lax.ppermute(values[ahead], "sector", route))
+    return sent
+
+
+def along_high_to_next_row(plan, values):
+    rows, sent = lax.axis_size("row"), []
+    for ahead in range(plan.high):
+        route = []
+        for row in range(rows):
+            for sector in range(plan.sectors):
+                target = row + 1 if sector < plan.half else row - 1
+                if 0 <= target < rows:
+                    to = target * plan.sectors + (sector + 2 * ahead) % plan.sectors
+                    route.append((row * plan.sectors + sector, to))
+        sent.append(lax.ppermute(values[ahead], ("row", "sector"), route))
+    return sent
 
 
 def on_device(state, interp_blocks, rotor_offset, axial_speed, row_swirl, diffusivity, coupling):
@@ -392,30 +485,27 @@
     place = jnp.stack([lax.axis_index("row"), lax.axis_index("sector")]).astype(jnp.int32)
     scalars = (axial_speed, row_swirl, diffusivity, coupling)
 
-    dealt = first_planes(plan, state)
-    lo_o, hi_o, lo_i, hi_i = first_edges(plan, state)
-    outer_edges, inner_edges = (lo_o, hi_o), (lo_i, hi_i)
-    chunks, waited = None, ()
-    history = []
+    keep, give = first_planes(plan, place, state)
+    edges = first_edges(plan, state)
+    chunks, history = None, []
     for stage in range(4):
-        got = lax.all_to_all(dealt, "sector", 0, 0, tiled=True)
-        outer_halos = exchange(outer_edges)
-        made = interp(plan, stage, place, rotor_offset, interp_blocks, got, waited)
-        hopped = row_hop(plan, made)
-        ghosts = lax.all_to_all(hopped, "sector", 0, 0, tiled=True)
-        inner_edges = lax.optimization_barrier((*inner_edges, ghosts))[:2]
-        inner_halos = exchange(inner_edges)
         last = stage == 3
+        gathered = gather(plan, place, keep, swap_low(plan, give), edges[:1])
+        *edges, _ = lax.optimization_barrier((*edges, gathered[0]))
+        came = along_high(plan, gathered)
+        halos = exchange(edges)
+        made = interp(plan, stage, place, rotor_offset, interp_blocks, came)
+        keep, give = sort(plan, place, along_high_to_next_row(plan, made))
         older = [(history[0][i], history[1][i]) if last else () for i in range(2)]
-        out_o, *rest = stage_call(plan, stage, True, scalars, state, chunks, outer_halos, ghosts, older[0])
-        token = rest[0] if last else rest[2]
-        out_i, *rest_i = stage_call(
-            plan, stage, False, scalars, state, chunks, inner_halos, token, older[1], out_o if last else None
+        ghosts = (place, keep, swap_low(plan, give))
+        out_o, *rest = stage_call(plan, stage, True, scalars, state, chunks, halos, ghosts, older[0])
+        after = rest if last else rest[:2]
+        out_i, *edges = stage_call(
+            plan, stage, False, scalars, state, chunks, halos, after, older[1], out_o if last else None
         )
         if last:
             return out_i
-        outer_edges, dealt = rest[:2], rest[3]
-        inner_edges, waited = rest_i[:2], rest_i[2:]
+        keep, give = rest[2:]
         chunks = (out_o, out_i)
         history.append(chunks)
 

time: 248 us -> 200 us (0.81)
  the two profiles are of different devices: /device:TPU:1 before, /device:TPU:0 now
where the time goes in v1:
time: 200 us; the launch traced here: 199 us
  starting transfers between devices  86.9 us (43%)
  waiting for transfers between devices  67.1 us (34%)
  Pallas kernels  41.5 us (21%)
    ppermute x16, starting transfers between devices, along_high_to_next_row(): sent.append(lax.ppermute(values[ahead], ('row', 'sector'), route))  48.8 us
    ppermute x12, waiting for transfers between devices, along_high(): sent.append(lax.ppermute(values[ahead], 'sector', route))  34.4 us
    pallas_call x8, Pallas kernels, stage_call(): pl.pallas_call(functools.partial(stage_kernel, plan, stage, outer), in_sp...  31.1 us
    ppermute x8, waiting for transfers between devices, swap_low(): lax.ppermute(value, 'sector', [(i, i + 1 - 2 * (i % 2)) for i in range(pl...  25.5 us
    ppermute x4, starting transfers between devices, exchange(): lax.ppermute(low_edges, 'sector', back)  16.5 us
    ppermute x12, starting transfers between devices, along_high(): sent.append(lax.ppermute(values[ahead], 'sector', route))  15.3 us
    ppermute x16, waiting for transfers between devices, along_high_to_next_row(): sent.append(lax.ppermute(values[ahead], ('row', 'sector'), route))  7.2 us
    pallas_call x4, Pallas kernels, interp(): pl.pallas_call(functools.partial(interp_kernel, plan, section), in_specs=...  4.84 us
  transfers between devices with their start and end apart: 44, of which 25 were waited for; matrix products, arithmetic and copies ran while one was open for 0% of the time, Pallas kernels for 9%

profile of v1, /device:TPU:0, one launch (start us, length us, event | category | flops | bytes accessed | tf_op | source)
XLA Modules:
  0.0 198.7 jit_solution(1575956847910799843)
XLA Ops:
  0.1 1.9 copy-done
  2.7 3.0 %collective-permute-start = (f32[4,3,16,128]{3,2,1,0:T(8,128)S(1)}, f32[4,3,16,128]{3,2,1,0:T(8,128)S(1)}, u32[]{:S(2)}, u32[]{:S(2)}) collective-permute-start(f32[4,3,16,128]{3,2,1,0:T(8,128)S(1)} %get-tuple-element.86), channel_id=1, source_target_pairs={{0,1},{1,0},{2,3},{3,2},{4,5},{5,4},{6,7},{7,6},{8,9},{9,8},{10,11... | collective-permute-start | bytes 294920 | tf_op jit(solution)/shard_map/ppermute | solution.py:458
  6.1 2.4 %collective-permute-done.came = f32[4,3,16,128]{3,2,1,0:T(8,128)S(1)} collective-permute-done((f32[4,3,16,128]{3,2,1,0:T(8,128)S(1)}, f32[4,3,16,128]{3,2,1,0:T(8,128)S(1)}, u32[]{:S(2)}, u32[]{:S(2)}) %collective-permute-start) | collective-permute-done | bytes 98336 | tf_op jit(solution)/shard_map/ppermute | solution.py:458
  9.1 1.9 collective-permute-start.1
  11.0 3.1 %collective-permute-start.2 = (f32[6,16,8,128]{3,2,1,0:T(8,128)S(1)}, f32[6,16,8,128]{3,2,1,0:T(8,128)S(1)}, u32[]{:S(2)}, u32[]{:S(2)}) collective-permute-start(f32[6,16,8,128]{3,2,1,0:T(8,128)S(1)} %get-tuple-element.89.refs_0_), channel_id=1, source_target_pairs={{0,7},{1,0},{2,1},{3,2},{4,3},{5,4},{6,5},{7,6},{8,15},{9,8},{10,9... | collective-permute-start | bytes 1179656 | tf_op jit(solution)/shard_map/ppermute | solution.py:454
  14.1 2.5 %collective-permute-start.4 = (f32[2,3,16,128]{3,2,1,0:T(8,128)S(1)}, f32[2,3,16,128]{3,2,1,0:T(8,128)S(1)}, u32[]{:S(2)}, u32[]{:S(2)}) collective-permute-start(f32[2,3,16,128]{3,2,1,0:T(8,128)S(1)} %get-tuple-element.91), channel_id=1, source_target_pairs={{0,4},{1,5},{2,6},{3,7},{4,0},{5,1},{6,2},{7,3},{8,12},{9,13},{10,... | collective-permute-start | bytes 147464 | tf_op jit(solution)/shard_map/ppermute | solution.py:465
  17.9 7.7 %collective-permute-done.3.refs_1_ = f32[2,3,16,128]{3,2,1,0:T(8,128)S(1)} collective-permute-done((f32[2,3,16,128]{3,2,1,0:T(8,128)S(1)}, f32[2,3,16,128]{3,2,1,0:T(8,128)S(1)}, u32[]{:S(2)}, u32[]{:S(2)}) %collective-permute-start.3) | collective-permute-done | bytes 49184 | tf_op jit(solution)/shard_map/ppermute | solution.py:465
  28.2 5.3 %collective-permute-start.7 = (f32[2,3,16,128]{3,2,1,0:T(8,128)S(1)}, f32[2,3,16,128]{3,2,1,0:T(8,128)S(1)}, u32[]{:S(2)}, u32[]{:S(2)}) collective-permute-start(f32[2,3,16,128]{3,2,1,0:T(8,128)S(1)} %get-tuple-element.94), channel_id=1, source_target_pairs={{0,10},{1,11},{2,12},{3,13},{8,18},{9,19},{10,20},{11,21},{12,6},{... | collective-permute-start | bytes 147464 | tf_op jit(solution)/shard_map/ppermute | solution.py:479
  33.4 2.6 %collective-permute-start.8 = (f32[2,3,16,128]{3,2,1,0:T(8,128)S(1)}, f32[2,3,16,128]{3,2,1,0:T(8,128)S(1)}, u32[]{:S(2)}, u32[]{:S(2)}) collective-permute-start(f32[2,3,16,128]{3,2,1,0:T(8,128)S(1)} %get-tuple-element.95), channel_id=1, source_target_pairs={{0,12},{1,13},{2,14},{3,15},{8,20},{9,21},{10,22},{11,23},{12,0},{... | collective-permute-start | bytes 147464 | tf_op jit(solution)/shard_map/ppermute | solution.py:479
  36.1 3.2 %collective-permute-start.9 = (f32[2,3,16,128]{3,2,1,0:T(8,128)S(1)}, f32[2,3,16,128]{3,2,1,0:T(8,128)S(1)}, u32[]{:S(2)}, u32[]{:S(2)}) collective-permute-start(f32[2,3,16,128]{3,2,1,0:T(8,128)S(1)} %get-tuple-element.96), channel_id=1, source_target_pairs={{0,14},{1,15},{2,8},{3,9},{8,22},{9,23},{10,16},{11,17},{12,2},{13... | collective-permute-start | bytes 147464 | tf_op jit(solution)/shard_map/ppermute | solution.py:479
  42.3 4.0 %collective-permute-done.10.refs_5_ = f32[4,3,16,128]{3,2,1,0:T(8,128)S(1)} collective-permute-done((f32[4,3,16,128]{3,2,1,0:T(8,128)S(1)}, f32[4,3,16,128]{3,2,1,0:T(8,128)S(1)}, u32[]{:S(2)}, u32[]{:S(2)}) %collective-permute-start.10) | collective-permute-done | bytes 98336 | tf_op jit(solution)/shard_map/ppermute | solution.py:458
  46.3 3.6 %stage0_outer.1 = (f32[6,32,16,128]{3,2,1,0:T(8,128)S(1)}, f32[6,8,8,128]{3,2,1,0:T(8,128)S(1)}, f32[6,8,8,128]{3,2,1,0:T(8,128)S(1)}, f32[4,3,16,128]{3,2,1,0:T(8,128)S(1)}, f32[4,3,16,128]{3,2,1,0:T(8,128)S(1)}) custom-call(f32[6]{0:T(128)S(1)} %copy-done.5, f32[1]{0:T(128)S(6)} %copy.10.swirl, f32[6]{0:T(128)S(1)} %copy-done.6, f32[6,6]{1,0:T(8,128)S(1)} %copy-done.3, ...), custom_call_target="tpu_custom_call" | custom-call | tf_op jit(solution)/shard_map/stage0_outer/pallas_call | solution.py:437
  50.0 3.6 %stage0_inner.1 = (f32[6,32,16,128]{3,2,1,0:T(8,128)S(1)}, f32[6,16,8,128]{3,2,1,0:T(8,128)S(1)}, f32[6,16,8,128]{3,2,1,0:T(8,128)S(1)}) custom-call(f32[6]{0:T(128)S(1)} %copy-done.5, f32[1]{0:T(128)S(6)} %copy.10.swirl, f32[6]{0:T(128)S(1)} %copy-done.6, f32[6,6]{1,0:T(8,128)S(1)} %copy-done.3, f32[6,64,16,128]{3,2,1,0:T(8,128)S(1)} %copy-done.1, ...), custom_call_target="tpu_custom_call" | custom-call | tf_op jit(solution)/shard_map/stage0_inner/pallas_call | solution.py:437
  53.5 1.8 collective-permute-done.11.came
  56.2 4.5 %collective-permute-start.13 = (f32[6,16,8,128]{3,2,1,0:T(8,128)S(1)}, f32[6,16,8,128]{3,2,1,0:T(8,128)S(1)}, u32[]{:S(2)}, u32[]{:S(2)}) collective-permute-start(f32[6,16,8,128]{3,2,1,0:T(8,128)S(1)} %get-tuple-element.109.refs_0_), channel_id=1, source_target_pairs={{0,7},{1,0},{2,1},{3,2},{4,3},{5,4},{6,5},{7,6},{8,15},{9,8},{10,9... | collective-permute-start | bytes 1179656 | tf_op jit(solution)/shard_map/ppermute | solution.py:454
  61.5 3.0 %collective-permute-start.16 = (f32[2,3,16,128]{3,2,1,0:T(8,128)S(1)}, f32[2,3,16,128]{3,2,1,0:T(8,128)S(1)}, u32[]{:S(2)}, u32[]{:S(2)}) collective-permute-start(f32[2,3,16,128]{3,2,1,0:T(8,128)S(1)} %get-tuple-element.112), channel_id=1, source_target_pairs={{0,6},{1,7},{2,0},{3,1},{4,2},{5,3},{6,4},{7,5},{8,14},{9,15},{10,... | collective-permute-start | bytes 147464 | tf_op jit(solution)/shard_map/ppermute | solution.py:465
  64.5 6.7 %collective-permute-done.14.refs_1_ = f32[2,3,16,128]{3,2,1,0:T(8,128)S(1)} collective-permute-done((f32[2,3,16,128]{3,2,1,0:T(8,128)S(1)}, f32[2,3,16,128]{3,2,1,0:T(8,128)S(1)}, u32[]{:S(2)}, u32[]{:S(2)}) %collective-permute-start.14) | collective-permute-done | bytes 49184 | tf_op jit(solution)/shard_map/ppermute | solution.py:465
  71.2 1.5 collective-permute-done.15.refs_2_
  76.0 4.3 %collective-permute-start.18 = (f32[2,3,16,128]{3,2,1,0:T(8,128)S(1)}, f32[2,3,16,128]{3,2,1,0:T(8,128)S(1)}, u32[]{:S(2)}, u32[]{:S(2)}) collective-permute-start(f32[2,3,16,128]{3,2,1,0:T(8,128)S(1)} %get-tuple-element.114), channel_id=1, source_target_pairs={{0,10},{1,11},{2,12},{3,13},{8,18},{9,19},{10,20},{11,21},{12,6},{... | collective-permute-start | bytes 147464 | tf_op jit(solution)/shard_map/ppermute | solution.py:479
  80.4 3.3 %collective-permute-start.19 = (f32[2,3,16,128]{3,2,1,0:T(8,128)S(1)}, f32[2,3,16,128]{3,2,1,0:T(8,128)S(1)}, u32[]{:S(2)}, u32[]{:S(2)}) collective-permute-start(f32[2,3,16,128]{3,2,1,0:T(8,128)S(1)} %get-tuple-element.115), channel_id=1, source_target_pairs={{0,12},{1,13},{2,14},{3,15},{8,20},{9,21},{10,22},{11,23},{12,0},{... | collective-permute-start | bytes 147464 | tf_op jit(solution)/shard_map/ppermute | solution.py:479
  83.7 3.1 %collective-permute-start.20 = (f32[2,3,16,128]{3,2,1,0:T(8,128)S(1)}, f32[2,3,16,128]{3,2,1,0:T(8,128)S(1)}, u32[]{:S(2)}, u32[]{:S(2)}) collective-permute-start(f32[2,3,16,128]{3,2,1,0:T(8,128)S(1)} %get-tuple-element.116), channel_id=1, source_target_pairs={{0,14},{1,15},{2,8},{3,9},{8,22},{9,23},{10,16},{11,17},{12,2},{13... | collective-permute-start | bytes 147464 | tf_op jit(solution)/shard_map/ppermute | solution.py:479
  89.2 4.6 %collective-permute-done.21.refs_7_ = f32[4,3,16,128]{3,2,1,0:T(8,128)S(1)} collective-permute-done((f32[4,3,16,128]{3,2,1,0:T(8,128)S(1)}, f32[4,3,16,128]{3,2,1,0:T(8,128)S(1)}, u32[]{:S(2)}, u32[]{:S(2)}) %collective-permute-start.21) | collective-permute-done | bytes 98336 | tf_op jit(solution)/shard_map/ppermute | solution.py:458
  93.8 3.6 %stage1_outer.1 = (f32[6,32,16,128]{3,2,1,0:T(8,128)S(1)}, f32[6,8,8,128]{3,2,1,0:T(8,128)S(1)}, f32[6,8,8,128]{3,2,1,0:T(8,128)S(1)}, f32[4,3,16,128]{3,2,1,0:T(8,128)S(1)}, f32[4,3,16,128]{3,2,1,0:T(8,128)S(1)}) custom-call(f32[6]{0:T(128)S(1)} %copy-done.5, f32[1]{0:T(128)S(6)} %copy.10.swirl, f32[6]{0:T(128)S(1)} %copy-done.6, f32[6,6]{1,0:T(8,128)S(1)} %copy-done.3, ...), custom_call_target="tpu_custom_call" | custom-call | tf_op jit(solution)/shard_map/stage1_outer/pallas_call | solution.py:437
  97.4 3.6 %stage1_inner.1 = (f32[6,32,16,128]{3,2,1,0:T(8,128)S(1)}, f32[6,16,8,128]{3,2,1,0:T(8,128)S(1)}, f32[6,16,8,128]{3,2,1,0:T(8,128)S(1)}) custom-call(f32[6]{0:T(128)S(1)} %copy-done.5, f32[1]{0:T(128)S(6)} %copy.10.swirl, f32[6]{0:T(128)S(1)} %copy-done.6, f32[6,6]{1,0:T(8,128)S(1)} %copy-done.3, f32[6,64,16,128]{3,2,1,0:T(8,128)S(1)} %copy-done.1, ...), custom_call_target="tpu_custom_call" | custom-call | tf_op jit(solution)/shard_map/stage1_inner/pallas_call | solution.py:437
  101.0 1.7 collective-permute-done.22.came
  103.6 4.4 %collective-permute-start.24 = (f32[6,16,8,128]{3,2,1,0:T(8,128)S(1)}, f32[6,16,8,128]{3,2,1,0:T(8,128)S(1)}, u32[]{:S(2)}, u32[]{:S(2)}) collective-permute-start(f32[6,16,8,128]{3,2,1,0:T(8,128)S(1)} %get-tuple-element.129.refs_0_), channel_id=1, source_target_pairs={{0,7},{1,0},{2,1},{3,2},{4,3},{5,4},{6,5},{7,6},{8,15},{9,8},{10,9... | collective-permute-start | bytes 1179656 | tf_op jit(solution)/shard_map/ppermute | solution.py:454
  109.0 2.8 %collective-permute-start.27 = (f32[2,3,16,128]{3,2,1,0:T(8,128)S(1)}, f32[2,3,16,128]{3,2,1,0:T(8,128)S(1)}, u32[]{:S(2)}, u32[]{:S(2)}) collective-permute-start(f32[2,3,16,128]{3,2,1,0:T(8,128)S(1)} %get-tuple-element.132), channel_id=1, source_target_pairs={{0,6},{1,7},{2,0},{3,1},{4,2},{5,3},{6,4},{7,5},{8,14},{9,15},{10,... | collective-permute-start | bytes 147464 | tf_op jit(solution)/shard_map/ppermute | solution.py:465
  111.9 6.8 %collective-permute-done.25.refs_1_ = f32[2,3,16,128]{3,2,1,0:T(8,128)S(1)} collective-permute-done((f32[2,3,16,128]{3,2,1,0:T(8,128)S(1)}, f32[2,3,16,128]{3,2,1,0:T(8,128)S(1)}, u32[]{:S(2)}, u32[]{:S(2)}) %collective-permute-start.25) | collective-permute-done | bytes 49184 | tf_op jit(solution)/shard_map/ppermute | solution.py:465
  118.6 1.6 collective-permute-done.26.refs_2_
  123.4 4.2 %collective-permute-start.29 = (f32[2,3,16,128]{3,2,1,0:T(8,128)S(1)}, f32[2,3,16,128]{3,2,1,0:T(8,128)S(1)}, u32[]{:S(2)}, u32[]{:S(2)}) collective-permute-start(f32[2,3,16,128]{3,2,1,0:T(8,128)S(1)} %get-tuple-element.134), channel_id=1, source_target_pairs={{0,10},{1,11},{2,12},{3,13},{8,18},{9,19},{10,20},{11,21},{12,6},{... | collective-permute-start | bytes 147464 | tf_op jit(solution)/shard_map/ppermute | solution.py:479
  127.6 3.5 %collective-permute-start.30 = (f32[2,3,16,128]{3,2,1,0:T(8,128)S(1)}, f32[2,3,16,128]{3,2,1,0:T(8,128)S(1)}, u32[]{:S(2)}, u32[]{:S(2)}) collective-permute-start(f32[2,3,16,128]{3,2,1,0:T(8,128)S(1)} %get-tuple-element.135), channel_id=1, source_target_pairs={{0,12},{1,13},{2,14},{3,15},{8,20},{9,21},{10,22},{11,23},{12,0},{... | collective-permute-start | bytes 147464 | tf_op jit(solution)/shard_map/ppermute | solution.py:479
  131.1 3.1 %collective-permute-start.31 = (f32[2,3,16,128]{3,2,1,0:T(8,128)S(1)}, f32[2,3,16,128]{3,2,1,0:T(8,128)S(1)}, u32[]{:S(2)}, u32[]{:S(2)}) collective-permute-start(f32[2,3,16,128]{3,2,1,0:T(8,128)S(1)} %get-tuple-element.136), channel_id=1, source_target_pairs={{0,14},{1,15},{2,8},{3,9},{8,22},{9,23},{10,16},{11,17},{12,2},{13... | collective-permute-start | bytes 147464 | tf_op jit(solution)/shard_map/ppermute | solution.py:479
  134.5 1.6 collective-permute-done.31.refs_3_
  136.7 4.6 %collective-permute-done.32.refs_7_ = f32[4,3,16,128]{3,2,1,0:T(8,128)S(1)} collective-permute-done((f32[4,3,16,128]{3,2,1,0:T(8,128)S(1)}, f32[4,3,16,128]{3,2,1,0:T(8,128)S(1)}, u32[]{:S(2)}, u32[]{:S(2)}) %collective-permute-start.32) | collective-permute-done | bytes 98336 | tf_op jit(solution)/shard_map/ppermute | solution.py:458
  141.3 3.6 %stage2_outer.1 = (f32[6,32,16,128]{3,2,1,0:T(8,128)S(1)}, f32[6,8,8,128]{3,2,1,0:T(8,128)S(1)}, f32[6,8,8,128]{3,2,1,0:T(8,128)S(1)}, f32[4,3,16,128]{3,2,1,0:T(8,128)S(1)}, f32[4,3,16,128]{3,2,1,0:T(8,128)S(1)}) custom-call(f32[6]{0:T(128)S(1)} %copy-done.5, f32[1]{0:T(128)S(6)} %copy.10.swirl, f32[6]{0:T(128)S(1)} %copy-done.6, f32[6,6]{1,0:T(8,128)S(1)} %copy-done.3, ...), custom_call_target="tpu_custom_call" | custom-call | tf_op jit(solution)/shard_map/stage2_outer/pallas_call | solution.py:437
  145.0 3.6 %stage2_inner.1 = (f32[6,32,16,128]{3,2,1,0:T(8,128)S(1)}, f32[6,16,8,128]{3,2,1,0:T(8,128)S(1)}, f32[6,16,8,128]{3,2,1,0:T(8,128)S(1)}) custom-call(f32[6]{0:T(128)S(1)} %copy-done.5, f32[1]{0:T(128)S(6)} %copy.10.swirl, f32[6]{0:T(128)S(1)} %copy-done.6, f32[6,6]{1,0:T(8,128)S(1)} %copy-done.3, f32[6,64,16,128]{3,2,1,0:T(8,128)S(1)} %copy-done.1, ...), custom_call_target="tpu_custom_call" | custom-call | tf_op jit(solution)/shard_map/stage2_inner/pallas_call | solution.py:437
  148.6 1.8 collective-permute-done.33.came
  151.2 4.5 %collective-permute-start.35 = (f32[6,16,8,128]{3,2,1,0:T(8,128)S(1)}, f32[6,16,8,128]{3,2,1,0:T(8,128)S(1)}, u32[]{:S(2)}, u32[]{:S(2)}) collective-permute-start(f32[6,16,8,128]{3,2,1,0:T(8,128)S(1)} %get-tuple-element.149.refs_0_), channel_id=1, source_target_pairs={{0,7},{1,0},{2,1},{3,2},{4,3},{5,4},{6,5},{7,6},{8,15},{9,8},{10,9... | collective-permute-start | bytes 1179656 | tf_op jit(solution)/shard_map/ppermute | solution.py:454
  156.5 3.0 %collective-permute-start.38 = (f32[2,3,16,128]{3,2,1,0:T(8,128)S(1)}, f32[2,3,16,128]{3,2,1,0:T(8,128)S(1)}, u32[]{:S(2)}, u32[]{:S(2)}) collective-permute-start(f32[2,3,16,128]{3,2,1,0:T(8,128)S(1)} %get-tuple-element.152), channel_id=1, source_target_pairs={{0,6},{1,7},{2,0},{3,1},{4,2},{5,3},{6,4},{7,5},{8,14},{9,15},{10,... | collective-permute-start | bytes 147464 | tf_op jit(solution)/shard_map/ppermute | solution.py:465
  159.5 6.7 %collective-permute-done.36.refs_1_ = f32[2,3,16,128]{3,2,1,0:T(8,128)S(1)} collective-permute-done((f32[2,3,16,128]{3,2,1,0:T(8,128)S(1)}, f32[2,3,16,128]{3,2,1,0:T(8,128)S(1)}, u32[]{:S(2)}, u32[]{:S(2)}) %collective-permute-start.36) | collective-permute-done | bytes 49184 | tf_op jit(solution)/shard_map/ppermute | solution.py:465
  166.2 1.7 collective-permute-done.37.refs_2_
  170.7 3.9 %collective-permute-start.40 = (f32[2,3,16,128]{3,2,1,0:T(8,128)S(1)}, f32[2,3,16,128]{3,2,1,0:T(8,128)S(1)}, u32[]{:S(2)}, u32[]{:S(2)}) collective-permute-start(f32[2,3,16,128]{3,2,1,0:T(8,128)S(1)} %get-tuple-element.154), channel_id=1, source_target_pairs={{0,10},{1,11},{2,12},{3,13},{8,18},{9,19},{10,20},{11,21},{12,6},{... | collective-permute-start | bytes 147464 | tf_op jit(solution)/shard_map/ppermute | solution.py:479
  174.6 4.1 %collective-permute-start.41 = (f32[2,3,16,128]{3,2,1,0:T(8,128)S(1)}, f32[2,3,16,128]{3,2,1,0:T(8,128)S(1)}, u32[]{:S(2)}, u32[]{:S(2)}) collective-permute-start(f32[2,3,16,128]{3,2,1,0:T(8,128)S(1)} %get-tuple-element.155), channel_id=1, source_target_pairs={{0,12},{1,13},{2,14},{3,15},{8,20},{9,21},{10,22},{11,23},{12,0},{... | collective-permute-start | bytes 147464 | tf_op jit(solution)/shard_map/ppermute | solution.py:479
  178.7 3.1 %collective-permute-start.42 = (f32[2,3,16,128]{3,2,1,0:T(8,128)S(1)}, f32[2,3,16,128]{3,2,1,0:T(8,128)S(1)}, u32[]{:S(2)}, u32[]{:S(2)}) collective-permute-start(f32[2,3,16,128]{3,2,1,0:T(8,128)S(1)} %get-tuple-element.156), channel_id=1, source_target_pairs={{0,14},{1,15},{2,8},{3,9},{8,22},{9,23},{10,16},{11,17},{12,2},{13... | collective-permute-start | bytes 147464 | tf_op jit(solution)/shard_map/ppermute | solution.py:479
  181.8 1.9 collective-permute-done.42.refs_3_
  184.4 4.6 %collective-permute-done.43.refs_7_ = f32[4,3,16,128]{3,2,1,0:T(8,128)S(1)} collective-permute-done((f32[4,3,16,128]{3,2,1,0:T(8,128)S(1)}, f32[4,3,16,128]{3,2,1,0:T(8,128)S(1)}, u32[]{:S(2)}, u32[]{:S(2)}) %collective-permute-start.43) | collective-permute-done | bytes 98336 | tf_op jit(solution)/shard_map/ppermute | solution.py:458
  189.0 4.8 %stage3_outer.1 = (f32[6,64,16,128]{3,2,1,0:T(8,128)}, f32[8,128]{1,0:T(8,128)S(1)}) custom-call(f32[6]{0:T(128)S(1)} %copy-done.5, f32[1]{0:T(128)S(6)} %copy.10.swirl, f32[6]{0:T(128)S(1)} %copy-done.6, f32[6,6]{1,0:T(8,128)S(1)} %copy-done.3, f32[6,64,16,128]{3,2,1,0:T(8,128)S(1)} %copy-done.1, f32[6,32,16,128]{3,2,1,0:T(8,128)S(1)} %get-tuple-element.139.refs_1_, ...), custom_call_target="tpu_custom_call" | custom-call | tf_op jit(solution)/shard_map/stage3_outer/pallas_call | solution.py:437
  193.8 4.8 %stage3_inner.1 = f32[6,64,16,128]{3,2,1,0:T(8,128)} custom-call(f32[6]{0:T(128)S(1)} %copy-done.5, f32[1]{0:T(128)S(6)} %copy.10.swirl, f32[6]{0:T(128)S(1)} %copy-done.6, f32[6,6]{1,0:T(8,128)S(1)} %copy-done.3, f32[6,64,16,128]{3,2,1,0:T(8,128)S(1)} %copy-done.1, ...), custom_call_target="tpu_custom_call", output_to_operand_aliasing={{}: (12, {})} | custom-call | tf_op jit(solution)/shard_map/stage3_inner/pallas_call | solution.py:437
  (77 shorter events, 26.5 us)
Async XLA Ops:
  2.6 43.6 %copy-start.1 = (f32[6,64,16,128]{3,2,1,0:T(8,128)S(1)}, f32[6,64,16,128]{3,2,1,0:T(8,128)}, u32[]{:S(2)}) copy-start(f32[6,64,16,128]{3,2,1,0:T(8,128)} %refs_0_.15) | copy-start | bytes 9437188
  2.6 43.6 %copy-start.3 = (f32[6,6]{1,0:T(8,128)S(1)}, f32[6,6]{1,0:T(8,128)}, u32[]{:S(2)}) copy-start(f32[6,6]{1,0:T(8,128)} %coupling.15) | copy-start | bytes 436
  2.7 43.6 %copy-start.5 = (f32[6]{0:T(128)S(1)}, f32[6]{0:T(128)}, u32[]{:S(2)}) copy-start(f32[6]{0:T(128)} %speed.15) | copy-start | bytes 76
  2.7 43.6 %copy-start.6 = (f32[6]{0:T(128)S(1)}, f32[6]{0:T(128)}, u32[]{:S(2)}) copy-start(f32[6]{0:T(128)} %diffusion.15) | copy-start | bytes 76
  2.7 5.8 %collective-permute-start = (f32[4,3,16,128]{3,2,1,0:T(8,128)S(1)}, f32[4,3,16,128]{3,2,1,0:T(8,128)S(1)}, u32[]{:S(2)}, u32[]{:S(2)}) collective-permute-start(f32[4,3,16,128]{3,2,1,0:T(8,128)S(1)} %get-tuple-element.86), channel_id=1, source_target_pairs={{0,1},{1,0},{2,3},{3,2},{4,5},{5,4},{6,7},{7,6},{8,9},{9,8},{10,11... | collective-permute-start | bytes 294920 | tf_op jit(solution)/shard_map/ppermute | solution.py:458
  9.1 37.2 %collective-permute-start.1 = (f32[6,16,8,128]{3,2,1,0:T(8,128)S(1)}, f32[6,16,8,128]{3,2,1,0:T(8,128)S(1)}, u32[]{:S(2)}, u32[]{:S(2)}) collective-permute-start(f32[6,16,8,128]{3,2,1,0:T(8,128)S(1)} %get-tuple-element.88), channel_id=1, source_target_pairs={{0,1},{1,2},{2,3},{3,4},{4,5},{5,6},{6,7},{7,0},{8,9},{9,10},{10,1... | collective-permute-start | bytes 1179656 | tf_op jit(solution)/shard_map/ppermute | solution.py:454
  11.0 35.3 %collective-permute-start.2 = (f32[6,16,8,128]{3,2,1,0:T(8,128)S(1)}, f32[6,16,8,128]{3,2,1,0:T(8,128)S(1)}, u32[]{:S(2)}, u32[]{:S(2)}) collective-permute-start(f32[6,16,8,128]{3,2,1,0:T(8,128)S(1)} %get-tuple-element.89.refs_0_), channel_id=1, source_target_pairs={{0,7},{1,0},{2,1},{3,2},{4,3},{5,4},{6,5},{7,6},{8,15},{9,8},{10,9... | collective-permute-start | bytes 1179656 | tf_op jit(solution)/shard_map/ppermute | solution.py:454
  14.1 11.6 %collective-permute-start.3 = (f32[2,3,16,128]{3,2,1,0:T(8,128)S(1)}, f32[2,3,16,128]{3,2,1,0:T(8,128)S(1)}, u32[]{:S(2)}, u32[]{:S(2)}) collective-permute-start(f32[2,3,16,128]{3,2,1,0:T(8,128)S(1)} %get-tuple-element.90), channel_id=1, source_target_pairs={{0,2},{1,3},{2,4},{3,5},{4,6},{5,7},{6,0},{7,1},{8,10},{9,11},{10,... | collective-permute-start | bytes 147464 | tf_op jit(solution)/shard_map/ppermute | solution.py:465
  14.1 11.6 %collective-permute-start.4 = (f32[2,3,16,128]{3,2,1,0:T(8,128)S(1)}, f32[2,3,16,128]{3,2,1,0:T(8,128)S(1)}, u32[]{:S(2)}, u32[]{:S(2)}) collective-permute-start(f32[2,3,16,128]{3,2,1,0:T(8,128)S(1)} %get-tuple-element.91), channel_id=1, source_target_pairs={{0,4},{1,5},{2,6},{3,7},{4,0},{5,1},{6,2},{7,3},{8,12},{9,13},{10,... | collective-permute-start | bytes 147464 | tf_op jit(solution)/shard_map/ppermute | solution.py:465
  16.5 9.1 %collective-permute-start.5 = (f32[2,3,16,128]{3,2,1,0:T(8,128)S(1)}, f32[2,3,16,128]{3,2,1,0:T(8,128)S(1)}, u32[]{:S(2)}, u32[]{:S(2)}) collective-permute-start(f32[2,3,16,128]{3,2,1,0:T(8,128)S(1)} %get-tuple-element.92), channel_id=1, source_target_pairs={{0,6},{1,7},{2,0},{3,1},{4,2},{5,3},{6,4},{7,5},{8,14},{9,15},{10,... | collective-permute-start | bytes 147464 | tf_op jit(solution)/shard_map/ppermute | solution.py:465
  26.9 9.2 %collective-permute-start.6 = (f32[2,3,16,128]{3,2,1,0:T(8,128)S(1)}, f32[2,3,16,128]{3,2,1,0:T(8,128)S(1)}, u32[]{:S(2)}, u32[]{:S(2)}) collective-permute-start(f32[2,3,16,128]{3,2,1,0:T(8,128)S(1)} %get-tuple-element.93), channel_id=1, source_target_pairs={{0,8},{1,9},{2,10},{3,11},{8,16},{9,17},{10,18},{11,19},{12,4},{13... | collective-permute-start | bytes 147464 | tf_op jit(solution)/shard_map/ppermute | solution.py:479
  28.2 11.1 %collective-permute-start.7 = (f32[2,3,16,128]{3,2,1,0:T(8,128)S(1)}, f32[2,3,16,128]{3,2,1,0:T(8,128)S(1)}, u32[]{:S(2)}, u32[]{:S(2)}) collective-permute-start(f32[2,3,16,128]{3,2,1,0:T(8,128)S(1)} %get-tuple-element.94), channel_id=1, source_target_pairs={{0,10},{1,11},{2,12},{3,13},{8,18},{9,19},{10,20},{11,21},{12,6},{... | collective-permute-start | bytes 147464 | tf_op jit(solution)/shard_map/ppermute | solution.py:479
  33.4 6.3 %collective-permute-start.8 = (f32[2,3,16,128]{3,2,1,0:T(8,128)S(1)}, f32[2,3,16,128]{3,2,1,0:T(8,128)S(1)}, u32[]{:S(2)}, u32[]{:S(2)}) collective-permute-start(f32[2,3,16,128]{3,2,1,0:T(8,128)S(1)} %get-tuple-element.95), channel_id=1, source_target_pairs={{0,12},{1,13},{2,14},{3,15},{8,20},{9,21},{10,22},{11,23},{12,0},{... | collective-permute-start | bytes 147464 | tf_op jit(solution)/shard_map/ppermute | solution.py:479
  36.1 4.9 %collective-permute-start.9 = (f32[2,3,16,128]{3,2,1,0:T(8,128)S(1)}, f32[2,3,16,128]{3,2,1,0:T(8,128)S(1)}, u32[]{:S(2)}, u32[]{:S(2)}) collective-permute-start(f32[2,3,16,128]{3,2,1,0:T(8,128)S(1)} %get-tuple-element.96), channel_id=1, source_target_pairs={{0,14},{1,15},{2,8},{3,9},{8,22},{9,23},{10,16},{11,17},{12,2},{13... | collective-permute-start | bytes 147464 | tf_op jit(solution)/shard_map/ppermute | solution.py:479
  41.6 4.7 %collective-permute-start.10 = (f32[4,3,16,128]{3,2,1,0:T(8,128)S(1)}, f32[4,3,16,128]{3,2,1,0:T(8,128)S(1)}, u32[]{:S(2)}, u32[]{:S(2)}) collective-permute-start(f32[4,3,16,128]{3,2,1,0:T(8,128)S(1)} %get-tuple-element.98), channel_id=1, source_target_pairs={{0,1},{1,0},{2,3},{3,2},{4,5},{5,4},{6,7},{7,6},{8,9},{9,8},{10,11... | collective-permute-start | bytes 294920 | tf_op jit(solution)/shard_map/ppermute | solution.py:458
  49.9 5.4 %collective-permute-start.11 = (f32[4,3,16,128]{3,2,1,0:T(8,128)S(1)}, f32[4,3,16,128]{3,2,1,0:T(8,128)S(1)}, u32[]{:S(2)}, u32[]{:S(2)}) collective-permute-start(f32[4,3,16,128]{3,2,1,0:T(8,128)S(1)} %get-tuple-element.106), channel_id=1, source_target_pairs={{0,1},{1,0},{2,3},{3,2},{4,5},{5,4},{6,7},{7,6},{8,9},{9,8},{10,11... | collective-permute-start | bytes 294920 | tf_op jit(solution)/shard_map/ppermute | solution.py:458
  55.9 37.9 %collective-permute-start.12 = (f32[6,16,8,128]{3,2,1,0:T(8,128)S(1)}, f32[6,16,8,128]{3,2,1,0:T(8,128)S(1)}, u32[]{:S(2)}, u32[]{:S(2)}) collective-permute-start(f32[6,16,8,128]{3,2,1,0:T(8,128)S(1)} %get-tuple-element.108), channel_id=1, source_target_pairs={{0,1},{1,2},{2,3},{3,4},{4,5},{5,6},{6,7},{7,0},{8,9},{9,10},{10,1... | collective-permute-start | bytes 1179656 | tf_op jit(solution)/shard_map/ppermute | solution.py:454
  56.2 37.6 %collective-permute-start.13 = (f32[6,16,8,128]{3,2,1,0:T(8,128)S(1)}, f32[6,16,8,128]{3,2,1,0:T(8,128)S(1)}, u32[]{:S(2)}, u32[]{:S(2)}) collective-permute-start(f32[6,16,8,128]{3,2,1,0:T(8,128)S(1)} %get-tuple-element.109.refs_0_), channel_id=1, source_target_pairs={{0,7},{1,0},{2,1},{3,2},{4,3},{5,4},{6,5},{7,6},{8,15},{9,8},{10,9... | collective-permute-start | bytes 1179656 | tf_op jit(solution)/shard_map/ppermute | solution.py:454
  60.7 10.5 %collective-permute-start.14 = (f32[2,3,16,128]{3,2,1,0:T(8,128)S(1)}, f32[2,3,16,128]{3,2,1,0:T(8,128)S(1)}, u32[]{:S(2)}, u32[]{:S(2)}) collective-permute-start(f32[2,3,16,128]{3,2,1,0:T(8,128)S(1)} %get-tuple-element.110), channel_id=1, source_target_pairs={{0,2},{1,3},{2,4},{3,5},{4,6},{5,7},{6,0},{7,1},{8,10},{9,11},{10,... | collective-permute-start | bytes 147464 | tf_op jit(solution)/shard_map/ppermute | solution.py:465
  61.5 11.2 %collective-permute-start.15 = (f32[2,3,16,128]{3,2,1,0:T(8,128)S(1)}, f32[2,3,16,128]{3,2,1,0:T(8,128)S(1)}, u32[]{:S(2)}, u32[]{:S(2)}) collective-permute-start(f32[2,3,16,128]{3,2,1,0:T(8,128)S(1)} %get-tuple-element.111), channel_id=1, source_target_pairs={{0,4},{1,5},{2,6},{3,7},{4,0},{5,1},{6,2},{7,3},{8,12},{9,13},{10,... | collective-permute-start | bytes 147464 | tf_op jit(solution)/shard_map/ppermute | solution.py:465
  61.5 12.0 %collective-permute-start.16 = (f32[2,3,16,128]{3,2,1,0:T(8,128)S(1)}, f32[2,3,16,128]{3,2,1,0:T(8,128)S(1)}, u32[]{:S(2)}, u32[]{:S(2)}) collective-permute-start(f32[2,3,16,128]{3,2,1,0:T(8,128)S(1)} %get-tuple-element.112), channel_id=1, source_target_pairs={{0,6},{1,7},{2,0},{3,1},{4,2},{5,3},{6,4},{7,5},{8,14},{9,15},{10,... | collective-permute-start | bytes 147464 | tf_op jit(solution)/shard_map/ppermute | solution.py:465
  74.7 8.9 %collective-permute-start.17 = (f32[2,3,16,128]{3,2,1,0:T(8,128)S(1)}, f32[2,3,16,128]{3,2,1,0:T(8,128)S(1)}, u32[]{:S(2)}, u32[]{:S(2)}) collective-permute-start(f32[2,3,16,128]{3,2,1,0:T(8,128)S(1)} %get-tuple-element.113), channel_id=1, source_target_pairs={{0,8},{1,9},{2,10},{3,11},{8,16},{9,17},{10,18},{11,19},{12,4},{13... | collective-permute-start | bytes 147464 | tf_op jit(solution)/shard_map/ppermute | solution.py:479
  76.0 10.7 %collective-permute-start.18 = (f32[2,3,16,128]{3,2,1,0:T(8,128)S(1)}, f32[2,3,16,128]{3,2,1,0:T(8,128)S(1)}, u32[]{:S(2)}, u32[]{:S(2)}) collective-permute-start(f32[2,3,16,128]{3,2,1,0:T(8,128)S(1)} %get-tuple-element.114), channel_id=1, source_target_pairs={{0,10},{1,11},{2,12},{3,13},{8,18},{9,19},{10,20},{11,21},{12,6},{... | collective-permute-start | bytes 147464 | tf_op jit(solution)/shard_map/ppermute | solution.py:479
  80.4 6.7 %collective-permute-start.19 = (f32[2,3,16,128]{3,2,1,0:T(8,128)S(1)}, f32[2,3,16,128]{3,2,1,0:T(8,128)S(1)}, u32[]{:S(2)}, u32[]{:S(2)}) collective-permute-start(f32[2,3,16,128]{3,2,1,0:T(8,128)S(1)} %get-tuple-element.115), channel_id=1, source_target_pairs={{0,12},{1,13},{2,14},{3,15},{8,20},{9,21},{10,22},{11,23},{12,0},{... | collective-permute-start | bytes 147464 | tf_op jit(solution)/shard_map/ppermute | solution.py:479
  83.7 4.8 %collective-permute-start.20 = (f32[2,3,16,128]{3,2,1,0:T(8,128)S(1)}, f32[2,3,16,128]{3,2,1,0:T(8,128)S(1)}, u32[]{:S(2)}, u32[]{:S(2)}) collective-permute-start(f32[2,3,16,128]{3,2,1,0:T(8,128)S(1)} %get-tuple-element.116), channel_id=1, source_target_pairs={{0,14},{1,15},{2,8},{3,9},{8,22},{9,23},{10,16},{11,17},{12,2},{13... | collective-permute-start | bytes 147464 | tf_op jit(solution)/shard_map/ppermute | solution.py:479
  89.1 4.7 %collective-permute-start.21 = (f32[4,3,16,128]{3,2,1,0:T(8,128)S(1)}, f32[4,3,16,128]{3,2,1,0:T(8,128)S(1)}, u32[]{:S(2)}, u32[]{:S(2)}) collective-permute-start(f32[4,3,16,128]{3,2,1,0:T(8,128)S(1)} %get-tuple-element.118), channel_id=1, source_target_pairs={{0,1},{1,0},{2,3},{3,2},{4,5},{5,4},{6,7},{7,6},{8,9},{9,8},{10,11... | collective-permute-start | bytes 294920 | tf_op jit(solution)/shard_map/ppermute | solution.py:458
  97.4 5.3 %collective-permute-start.22 = (f32[4,3,16,128]{3,2,1,0:T(8,128)S(1)}, f32[4,3,16,128]{3,2,1,0:T(8,128)S(1)}, u32[]{:S(2)}, u32[]{:S(2)}) collective-permute-start(f32[4,3,16,128]{3,2,1,0:T(8,128)S(1)} %get-tuple-element.126), channel_id=1, source_target_pairs={{0,1},{1,0},{2,3},{3,2},{4,5},{5,4},{6,7},{7,6},{8,9},{9,8},{10,11... | collective-permute-start | bytes 294920 | tf_op jit(solution)/shard_map/ppermute | solution.py:458
  103.3 38.1 %collective-permute-start.23 = (f32[6,16,8,128]{3,2,1,0:T(8,128)S(1)}, f32[6,16,8,128]{3,2,1,0:T(8,128)S(1)}, u32[]{:S(2)}, u32[]{:S(2)}) collective-permute-start(f32[6,16,8,128]{3,2,1,0:T(8,128)S(1)} %get-tuple-element.128), channel_id=1, source_target_pairs={{0,1},{1,2},{2,3},{3,4},{4,5},{5,6},{6,7},{7,0},{8,9},{9,10},{10,1... | collective-permute-start | bytes 1179656 | tf_op jit(solution)/shard_map/ppermute | solution.py:454
  103.6 37.7 %collective-permute-start.24 = (f32[6,16,8,128]{3,2,1,0:T(8,128)S(1)}, f32[6,16,8,128]{3,2,1,0:T(8,128)S(1)}, u32[]{:S(2)}, u32[]{:S(2)}) collective-permute-start(f32[6,16,8,128]{3,2,1,0:T(8,128)S(1)} %get-tuple-element.129.refs_0_), channel_id=1, source_target_pairs={{0,7},{1,0},{2,1},{3,2},{4,3},{5,4},{6,5},{7,6},{8,15},{9,8},{10,9... | collective-permute-start | bytes 1179656 | tf_op jit(solution)/shard_map/ppermute | solution.py:454
  108.0 10.6 %collective-permute-start.25 = (f32[2,3,16,128]{3,2,1,0:T(8,128)S(1)}, f32[2,3,16,128]{3,2,1,0:T(8,128)S(1)}, u32[]{:S(2)}, u32[]{:S(2)}) collective-permute-start(f32[2,3,16,128]{3,2,1,0:T(8,128)S(1)} %get-tuple-element.130), channel_id=1, source_target_pairs={{0,2},{1,3},{2,4},{3,5},{4,6},{5,7},{6,0},{7,1},{8,10},{9,11},{10,... | collective-permute-start | bytes 147464 | tf_op jit(solution)/shard_map/ppermute | solution.py:465
  109.0 11.2 %collective-permute-start.26 = (f32[2,3,16,128]{3,2,1,0:T(8,128)S(1)}, f32[2,3,16,128]{3,2,1,0:T(8,128)S(1)}, u32[]{:S(2)}, u32[]{:S(2)}) collective-permute-start(f32[2,3,16,128]{3,2,1,0:T(8,128)S(1)} %get-tuple-element.131), channel_id=1, source_target_pairs={{0,4},{1,5},{2,6},{3,7},{4,0},{5,1},{6,2},{7,3},{8,12},{9,13},{10,... | collective-permute-start | bytes 147464 | tf_op jit(solution)/shard_map/ppermute | solution.py:465
  109.0 11.9 %collective-permute-start.27 = (f32[2,3,16,128]{3,2,1,0:T(8,128)S(1)}, f32[2,3,16,128]{3,2,1,0:T(8,128)S(1)}, u32[]{:S(2)}, u32[]{:S(2)}) collective-permute-start(f32[2,3,16,128]{3,2,1,0:T(8,128)S(1)} %get-tuple-element.132), channel_id=1, source_target_pairs={{0,6},{1,7},{2,0},{3,1},{4,2},{5,3},{6,4},{7,5},{8,14},{9,15},{10,... | collective-permute-start | bytes 147464 | tf_op jit(solution)/shard_map/ppermute | solution.py:465
  122.1 9.0 %collective-permute-start.28 = (f32[2,3,16,128]{3,2,1,0:T(8,128)S(1)}, f32[2,3,16,128]{3,2,1,0:T(8,128)S(1)}, u32[]{:S(2)}, u32[]{:S(2)}) collective-permute-start(f32[2,3,16,128]{3,2,1,0:T(8,128)S(1)} %get-tuple-element.133), channel_id=1, source_target_pairs={{0,8},{1,9},{2,10},{3,11},{8,16},{9,17},{10,18},{11,19},{12,4},{13... | collective-permute-start | bytes 147464 | tf_op jit(solution)/shard_map/ppermute | solution.py:479
  123.4 10.8 %collective-permute-start.29 = (f32[2,3,16,128]{3,2,1,0:T(8,128)S(1)}, f32[2,3,16,128]{3,2,1,0:T(8,128)S(1)}, u32[]{:S(2)}, u32[]{:S(2)}) collective-permute-start(f32[2,3,16,128]{3,2,1,0:T(8,128)S(1)} %get-tuple-element.134), channel_id=1, source_target_pairs={{0,10},{1,11},{2,12},{3,13},{8,18},{9,19},{10,20},{11,21},{12,6},{... | collective-permute-start | bytes 147464 | tf_op jit(solution)/shard_map/ppermute | solution.py:479
  127.6 6.8 %collective-permute-start.30 = (f32[2,3,16,128]{3,2,1,0:T(8,128)S(1)}, f32[2,3,16,128]{3,2,1,0:T(8,128)S(1)}, u32[]{:S(2)}, u32[]{:S(2)}) collective-permute-start(f32[2,3,16,128]{3,2,1,0:T(8,128)S(1)} %get-tuple-element.135), channel_id=1, source_target_pairs={{0,12},{1,13},{2,14},{3,15},{8,20},{9,21},{10,22},{11,23},{12,0},{... | collective-permute-start | bytes 147464 | tf_op jit(solution)/shard_map/ppermute | solution.py:479
  131.1 4.9 %collective-permute-start.31 = (f32[2,3,16,128]{3,2,1,0:T(8,128)S(1)}, f32[2,3,16,128]{3,2,1,0:T(8,128)S(1)}, u32[]{:S(2)}, u32[]{:S(2)}) collective-permute-start(f32[2,3,16,128]{3,2,1,0:T(8,128)S(1)} %get-tuple-element.136), channel_id=1, source_target_pairs={{0,14},{1,15},{2,8},{3,9},{8,22},{9,23},{10,16},{11,17},{12,2},{13... | collective-permute-start | bytes 147464 | tf_op jit(solution)/shard_map/ppermute | solution.py:479
  136.6 4.7 %collective-permute-start.32 = (f32[4,3,16,128]{3,2,1,0:T(8,128)S(1)}, f32[4,3,16,128]{3,2,1,0:T(8,128)S(1)}, u32[]{:S(2)}, u32[]{:S(2)}) collective-permute-start(f32[4,3,16,128]{3,2,1,0:T(8,128)S(1)} %get-tuple-element.138), channel_id=1, source_target_pairs={{0,1},{1,0},{2,3},{3,2},{4,5},{5,4},{6,7},{7,6},{8,9},{9,8},{10,11... | collective-permute-start | bytes 294920 | tf_op jit(solution)/shard_map/ppermute | solution.py:458
  144.9 5.4 %collective-permute-start.33 = (f32[4,3,16,128]{3,2,1,0:T(8,128)S(1)}, f32[4,3,16,128]{3,2,1,0:T(8,128)S(1)}, u32[]{:S(2)}, u32[]{:S(2)}) collective-permute-start(f32[4,3,16,128]{3,2,1,0:T(8,128)S(1)} %get-tuple-element.146), channel_id=1, source_target_pairs={{0,1},{1,0},{2,3},{3,2},{4,5},{5,4},{6,7},{7,6},{8,9},{9,8},{10,11... | collective-permute-start | bytes 294920 | tf_op jit(solution)/shard_map/ppermute | solution.py:458
  150.9 38.1 %collective-permute-start.34 = (f32[6,16,8,128]{3,2,1,0:T(8,128)S(1)}, f32[6,16,8,128]{3,2,1,0:T(8,128)S(1)}, u32[]{:S(2)}, u32[]{:S(2)}) collective-permute-start(f32[6,16,8,128]{3,2,1,0:T(8,128)S(1)} %get-tuple-element.148), channel_id=1, source_target_pairs={{0,1},{1,2},{2,3},{3,4},{4,5},{5,6},{6,7},{7,0},{8,9},{9,10},{10,1... | collective-permute-start | bytes 1179656 | tf_op jit(solution)/shard_map/ppermute | solution.py:454
  151.2 37.8 %collective-permute-start.35 = (f32[6,16,8,128]{3,2,1,0:T(8,128)S(1)}, f32[6,16,8,128]{3,2,1,0:T(8,128)S(1)}, u32[]{:S(2)}, u32[]{:S(2)}) collective-permute-start(f32[6,16,8,128]{3,2,1,0:T(8,128)S(1)} %get-tuple-element.149.refs_0_), channel_id=1, source_target_pairs={{0,7},{1,0},{2,1},{3,2},{4,3},{5,4},{6,5},{7,6},{8,15},{9,8},{10,9... | collective-permute-start | bytes 1179656 | tf_op jit(solution)/shard_map/ppermute | solution.py:454
  155.7 10.5 %collective-permute-start.36 = (f32[2,3,16,128]{3,2,1,0:T(8,128)S(1)}, f32[2,3,16,128]{3,2,1,0:T(8,128)S(1)}, u32[]{:S(2)}, u32[]{:S(2)}) collective-permute-start(f32[2,3,16,128]{3,2,1,0:T(8,128)S(1)} %get-tuple-element.150), channel_id=1, source_target_pairs={{0,2},{1,3},{2,4},{3,5},{4,6},{5,7},{6,0},{7,1},{8,10},{9,11},{10,... | collective-permute-start | bytes 147464 | tf_op jit(solution)/shard_map/ppermute | solution.py:465
  156.5 11.5 %collective-permute-start.37 = (f32[2,3,16,128]{3,2,1,0:T(8,128)S(1)}, f32[2,3,16,128]{3,2,1,0:T(8,128)S(1)}, u32[]{:S(2)}, u32[]{:S(2)}) collective-permute-start(f32[2,3,16,128]{3,2,1,0:T(8,128)S(1)} %get-tuple-element.151), channel_id=1, source_target_pairs={{0,4},{1,5},{2,6},{3,7},{4,0},{5,1},{6,2},{7,3},{8,12},{9,13},{10,... | collective-permute-start | bytes 147464 | tf_op jit(solution)/shard_map/ppermute | solution.py:465
  156.5 11.7 %collective-permute-start.38 = (f32[2,3,16,128]{3,2,1,0:T(8,128)S(1)}, f32[2,3,16,128]{3,2,1,0:T(8,128)S(1)}, u32[]{:S(2)}, u32[]{:S(2)}) collective-permute-start(f32[2,3,16,128]{3,2,1,0:T(8,128)S(1)} %get-tuple-element.152), channel_id=1, source_target_pairs={{0,6},{1,7},{2,0},{3,1},{4,2},{5,3},{6,4},{7,5},{8,14},{9,15},{10,... | collective-permute-start | bytes 147464 | tf_op jit(solution)/shard_map/ppermute | solution.py:465
  169.4 9.3 %collective-permute-start.39 = (f32[2,3,16,128]{3,2,1,0:T(8,128)S(1)}, f32[2,3,16,128]{3,2,1,0:T(8,128)S(1)}, u32[]{:S(2)}, u32[]{:S(2)}) collective-permute-start(f32[2,3,16,128]{3,2,1,0:T(8,128)S(1)} %get-tuple-element.153), channel_id=1, source_target_pairs={{0,8},{1,9},{2,10},{3,11},{8,16},{9,17},{10,18},{11,19},{12,4},{13... | collective-permute-start | bytes 147464 | tf_op jit(solution)/shard_map/ppermute | solution.py:479
  170.7 11.1 %collective-permute-start.40 = (f32[2,3,16,128]{3,2,1,0:T(8,128)S(1)}, f32[2,3,16,128]{3,2,1,0:T(8,128)S(1)}, u32[]{:S(2)}, u32[]{:S(2)}) collective-permute-start(f32[2,3,16,128]{3,2,1,0:T(8,128)S(1)} %get-tuple-element.154), channel_id=1, source_target_pairs={{0,10},{1,11},{2,12},{3,13},{8,18},{9,19},{10,20},{11,21},{12,6},{... | collective-permute-start | bytes 147464 | tf_op jit(solution)/shard_map/ppermute | solution.py:479
  174.6 7.2 %collective-permute-start.41 = (f32[2,3,16,128]{3,2,1,0:T(8,128)S(1)}, f32[2,3,16,128]{3,2,1,0:T(8,128)S(1)}, u32[]{:S(2)}, u32[]{:S(2)}) collective-permute-start(f32[2,3,16,128]{3,2,1,0:T(8,128)S(1)} %get-tuple-element.155), channel_id=1, source_target_pairs={{0,12},{1,13},{2,14},{3,15},{8,20},{9,21},{10,22},{11,23},{12,0},{... | collective-permute-start | bytes 147464 | tf_op jit(solution)/shard_map/ppermute | solution.py:479
  178.7 5.0 %collective-permute-start.42 = (f32[2,3,16,128]{3,2,1,0:T(8,128)S(1)}, f32[2,3,16,128]{3,2,1,0:T(8,128)S(1)}, u32[]{:S(2)}, u32[]{:S(2)}) collective-permute-start(f32[2,3,16,128]{3,2,1,0:T(8,128)S(1)} %get-tuple-element.156), channel_id=1, source_target_pairs={{0,14},{1,15},{2,8},{3,9},{8,22},{9,23},{10,16},{11,17},{12,2},{13... | collective-permute-start | bytes 147464 | tf_op jit(solution)/shard_map/ppermute | solution.py:479
  184.3 4.7 %collective-permute-start.43 = (f32[4,3,16,128]{3,2,1,0:T(8,128)S(1)}, f32[4,3,16,128]{3,2,1,0:T(8,128)S(1)}, u32[]{:S(2)}, u32[]{:S(2)}) collective-permute-start(f32[4,3,16,128]{3,2,1,0:T(8,128)S(1)} %get-tuple-element.158), channel_id=1, source_target_pairs={{0,1},{1,0},{2,3},{3,2},{4,5},{5,4},{6,7},{7,6},{8,9},{9,8},{10,11... | collective-permute-start | bytes 294920 | tf_op jit(solution)/shard_map/ppermute | solution.py:458
  (3 other events, 47.9 us)

commit v2 on v0

--- a/solution.py
+++ b/solution.py
@@ -11,6 +11,7 @@
 highest = lax.Precision.HIGHEST
 VMEM = pltpu.VMEM
 SMEM = pltpu.SMEM
+EXTRA = 4
 LOW = 8
 
 
@@ -37,13 +38,12 @@
         strip = self.axial // 4
         self.outer = ((0, strip), (self.axial - strip, self.axial))
         self.inner = ((strip, self.axial - strip),)
-        self.half = sectors // 2
-        self.per = -(-2 * self.fields // self.half)
-        self.dealt = (sectors, self.per, self.cycle, self.radial)
-
-    def combo(self, side, field, plane):
-        place = side * self.per * self.half + field * 2 + plane
-        return place // self.per, place % self.per
+        self.ghost = (2, self.fields, 2, self.cycle, self.radial)
+        self.deep = 8
+        self.full = self.cycle * sectors
+        self.mine = self.radial // sectors
+        self.wide = self.mine + 2 * EXTRA
+        self.packed = self.deep * self.cycle
 
 
 def count(ranges):
@@ -56,49 +56,202 @@
     high_ref[field, tile, row : row + 2, :] = value[plan.cycle - 2 :]
 
 
-def gather_planes(plan, buffer, upper, lower):
-    for field in range(plan.fields):
-        for plane in range(2):
-            piece, slot = plan.combo(0, field, plane)
-            buffer[piece, slot] = upper(field, plane)
-            piece, slot = plan.combo(1, field, plane)
-            buffer[piece, slot] = lower(field, plane)
-
-
-def clear_spare(plan, buffer):
-    used = {plan.combo(side, field, plane) for side in range(2) for field in range(plan.fields) for plane in range(2)}
-    for piece in range(plan.sectors):
-        for slot in range(plan.per):
-            if (piece, slot) not in used:
-                buffer[piece, slot] = jnp.zeros((plan.cycle, plan.radial), jnp.float32)
-
-
-def planes_kernel(plan, state, dealt, planes, sems):
-    copies = [
-        pltpu.make_async_copy(state.at[:, plan.axial - 2 : plan.axial], planes.at[0], sems.at[0]),
-        pltpu.make_async_copy(state.at[:, 0:2], planes.at[1], sems.at[1]),
-    ]
-    for item in copies:
-        item.start()
-    clear_spare(plan, dealt)
-    for item in copies:
-        item.wait()
-    gather_planes(plan, dealt, lambda f, p: planes[0, f, p], lambda f, p: planes[1, f, p])
-
-
-def first_planes(plan, state):
+def pack_kernel(plan, state, below, out, planes, tall, sem):
+    copy = pltpu.make_async_copy(state.at[:, plan.axial - plan.deep : plan.axial], planes, sem.at[0])
+    copy.start()
+    tall[...] = jnp.zeros(tall.shape, jnp.float32)
+    copy.wait()
+    for side, source in enumerate((planes, below)):
+        for field in range(plan.fields):
+            flat = source[field].reshape(plan.packed, plan.radial)
+            tall[EXTRA : EXTRA + plan.radial, :] = flat.T
+            for sector in range(plan.sectors):
+                out[sector, side * plan.fields + field] = tall[sector * plan.mine : sector * plan.mine + plan.wide, :]
+
+
+def pack(plan, state, below):
     return pl.pallas_call(
-        functools.partial(planes_kernel, plan),
-        in_specs=[whole(pl.ANY)],
+        functools.partial(pack_kernel, plan),
+        in_specs=[whole(pl.ANY), whole(VMEM)],
         out_specs=whole(VMEM),
-        out_shape=held(plan.dealt),
+        out_shape=jax.ShapeDtypeStruct((plan.sectors, 2 * plan.fields, plan.wide, plan.packed), jnp.float32),
         scratch_shapes=[
-            held((2, plan.fields, 2, plan.cycle, plan.radial)),
-            pltpu.SemaphoreType.DMA((2,)),
+            held((plan.fields, plan.deep, plan.cycle, plan.radial)),
+            held((plan.radial + 2 * EXTRA, plan.packed)),
+            pltpu.SemaphoreType.DMA((1,)),
         ],
         compiler_params=params(),
-        name="first_planes",
-    )(state)
+        name="pack_zone",
+    )(state, below)
+
+
+def zone_kernel(plan, place, offsets, speed, swirl, next_swirl, diffusion, coupling, weights, got, *refs):
+    to_here, to_next, base, now, later, spread, matrix, made = refs
+    fields, deep, cycle, full, wide = plan.fields, plan.deep, plan.cycle, plan.full, plan.wide
+    sections = offsets.shape[0]
+    row, sector = place[0], place[1]
+    terms = fields + 9
+    rows = slice(LOW, LOW + wide)
+    lane = lax.broadcasted_iota(jnp.int32, (wide, plan.packed), 1) // cycle
+    own_lane = lax.broadcasted_iota(jnp.int32, (plan.mine, plan.packed), 1) // cycle
+    at_radius = lax.broadcasted_iota(jnp.int32, (wide, full), 0) + sector * plan.mine - EXTRA
+    inside = (at_radius >= 0) & (at_radius < plan.radial)
+    block = plan.packed // cycle
+
+    for side, w in enumerate((swirl, next_swirl)):
+        for f, (axial, around, d, mix) in enumerate(coefficients(plan, speed, w, diffusion, coupling)):
+            for number, factor in enumerate((d, *mix, *axial, *around)):
+                spread[side * fields * terms + f * terms + number] = jnp.full((wide, full), factor, jnp.float32)
+
+    for buffer in (base, now, later):
+        for side in range(2):
+            def clear(field, carry, buffer=buffer, side=side):
+                buffer[side, field] = jnp.zeros(buffer.shape[2:], jnp.float32)
+                return carry
+
+            lax.fori_loop(0, fields, clear, 0)
+
+    for side in range(2):
+        def spread_out(field, carry, side=side):
+            for plane in range(deep):
+                parts = []
+                for first in range(0, plan.sectors, block):
+                    total = jnp.zeros((wide, plan.packed), jnp.float32)
+                    for number in range(min(block, plan.sectors - first)):
+                        turned = got[first + number, side * fields + field]
+                        turn = (number - plane) * cycle % plan.packed
+                        if turn:
+                            turned = pltpu.roll(turned, turn, 1)
+                        total = jnp.where(lane == number, turned, total)
+                    parts.append(total)
+                value = parts[0] if len(parts) == 1 else jnp.concatenate(parts, axis=1)
+                base[side, field, 2 + plane, rows, :] = value
+                now[side, field, 2 + plane, rows, :] = value
+            return carry
+
+        lax.fori_loop(0, fields, spread_out, 0)
+
+    for section in range(sections):
+        offset = offsets[section, jnp.minimum(row, offsets.shape[1] - 1)]
+        for side in range(2):
+            here = lax.rem(full - offset, full) if side == 0 else offset
+            shift, cell = here // cycle, lax.rem(here, cycle)
+            for target in range(plan.sectors):
+                matrix[target * cycle : (target + 1) * cycle, :] = pltpu.roll(
+                    weights[cell], lax.rem(target + shift, plan.sectors) * cycle, 1
+                )
+            other = 1 - side
+            first = 2 if other == 1 else deep
+            to = deep + 2 if side == 0 else 0
+            pairs = [(field, plane) for field in range(fields) for plane in range(2)]
+            values = [now[other, field, first + plane, rows, :] for field, plane in pairs]
+            turn = matrix[...]
+            together = wide % 8 == 0
+            if together:
+                values = [jnp.concatenate(values, axis=0)]
+            results = [
+                lax.dot_general(
+                    value, turn, (((1,), (1,)), ((), ())), precision=highest, preferred_element_type=jnp.float32
+                )
+                for value in values
+            ]
+            for number, (field, plane) in enumerate(pairs):
+                if together:
+                    value = results[0][number * wide : (number + 1) * wide]
+                else:
+                    value = results[number]
+                now[side, field, to + plane, rows, :] = value
+                made[side, field, 2 * section + plane] = now[side, field, to + plane, LOW + EXTRA : LOW + EXTRA + plan.mine, :]
+        if section == sections - 1:
+            break
+        size = deep - 2 * (section + 1)
+        step_size = time_step if section == sections - 2 else 0.5 * time_step
+        for side in range(2):
+            begin = 2 + (deep - size if side == 0 else 0)
+
+            def advance(number, carry, side=side, begin=begin, now=now, later=later, step_size=step_size):
+                plane = begin + number
+                center = [now[side, e, plane, rows, :] for e in range(fields)]
+                for f in range(fields):
+                    factor = lambda k: spread[side * fields * terms + f * terms + k]
+                    total = factor(0) * (
+                        now[side, f, plane, LOW - 1 : LOW - 1 + wide, :] + now[side, f, plane, LOW + 1 : LOW + 1 + wide, :]
+                    )
+                    for e in range(fields):
+                        total += factor(1 + e) * center[e]
+                    for place_at, by in enumerate((-2, -1, 1, 2)):
+                        total += factor(1 + fields + place_at) * now[side, f, plane + by, rows, :]
+                        total += factor(5 + fields + place_at) * pltpu.roll(center[f], -by % full, 1)
+                    value = base[side, f, plane, rows, :] + step_size * total
+                    later[side, f, plane, rows, :] = jnp.where(inside, value, 0.0)
+                return carry
+
+            lax.fori_loop(0, size, advance, 0)
+        now, later = later, now
+
+    has_next = (row < offsets.shape[1]).astype(jnp.float32)
+    for side, out in enumerate((to_here, to_next)):
+        def hand_out(field, carry, side=side, out=out):
+            for target in range(plan.sectors):
+                total = jnp.zeros((plan.mine, plan.packed), jnp.float32)
+                first = target // block * plan.packed
+                for number in range(2 * sections):
+                    turned = made[side, field, number, :, first : first + plan.packed]
+                    turn = (number - target % block) * cycle % plan.packed
+                    if turn:
+                        turned = pltpu.roll(turned, turn, 1)
+                    total = jnp.where(own_lane == number, turned, total)
+                out[target, field] = total * has_next if side == 0 else total
+            return carry
+
+        lax.fori_loop(0, fields, hand_out, 0)
+
+
+def zone(plan, place, offsets, scalars, next_swirl, weights, got):
+    speed, swirl, diffusion, coupling = scalars
+    buffer = held((2, plan.fields, plan.deep + 4, LOW + plan.wide + 8, plan.full))
+    sent = jax.ShapeDtypeStruct((plan.sectors, plan.fields, plan.mine, plan.packed), jnp.float32)
+    return pl.pallas_call(
+        functools.partial(zone_kernel, plan),
+        in_specs=[whole(SMEM)] * 7 + [whole(VMEM)] * 2,
+        out_specs=[whole(VMEM)] * 2,
+        out_shape=[sent] * 2,
+        scratch_shapes=[
+            buffer,
+            buffer,
+            buffer,
+            held((2 * plan.fields * (plan.fields + 9), plan.wide, plan.full)),
+            held((plan.full, plan.full)),
+            held((2, plan.fields, 2 * offsets.shape[0], plan.mine, plan.full)),
+        ],
+        compiler_params=pltpu.CompilerParams(vmem_limit_bytes=48 * 1024 * 1024),
+        name="step_zone",
+    )(place, offsets, speed, swirl, next_swirl, diffusion, coupling, weights, got)
+
+
+def unpack_kernel(plan, got, *refs):
+    *outs, tall = refs
+    for side in range(2):
+        for field in range(plan.fields):
+            for sector in range(plan.sectors):
+                tall[sector * plan.mine : (sector + 1) * plan.mine, :] = got[sector, side * plan.fields + field]
+            flat = tall[...].T
+            for section, out in enumerate(outs):
+                for plane in range(2):
+                    start = (2 * section + plane) * plan.cycle
+                    out[side, field, plane] = flat[start : start + plan.cycle]
+
+
+def unpack(plan, got, sections):
+    return pl.pallas_call(
+        functools.partial(unpack_kernel, plan),
+        in_specs=[whole(VMEM)],
+        out_specs=[whole(VMEM)] * sections,
+        out_shape=[held(plan.ghost)] * sections,
+        scratch_shapes=[held((plan.radial, plan.packed))],
+        compiler_params=params(),
+        name="unpack_ghosts",
+    )(got)
 
 
 def first_kernel(plan, state, lo_o, hi_o, lo_i, hi_i):
@@ -124,7 +277,7 @@
     return held((plan.fields, count(ranges) // 4, 8, plan.radial))
 
 
-def first_edges(plan, state):
+def first(plan, state):
     return pl.pallas_call(
         functools.partial(first_kernel, plan),
         in_specs=[whole(VMEM)],
@@ -133,45 +286,6 @@
         compiler_params=params(),
         name="first_edges",
     )(state)
-
-
-def interp_kernel(plan, section, place, offsets, weights, ring, *refs):
-    *_, out, spread = refs
-    full = plan.cycle * plan.sectors
-    row, sector = place[0], place[1]
-    up = sector < plan.half
-    at = jnp.where(up, jnp.minimum(row, offsets.shape[1] - 1), jnp.maximum(row - 1, 0))
-    offset = offsets[section, at]
-    offset = jnp.where(up, offset, lax.rem(full - offset, full))
-    turn = offset // plan.cycle
-    cell = lax.rem(offset, plan.cycle)
-    matrix = weights[cell]
-    for k in range(2 * plan.cycle):
-        spread[k] = jnp.broadcast_to(matrix[:, k : k + 1], (plan.cycle, plan.radial))
-    for target in range(plan.sectors):
-        here = lax.rem(target + turn, plan.sectors)
-        after = lax.rem(here + 1, plan.sectors)
-        for slot in range(plan.per):
-            total = None
-            for k in range(2 * plan.cycle):
-                cell_at = k % plan.cycle
-                row_value = ring[here if k < plan.cycle else after, slot, cell_at : cell_at + 1, :]
-                term = spread[k] * jnp.broadcast_to(row_value, (plan.cycle, plan.radial))
-                total = term if total is None else total + term
-            out[target, slot] = total
-
-
-def interp(plan, section, place, offsets, weights, got, after):
-    operands = [place, offsets, weights, near(got), *map(near, after)]
-    return pl.pallas_call(
-        functools.partial(interp_kernel, plan, section),
-        in_specs=[whole(SMEM), whole(SMEM)] + [whole(VMEM)] * (len(operands) - 2),
-        out_specs=whole(VMEM),
-        out_shape=held(plan.dealt),
-        scratch_shapes=[held((2 * plan.cycle, plan.cycle, plan.radial))],
-        compiler_params=params(),
-        name="interpolate",
-    )(*operands)
 
 
 def coefficients(plan, speed, swirl, diffusion, coupling):
@@ -208,8 +322,6 @@
         out_buf, sem = take(2)
     else:
         out, low_out, high_out, token = take(4)
-        if outer:
-            (dealt,) = take(1)
     work, spread = take(2)
     cycle, radial = plan.cycle, plan.radial
     terms = plan.fields + 9
@@ -237,8 +349,7 @@
     def fill(field, at, to):
         ref, side, place = source(at)
         if side is not None:
-            piece, slot = plan.combo(side, field, place)
-            work[field, to, LOW : LOW + cycle, :] = ref[piece, slot]
+            work[field, to, LOW : LOW + cycle, :] = ref[side, field, place]
         else:
             work[field, to, LOW : LOW + cycle, :] = ref[field, place]
 
@@ -317,10 +428,6 @@
             begin += high - low
         for item in copies:
             item.wait()
-    elif outer:
-        total = count(ranges)
-        clear_spare(plan, dealt)
-        gather_planes(plan, dealt, lambda f, p: out[f, total - 2 + p], lambda f, p: out[f, p])
     if stage < 3 or outer:
         token[...] = jnp.zeros(token.shape, jnp.float32)
 
@@ -353,8 +460,6 @@
         scratch = [held(chunk), pltpu.SemaphoreType.DMA((len(ranges),))] + scratch
     else:
         out_shape = [held(chunk), edge_shape(plan, ranges), edge_shape(plan, ranges), token]
-        if outer:
-            out_shape.append(held(plan.dealt))
         out_specs = [whole(VMEM)] * len(out_shape)
     return pl.pallas_call(
         functools.partial(stage_kernel, plan, stage, outer),
@@ -376,46 +481,39 @@
     return lax.ppermute(high_edges, "sector", ahead), lax.ppermute(low_edges, "sector", back)
 
 
-def row_hop(plan, value):
-    rows = lax.axis_size("row")
-    route = []
-    for row in range(rows):
-        for sector in range(plan.sectors):
-            target = row + 1 if sector < plan.half else row - 1
-            if 0 <= target < rows:
-                route.append((row * plan.sectors + sector, target * plan.sectors + sector))
-    return lax.ppermute(value, ("row", "sector"), route)
-
-
 def on_device(state, interp_blocks, rotor_offset, axial_speed, row_swirl, diffusivity, coupling):
     plan = Plan(state, lax.axis_size("sector"))
+    rows = lax.axis_size("row")
+    sections = rotor_offset.shape[0]
     place = jnp.stack([lax.axis_index("row"), lax.axis_index("sector")]).astype(jnp.int32)
     scalars = (axial_speed, row_swirl, diffusivity, coupling)
-
-    dealt = first_planes(plan, state)
-    lo_o, hi_o, lo_i, hi_i = first_edges(plan, state)
+    back = [(row + 1, row) for row in range(rows - 1)]
+    ahead = [(row, row + 1) for row in range(rows - 1)]
+
+    below = lax.ppermute(state[:, : plan.deep], "row", back)
+    next_swirl = lax.ppermute(row_swirl, "row", back)
+    got = lax.all_to_all(pack(plan, state, below), "sector", 0, 0, tiled=True)
+    weights = jnp.pad(interp_blocks, ((0, 0), (0, 0), (0, plan.full - interp_blocks.shape[2])))
+    downstream, to_next = zone(plan, place, rotor_offset, scalars, next_swirl, weights, got)
+    upstream = lax.ppermute(to_next, "row", ahead)
+    returned = lax.all_to_all(jnp.concatenate([upstream, downstream], axis=1), "sector", 0, 0, tiled=True)
+    ghosts = unpack(plan, returned, sections)
+
+    lo_o, hi_o, lo_i, hi_i = first(plan, state)
     outer_edges, inner_edges = (lo_o, hi_o), (lo_i, hi_i)
-    chunks, waited = None, ()
-    history = []
+    chunks, history = None, []
     for stage in range(4):
-        got = lax.all_to_all(dealt, "sector", 0, 0, tiled=True)
-        outer_halos = exchange(outer_edges)
-        made = interp(plan, stage, place, rotor_offset, interp_blocks, got, waited)
-        hopped = row_hop(plan, made)
-        ghosts = lax.all_to_all(hopped, "sector", 0, 0, tiled=True)
-        inner_edges = lax.optimization_barrier((*inner_edges, ghosts))[:2]
-        inner_halos = exchange(inner_edges)
+        outer_halos, inner_halos = exchange(outer_edges), exchange(inner_edges)
         last = stage == 3
         older = [(history[0][i], history[1][i]) if last else () for i in range(2)]
-        out_o, *rest = stage_call(plan, stage, True, scalars, state, chunks, outer_halos, ghosts, older[0])
+        out_o, *rest = stage_call(plan, stage, True, scalars, state, chunks, outer_halos, ghosts[stage], older[0])
         token = rest[0] if last else rest[2]
         out_i, *rest_i = stage_call(
             plan, stage, False, scalars, state, chunks, inner_halos, token, older[1], out_o if last else None
         )
         if last:
             return out_i
-        outer_edges, dealt = rest[:2], rest[3]
-        inner_edges, waited = rest_i[:2], rest_i[2:]
+        outer_edges, inner_edges = rest[:2], rest_i[:2]
         chunks = (out_o, out_i)
         history.append(chunks)
 

time: 248 us -> 166 us (0.67)
  the two profiles are of different devices: /device:TPU:1 before, /device:TPU:0 now
where the time goes in v2:
time: 166 us; the launch traced here: 164 us
  starting transfers between devices  64.8 us (39%)
  Pallas kernels  54.2 us (33%)
  waiting for transfers between devices  40.3 us (24%)
  local copies, waits for them, and re-layouts  2.96 us (2%)
    pallas_call x8, Pallas kernels, stage_call(): pl.pallas_call(functools.partial(stage_kernel, plan, stage, outer), in_sp...  36.6 us
    ppermute x8, starting transfers between devices, exchange(): lax.ppermute(low_edges, 'sector', back)  28.4 us
    all_to_all x1, waiting for transfers between devices, on_device(): got = lax.all_to_all(pack(plan, state, below), 'sector', 0, 0, tiled=True)  20.1 us
    ppermute x8, starting transfers between devices, exchange(): lax.ppermute(high_edges, 'sector', ahead)  17.8 us
    pallas_call x1, Pallas kernels, zone(): pl.pallas_call(functools.partial(zone_kernel, plan), in_specs=[whole(SMEM...  13.5 us
    all_to_all x1, starting transfers between devices, on_device(): got = lax.all_to_all(pack(plan, state, below), 'sector', 0, 0, tiled=True)  7.42 us
    all_to_all x1, waiting for transfers between devices, on_device(): lax.all_to_all(jnp.concatenate([upstream, downstream], axis=1), 'sector',...  7.17 us
    ppermute x1, waiting for transfers between devices, on_device(): next_swirl = lax.ppermute(row_swirl, 'row', back)  5.8 us
  transfers between devices with their start and end apart: 21, of which 9 were waited for; matrix products, arithmetic and copies ran while one was open for 0% of the time, Pallas kernels for 21%

profile of v2, /device:TPU:0, one launch (start us, length us, event | category | flops | bytes accessed | tf_op | source)
XLA Modules:
  0.0 164.2 jit_solution(17772483372276537799)
XLA Ops:
  0.0 1.0 slice.3
  1.0 1.3 collective-permute-start.3
  2.3 2.3 %collective-permute-done.3.below = f32[6,8,16,128]{3,2,1,0:T(8,128)S(1)} collective-permute-done((f32[6,8,16,128]{3,2,1,0:T(8,128)S(1)}, f32[6,8,16,128]{3,2,1,0:T(8,128)S(1)}, u32[]{:S(2)}, u32[]{:S(2)}) %collective-permute-start.3) | collective-permute-done | bytes 393248 | tf_op jit(solution)/shard_map/ppermute | solution.py:493
  4.6 1.9 %copy-done = f32[6,64,16,128]{3,2,1,0:T(8,128)S(1)} copy-done((f32[6,64,16,128]{3,2,1,0:T(8,128)S(1)}, f32[6,64,16,128]{3,2,1,0:T(8,128)}, u32[]{:S(2)}) %copy-start) | copy-done | bytes 3145752
  6.5 1.4 pack_zone.1
  8.0 0.0 copy-start.6
  8.0 0.0 copy-start.2
  8.0 0.0 copy-start.3
  8.0 0.0 copy-start.4
  8.0 0.0 copy-start.5
  8.0 7.4 %all-to-all-start = ((f32[8,12,24,128]{3,2,1,0:T(8,128)}), f32[8,12,24,128]{3,2,1,0:T(8,128)S(1)}, u32[]{:S(2)}, u32[]{:S(2)}) async-start(f32[8,12,24,128]{3,2,1,0:T(8,128)} %pack_zone.1), calls=%async_computation | async-start | bytes 2359296 | tf_op jit(solution)/shard_map/all_to_all | solution.py:495
  15.5 1.3 collective-permute-start.2
  17.4 0.1 pad_add_fusion.place
  17.5 5.8 %collective-permute-done.2.next_swirl = f32[1]{0:T(128)} collective-permute-done((f32[1]{0:T(128)}, f32[1]{0:T(128)}, u32[]{:S(2)}, u32[]{:S(2)}) %collective-permute-start.2) | collective-permute-done | bytes 36 | tf_op jit(solution)/shard_map/ppermute | solution.py:494
  23.3 20.1 %all-to-all-done.got = f32[8,12,24,128]{3,2,1,0:T(8,128)S(1)} async-done(((f32[8,12,24,128]{3,2,1,0:T(8,128)}), f32[8,12,24,128]{3,2,1,0:T(8,128)S(1)}, u32[]{:S(2)}, u32[]{:S(2)}) %all-to-all-start) | async-done | bytes 1179680 | tf_op jit(solution)/shard_map/all_to_all | solution.py:495
  43.4 13.5 %step_zone.1 = (f32[8,6,16,128]{3,2,1,0:T(8,128)S(1)}, f32[8,6,16,128]{3,2,1,0:T(8,128)S(1)}) custom-call(s32[2]{0:T(128)S(1)} %pad_add_fusion.place, s32[4,3]{1,0:T(4,128)S(1)} %copy-done.5, f32[6]{0:T(128)S(1)} %copy-done.3, f32[1]{0:T(128)S(6)} %copy.10.swirl, f32[1]{0:T(128)} %collective-permute-done.2.next_swirl, f32[6]{0:T(128)S(1)} %copy-done.4, ...), custom_call_target="tpu_custom_call" | custom-call | tf_op jit(solution)/shard_map/step_zone/pallas_call | solution.py:214
  56.9 4.3 %collective-permute-start.4 = (f32[8,6,16,128]{3,2,1,0:T(8,128)S(1)}, f32[8,6,16,128]{3,2,1,0:T(8,128)S(1)}, u32[]{:S(2)}, u32[]{:S(2)}) collective-permute-start(f32[8,6,16,128]{3,2,1,0:T(8,128)S(1)} %get-tuple-element.40), channel_id=1, source_target_pairs={{0,8},{8,16},{16,24},{1,9},{9,17},{17,25},{2,10},{10,18},{18,26},{... | collective-permute-start | bytes 1179656 | tf_op jit(solution)/shard_map/ppermute | solution.py:498
  61.2 1.3 collective-permute-done.4
  62.6 0.9 pad_maximum_fusion
  63.5 4.3 %all-to-all-start.1 = ((f32[8,12,16,128]{3,2,1,0:T(8,128)}), f32[8,12,16,128]{3,2,1,0:T(8,128)}, u32[]{:S(2)}, u32[]{:S(2)}) async-start(f32[8,12,16,128]{3,2,1,0:T(8,128)} %pad_maximum_fusion), calls=%async_computation.1 | async-start | bytes 1572864 | tf_op jit(solution)/shard_map/all_to_all | solution.py:499
  67.9 1.3 first_edges.1
  69.1 1.9 %collective-permute-start = (f32[6,8,8,128]{3,2,1,0:T(8,128)}, f32[6,8,8,128]{3,2,1,0:T(8,128)}, u32[]{:S(2)}, u32[]{:S(2)}) collective-permute-start(f32[6,8,8,128]{3,2,1,0:T(8,128)} %get-tuple-element.38), channel_id=1, source_target_pairs={{0,1},{1,2},{2,3},{3,4},{4,5},{5,6},{6,7},{7,0},{8,9},{9,10},{10,1... | collective-permute-start | bytes 589832 | tf_op jit(solution)/shard_map/ppermute | solution.py:481
  71.0 2.8 %collective-permute-start.1 = (f32[6,8,8,128]{3,2,1,0:T(8,128)}, f32[6,8,8,128]{3,2,1,0:T(8,128)}, u32[]{:S(2)}, u32[]{:S(2)}) collective-permute-start(f32[6,8,8,128]{3,2,1,0:T(8,128)} %get-tuple-element.39), channel_id=1, source_target_pairs={{0,7},{1,0},{2,1},{3,2},{4,3},{5,4},{6,5},{7,6},{8,15},{9,8},{10,9... | collective-permute-start | bytes 589832 | tf_op jit(solution)/shard_map/ppermute | solution.py:481
  73.9 4.7 %collective-permute-start.6 = (f32[6,8,8,128]{3,2,1,0:T(8,128)}, f32[6,8,8,128]{3,2,1,0:T(8,128)S(1)}, u32[]{:S(2)}, u32[]{:S(2)}) collective-permute-start(f32[6,8,8,128]{3,2,1,0:T(8,128)} %get-tuple-element.45), channel_id=1, source_target_pairs={{0,7},{1,0},{2,1},{3,2},{4,3},{5,4},{6,5},{7,6},{8,15},{9,8},{10,9... | collective-permute-start | bytes 589832 | tf_op jit(solution)/shard_map/ppermute | solution.py:481
  78.6 7.2 %all-to-all-done.1.got = f32[8,12,16,128]{3,2,1,0:T(8,128)} async-done(((f32[8,12,16,128]{3,2,1,0:T(8,128)}), f32[8,12,16,128]{3,2,1,0:T(8,128)}, u32[]{:S(2)}, u32[]{:S(2)}) %all-to-all-start.1) | async-done | bytes 786464 | tf_op jit(solution)/shard_map/all_to_all | solution.py:499
  85.8 1.4 unpack_ghosts.1
  87.2 1.4 collective-permute-done.refs_1_
  88.5 4.4 %stage0_outer.1 = (f32[6,32,16,128]{3,2,1,0:T(8,128)S(1)}, f32[6,8,8,128]{3,2,1,0:T(8,128)S(1)}, f32[6,8,8,128]{3,2,1,0:T(8,128)S(1)}, f32[8,128]{1,0:T(8,128)S(1)}) custom-call(f32[6]{0:T(128)S(1)} %copy-done.3, f32[1]{0:T(128)S(6)} %copy.10.swirl, f32[6]{0:T(128)S(1)} %copy-done.4, f32[6,6]{1,0:T(8,128)S(1)} %copy-done.2, ...), custom_call_target="tpu_custom_call" | custom-call | tf_op jit(solution)/shard_map/stage0_outer/pallas_call | solution.py:464
  92.9 10.4 %collective-permute-start.7 = (f32[6,8,8,128]{3,2,1,0:T(8,128)S(1)}, f32[6,8,8,128]{3,2,1,0:T(8,128)S(1)}, u32[]{:S(2)}, u32[]{:S(2)}) collective-permute-start(f32[6,8,8,128]{3,2,1,0:T(8,128)S(1)} %get-tuple-element.48), channel_id=1, source_target_pairs={{0,1},{1,2},{2,3},{3,4},{4,5},{5,6},{6,7},{7,0},{8,9},{9,10},{10,1... | collective-permute-start | bytes 589832 | tf_op jit(solution)/shard_map/ppermute | solution.py:481
  103.3 4.6 %stage0_inner.1 = (f32[6,32,16,128]{3,2,1,0:T(8,128)S(1)}, f32[6,8,8,128]{3,2,1,0:T(8,128)S(1)}, f32[6,8,8,128]{3,2,1,0:T(8,128)S(1)}, f32[8,128]{1,0:T(8,128)}) custom-call(f32[6]{0:T(128)S(1)} %copy-done.3, f32[1]{0:T(128)S(6)} %copy.10.swirl, f32[6]{0:T(128)S(1)} %copy-done.4, f32[6,6]{1,0:T(8,128)S(1)} %copy-done.2, f32[6,64,16,128]{3,2,1,0:T(8,128)S(1)} %copy-done.1, ...), custom_call_target="tpu_custom_call" | custom-call | tf_op jit(solution)/shard_map/stage0_inner/pallas_call | solution.py:464
  107.9 2.0 %collective-permute-start.9 = (f32[6,8,8,128]{3,2,1,0:T(8,128)S(1)}, f32[6,8,8,128]{3,2,1,0:T(8,128)S(1)}, u32[]{:S(2)}, u32[]{:S(2)}) collective-permute-start(f32[6,8,8,128]{3,2,1,0:T(8,128)S(1)} %get-tuple-element.52), channel_id=1, source_target_pairs={{0,1},{1,2},{2,3},{3,4},{4,5},{5,6},{6,7},{7,0},{8,9},{9,10},{10,1... | collective-permute-start | bytes 589832 | tf_op jit(solution)/shard_map/ppermute | solution.py:481
  110.0 2.7 %collective-permute-start.10 = (f32[6,8,8,128]{3,2,1,0:T(8,128)S(1)}, f32[6,8,8,128]{3,2,1,0:T(8,128)S(1)}, u32[]{:S(2)}, u32[]{:S(2)}) collective-permute-start(f32[6,8,8,128]{3,2,1,0:T(8,128)S(1)} %get-tuple-element.53), channel_id=1, source_target_pairs={{0,7},{1,0},{2,1},{3,2},{4,3},{5,4},{6,5},{7,6},{8,15},{9,8},{10,9... | collective-permute-start | bytes 589832 | tf_op jit(solution)/shard_map/ppermute | solution.py:481
  112.7 4.0 %stage1_outer.1 = (f32[6,32,16,128]{3,2,1,0:T(8,128)S(1)}, f32[6,8,8,128]{3,2,1,0:T(8,128)S(1)}, f32[6,8,8,128]{3,2,1,0:T(8,128)S(1)}, f32[8,128]{1,0:T(8,128)S(1)}) custom-call(f32[6]{0:T(128)S(1)} %copy-done.3, f32[1]{0:T(128)S(6)} %copy.10.swirl, f32[6]{0:T(128)S(1)} %copy-done.4, f32[6,6]{1,0:T(8,128)S(1)} %copy-done.2, ...), custom_call_target="tpu_custom_call" | custom-call | tf_op jit(solution)/shard_map/stage1_outer/pallas_call | solution.py:464
  116.7 2.1 %collective-permute-start.11 = (f32[6,8,8,128]{3,2,1,0:T(8,128)S(1)}, f32[6,8,8,128]{3,2,1,0:T(8,128)S(1)}, u32[]{:S(2)}, u32[]{:S(2)}) collective-permute-start(f32[6,8,8,128]{3,2,1,0:T(8,128)S(1)} %get-tuple-element.56), channel_id=1, source_target_pairs={{0,1},{1,2},{2,3},{3,4},{4,5},{5,6},{6,7},{7,0},{8,9},{9,10},{10,1... | collective-permute-start | bytes 589832 | tf_op jit(solution)/shard_map/ppermute | solution.py:481
  118.7 2.7 %collective-permute-start.12 = (f32[6,8,8,128]{3,2,1,0:T(8,128)S(1)}, f32[6,8,8,128]{3,2,1,0:T(8,128)S(1)}, u32[]{:S(2)}, u32[]{:S(2)}) collective-permute-start(f32[6,8,8,128]{3,2,1,0:T(8,128)S(1)} %get-tuple-element.57), channel_id=1, source_target_pairs={{0,7},{1,0},{2,1},{3,2},{4,3},{5,4},{6,5},{7,6},{8,15},{9,8},{10,9... | collective-permute-start | bytes 589832 | tf_op jit(solution)/shard_map/ppermute | solution.py:481
  121.4 0.3 collective-permute-done.10.refs_4_
  121.8 4.6 %stage1_inner.1 = (f32[6,32,16,128]{3,2,1,0:T(8,128)S(1)}, f32[6,8,8,128]{3,2,1,0:T(8,128)S(1)}, f32[6,8,8,128]{3,2,1,0:T(8,128)S(1)}, f32[8,128]{1,0:T(8,128)}) custom-call(f32[6]{0:T(128)S(1)} %copy-done.3, f32[1]{0:T(128)S(6)} %copy.10.swirl, f32[6]{0:T(128)S(1)} %copy-done.4, f32[6,6]{1,0:T(8,128)S(1)} %copy-done.2, f32[6,64,16,128]{3,2,1,0:T(8,128)S(1)} %copy-done.1, ...), custom_call_target="tpu_custom_call" | custom-call | tf_op jit(solution)/shard_map/stage1_inner/pallas_call | solution.py:464
  126.4 1.4 collective-permute-start.13
  127.7 3.4 %collective-permute-start.14 = (f32[6,8,8,128]{3,2,1,0:T(8,128)S(1)}, f32[6,8,8,128]{3,2,1,0:T(8,128)S(1)}, u32[]{:S(2)}, u32[]{:S(2)}) collective-permute-start(f32[6,8,8,128]{3,2,1,0:T(8,128)S(1)} %get-tuple-element.61), channel_id=1, source_target_pairs={{0,7},{1,0},{2,1},{3,2},{4,3},{5,4},{6,5},{7,6},{8,15},{9,8},{10,9... | collective-permute-start | bytes 589832 | tf_op jit(solution)/shard_map/ppermute | solution.py:481
  131.1 4.0 %stage2_outer.1 = (f32[6,32,16,128]{3,2,1,0:T(8,128)S(1)}, f32[6,8,8,128]{3,2,1,0:T(8,128)S(1)}, f32[6,8,8,128]{3,2,1,0:T(8,128)S(1)}, f32[8,128]{1,0:T(8,128)S(1)}) custom-call(f32[6]{0:T(128)S(1)} %copy-done.3, f32[1]{0:T(128)S(6)} %copy.10.swirl, f32[6]{0:T(128)S(1)} %copy-done.4, f32[6,6]{1,0:T(8,128)S(1)} %copy-done.2, ...), custom_call_target="tpu_custom_call" | custom-call | tf_op jit(solution)/shard_map/stage2_outer/pallas_call | solution.py:464
  135.1 0.1 collective-permute-start.17
  135.2 7.3 %collective-permute-start.18 = (f32[6,8,8,128]{3,2,1,0:T(8,128)S(1)}, f32[6,8,8,128]{3,2,1,0:T(8,128)S(1)}, u32[]{:S(2)}, u32[]{:S(2)}) collective-permute-start(f32[6,8,8,128]{3,2,1,0:T(8,128)S(1)} %get-tuple-element.67), channel_id=1, source_target_pairs={{0,7},{1,0},{2,1},{3,2},{4,3},{5,4},{6,5},{7,6},{8,15},{9,8},{10,9... | collective-permute-start | bytes 589832 | tf_op jit(solution)/shard_map/ppermute | solution.py:481
  142.5 4.6 %stage2_inner.1 = (f32[6,32,16,128]{3,2,1,0:T(8,128)S(1)}, f32[6,8,8,128]{3,2,1,0:T(8,128)S(1)}, f32[6,8,8,128]{3,2,1,0:T(8,128)S(1)}, f32[8,128]{1,0:T(8,128)}) custom-call(f32[6]{0:T(128)S(1)} %copy-done.3, f32[1]{0:T(128)S(6)} %copy.10.swirl, f32[6]{0:T(128)S(1)} %copy-done.4, f32[6,6]{1,0:T(8,128)S(1)} %copy-done.2, f32[6,64,16,128]{3,2,1,0:T(8,128)S(1)} %copy-done.1, ...), custom_call_target="tpu_custom_call" | custom-call | tf_op jit(solution)/shard_map/stage2_inner/pallas_call | solution.py:464
  147.1 4.7 %collective-permute-start.16 = (f32[6,8,8,128]{3,2,1,0:T(8,128)S(1)}, f32[6,8,8,128]{3,2,1,0:T(8,128)S(1)}, u32[]{:S(2)}, u32[]{:S(2)}) collective-permute-start(f32[6,8,8,128]{3,2,1,0:T(8,128)S(1)} %get-tuple-element.65), channel_id=1, source_target_pairs={{0,7},{1,0},{2,1},{3,2},{4,3},{5,4},{6,5},{7,6},{8,15},{9,8},{10,9... | collective-permute-start | bytes 589832 | tf_op jit(solution)/shard_map/ppermute | solution.py:481
  151.8 5.2 %stage3_outer.1 = (f32[6,64,16,128]{3,2,1,0:T(8,128)}, f32[8,128]{1,0:T(8,128)S(1)}) custom-call(f32[6]{0:T(128)S(1)} %copy-done.3, f32[1]{0:T(128)S(6)} %copy.10.swirl, f32[6]{0:T(128)S(1)} %copy-done.4, f32[6,6]{1,0:T(8,128)S(1)} %copy-done.2, f32[6,64,16,128]{3,2,1,0:T(8,128)S(1)} %copy-done.1, f32[6,32,16,128]{3,2,1,0:T(8,128)S(1)} %get-tuple-element.59.refs_1_, ...), custom_call_target="tpu_custom_call" | custom-call | tf_op jit(solution)/shard_map/stage3_outer/pallas_call | solution.py:464
  157.0 0.2 collective-permute-done.15.refs_3_
  157.3 1.7 %collective-permute-done.16.refs_4_ = f32[6,8,8,128]{3,2,1,0:T(8,128)S(1)} collective-permute-done((f32[6,8,8,128]{3,2,1,0:T(8,128)S(1)}, f32[6,8,8,128]{3,2,1,0:T(8,128)S(1)}, u32[]{:S(2)}, u32[]{:S(2)}) %collective-permute-start.16) | collective-permute-done | bytes 196640 | tf_op jit(solution)/shard_map/ppermute | solution.py:481
  159.0 5.2 %stage3_inner.1 = f32[6,64,16,128]{3,2,1,0:T(8,128)} custom-call(f32[6]{0:T(128)S(1)} %copy-done.3, f32[1]{0:T(128)S(6)} %copy.10.swirl, f32[6]{0:T(128)S(1)} %copy-done.4, f32[6,6]{1,0:T(8,128)S(1)} %copy-done.2, f32[6,64,16,128]{3,2,1,0:T(8,128)S(1)} %copy-done.1, ...), custom_call_target="tpu_custom_call", output_to_operand_aliasing={{}: (12, {})} | custom-call | tf_op jit(solution)/shard_map/stage3_inner/pallas_call | solution.py:464
  (24 shorter events, 0.1 us)
Async XLA Ops:
  1.0 3.6 %collective-permute-start.3 = (f32[6,8,16,128]{3,2,1,0:T(8,128)S(1)}, f32[6,8,16,128]{3,2,1,0:T(8,128)S(1)}, u32[]{:S(2)}, u32[]{:S(2)}) collective-permute-start(f32[6,8,16,128]{3,2,1,0:T(8,128)S(1)} %slice.3), channel_id=1, source_target_pairs={{8,0},{16,8},{24,16},{9,1},{17,9},{25,17},{10,2},{18,10},{26,18},{... | collective-permute-start | bytes 1179656 | tf_op jit(solution)/shard_map/ppermute | solution.py:493
  4.6 1.9 %copy-start = (f32[6,64,16,128]{3,2,1,0:T(8,128)S(1)}, f32[6,64,16,128]{3,2,1,0:T(8,128)}, u32[]{:S(2)}) copy-start(f32[6,64,16,128]{3,2,1,0:T(8,128)} %refs_0_.15) | copy-start | bytes 9437188
  8.0 9.4 %copy-start.6 = (f32[16,16,32]{2,1,0:T(8,128)S(1)}, f32[16,16,32]{2,1,0:T(8,128)}, u32[]{:S(2)}) copy-start(f32[16,16,32]{2,1,0:T(8,128)} %param.8) | copy-start | bytes 98308
  8.0 35.4 %copy-start.2 = (f32[6,6]{1,0:T(8,128)S(1)}, f32[6,6]{1,0:T(8,128)}, u32[]{:S(2)}) copy-start(f32[6,6]{1,0:T(8,128)} %coupling.17) | copy-start | bytes 436
  8.0 35.4 %copy-start.3 = (f32[6]{0:T(128)S(1)}, f32[6]{0:T(128)}, u32[]{:S(2)}) copy-start(f32[6]{0:T(128)} %speed.17) | copy-start | bytes 76
  8.0 35.4 %copy-start.4 = (f32[6]{0:T(128)S(1)}, f32[6]{0:T(128)}, u32[]{:S(2)}) copy-start(f32[6]{0:T(128)} %diffusion.17) | copy-start | bytes 76
  8.0 35.4 %copy-start.5 = (s32[4,3]{1,0:T(4,128)S(1)}, s32[4,3]{1,0:T(4,128)}, u32[]{:S(2)}) copy-start(s32[4,3]{1,0:T(4,128)} %offsets.1) | copy-start | bytes 148
  8.0 35.3 %all-to-all-start = ((f32[8,12,24,128]{3,2,1,0:T(8,128)}), f32[8,12,24,128]{3,2,1,0:T(8,128)S(1)}, u32[]{:S(2)}, u32[]{:S(2)}) async-start(f32[8,12,24,128]{3,2,1,0:T(8,128)} %pack_zone.1), calls=%async_computation | async-start | bytes 2359296 | tf_op jit(solution)/shard_map/all_to_all | solution.py:495
  15.5 7.8 %collective-permute-start.2 = (f32[1]{0:T(128)}, f32[1]{0:T(128)}, u32[]{:S(2)}, u32[]{:S(2)}) collective-permute-start(f32[1]{0:T(128)} %param.11), channel_id=1, source_target_pairs={{8,0},{16,8},{24,16},{9,1},{17,9},{25,17},{10,2},{18,10},{26,18},{... | collective-permute-start | bytes 20 | tf_op jit(solution)/shard_map/ppermute | solution.py:494
  56.9 5.6 %collective-permute-start.4 = (f32[8,6,16,128]{3,2,1,0:T(8,128)S(1)}, f32[8,6,16,128]{3,2,1,0:T(8,128)S(1)}, u32[]{:S(2)}, u32[]{:S(2)}) collective-permute-start(f32[8,6,16,128]{3,2,1,0:T(8,128)S(1)} %get-tuple-element.40), channel_id=1, source_target_pairs={{0,8},{8,16},{16,24},{1,9},{9,17},{17,25},{2,10},{10,18},{18,26},{... | collective-permute-start | bytes 1179656 | tf_op jit(solution)/shard_map/ppermute | solution.py:498
  62.6 5.3 %copy-start.1 = (f32[6,64,16,128]{3,2,1,0:T(8,128)S(1)}, f32[6,64,16,128]{3,2,1,0:T(8,128)}, u32[]{:S(2)}) copy-start(f32[6,64,16,128]{3,2,1,0:T(8,128)} %refs_0_.15) | copy-start | bytes 9437188
  63.5 22.3 %all-to-all-start.1 = ((f32[8,12,16,128]{3,2,1,0:T(8,128)}), f32[8,12,16,128]{3,2,1,0:T(8,128)}, u32[]{:S(2)}, u32[]{:S(2)}) async-start(f32[8,12,16,128]{3,2,1,0:T(8,128)} %pad_maximum_fusion), calls=%async_computation.1 | async-start | bytes 1572864 | tf_op jit(solution)/shard_map/all_to_all | solution.py:499
  69.1 19.4 %collective-permute-start = (f32[6,8,8,128]{3,2,1,0:T(8,128)}, f32[6,8,8,128]{3,2,1,0:T(8,128)}, u32[]{:S(2)}, u32[]{:S(2)}) collective-permute-start(f32[6,8,8,128]{3,2,1,0:T(8,128)} %get-tuple-element.38), channel_id=1, source_target_pairs={{0,1},{1,2},{2,3},{3,4},{4,5},{5,6},{6,7},{7,0},{8,9},{9,10},{10,1... | collective-permute-start | bytes 589832 | tf_op jit(solution)/shard_map/ppermute | solution.py:481
  71.0 17.5 %collective-permute-start.1 = (f32[6,8,8,128]{3,2,1,0:T(8,128)}, f32[6,8,8,128]{3,2,1,0:T(8,128)}, u32[]{:S(2)}, u32[]{:S(2)}) collective-permute-start(f32[6,8,8,128]{3,2,1,0:T(8,128)} %get-tuple-element.39), channel_id=1, source_target_pairs={{0,7},{1,0},{2,1},{3,2},{4,3},{5,4},{6,5},{7,6},{8,15},{9,8},{10,9... | collective-permute-start | bytes 589832 | tf_op jit(solution)/shard_map/ppermute | solution.py:481
  73.9 29.5 %collective-permute-start.5 = (f32[6,8,8,128]{3,2,1,0:T(8,128)}, f32[6,8,8,128]{3,2,1,0:T(8,128)S(1)}, u32[]{:S(2)}, u32[]{:S(2)}) collective-permute-start(f32[6,8,8,128]{3,2,1,0:T(8,128)} %get-tuple-element.44), channel_id=1, source_target_pairs={{0,1},{1,2},{2,3},{3,4},{4,5},{5,6},{6,7},{7,0},{8,9},{9,10},{10,1... | collective-permute-start | bytes 589832 | tf_op jit(solution)/shard_map/ppermute | solution.py:481
  73.9 29.5 %collective-permute-start.6 = (f32[6,8,8,128]{3,2,1,0:T(8,128)}, f32[6,8,8,128]{3,2,1,0:T(8,128)S(1)}, u32[]{:S(2)}, u32[]{:S(2)}) collective-permute-start(f32[6,8,8,128]{3,2,1,0:T(8,128)} %get-tuple-element.45), channel_id=1, source_target_pairs={{0,7},{1,0},{2,1},{3,2},{4,3},{5,4},{6,5},{7,6},{8,15},{9,8},{10,9... | collective-permute-start | bytes 589832 | tf_op jit(solution)/shard_map/ppermute | solution.py:481
  92.9 19.8 %collective-permute-start.7 = (f32[6,8,8,128]{3,2,1,0:T(8,128)S(1)}, f32[6,8,8,128]{3,2,1,0:T(8,128)S(1)}, u32[]{:S(2)}, u32[]{:S(2)}) collective-permute-start(f32[6,8,8,128]{3,2,1,0:T(8,128)S(1)} %get-tuple-element.48), channel_id=1, source_target_pairs={{0,1},{1,2},{2,3},{3,4},{4,5},{5,6},{6,7},{7,0},{8,9},{9,10},{10,1... | collective-permute-start | bytes 589832 | tf_op jit(solution)/shard_map/ppermute | solution.py:481
  103.3 9.3 %collective-permute-start.8 = (f32[6,8,8,128]{3,2,1,0:T(8,128)S(1)}, f32[6,8,8,128]{3,2,1,0:T(8,128)S(1)}, u32[]{:S(2)}, u32[]{:S(2)}) collective-permute-start(f32[6,8,8,128]{3,2,1,0:T(8,128)S(1)} %get-tuple-element.49), channel_id=1, source_target_pairs={{0,7},{1,0},{2,1},{3,2},{4,3},{5,4},{6,5},{7,6},{8,15},{9,8},{10,9... | collective-permute-start | bytes 589832 | tf_op jit(solution)/shard_map/ppermute | solution.py:481
  107.9 13.5 %collective-permute-start.9 = (f32[6,8,8,128]{3,2,1,0:T(8,128)S(1)}, f32[6,8,8,128]{3,2,1,0:T(8,128)S(1)}, u32[]{:S(2)}, u32[]{:S(2)}) collective-permute-start(f32[6,8,8,128]{3,2,1,0:T(8,128)S(1)} %get-tuple-element.52), channel_id=1, source_target_pairs={{0,1},{1,2},{2,3},{3,4},{4,5},{5,6},{6,7},{7,0},{8,9},{9,10},{10,1... | collective-permute-start | bytes 589832 | tf_op jit(solution)/shard_map/ppermute | solution.py:481
  110.0 11.8 %collective-permute-start.10 = (f32[6,8,8,128]{3,2,1,0:T(8,128)S(1)}, f32[6,8,8,128]{3,2,1,0:T(8,128)S(1)}, u32[]{:S(2)}, u32[]{:S(2)}) collective-permute-start(f32[6,8,8,128]{3,2,1,0:T(8,128)S(1)} %get-tuple-element.53), channel_id=1, source_target_pairs={{0,7},{1,0},{2,1},{3,2},{4,3},{5,4},{6,5},{7,6},{8,15},{9,8},{10,9... | collective-permute-start | bytes 589832 | tf_op jit(solution)/shard_map/ppermute | solution.py:481
  116.7 14.5 %collective-permute-start.11 = (f32[6,8,8,128]{3,2,1,0:T(8,128)S(1)}, f32[6,8,8,128]{3,2,1,0:T(8,128)S(1)}, u32[]{:S(2)}, u32[]{:S(2)}) collective-permute-start(f32[6,8,8,128]{3,2,1,0:T(8,128)S(1)} %get-tuple-element.56), channel_id=1, source_target_pairs={{0,1},{1,2},{2,3},{3,4},{4,5},{5,6},{6,7},{7,0},{8,9},{9,10},{10,1... | collective-permute-start | bytes 589832 | tf_op jit(solution)/shard_map/ppermute | solution.py:481
  118.7 12.4 %collective-permute-start.12 = (f32[6,8,8,128]{3,2,1,0:T(8,128)S(1)}, f32[6,8,8,128]{3,2,1,0:T(8,128)S(1)}, u32[]{:S(2)}, u32[]{:S(2)}) collective-permute-start(f32[6,8,8,128]{3,2,1,0:T(8,128)S(1)} %get-tuple-element.57), channel_id=1, source_target_pairs={{0,7},{1,0},{2,1},{3,2},{4,3},{5,4},{6,5},{7,6},{8,15},{9,8},{10,9... | collective-permute-start | bytes 589832 | tf_op jit(solution)/shard_map/ppermute | solution.py:481
  126.4 16.1 %collective-permute-start.13 = (f32[6,8,8,128]{3,2,1,0:T(8,128)S(1)}, f32[6,8,8,128]{3,2,1,0:T(8,128)S(1)}, u32[]{:S(2)}, u32[]{:S(2)}) collective-permute-start(f32[6,8,8,128]{3,2,1,0:T(8,128)S(1)} %get-tuple-element.60), channel_id=1, source_target_pairs={{0,1},{1,2},{2,3},{3,4},{4,5},{5,6},{6,7},{7,0},{8,9},{9,10},{10,1... | collective-permute-start | bytes 589832 | tf_op jit(solution)/shard_map/ppermute | solution.py:481
  127.7 14.7 %collective-permute-start.14 = (f32[6,8,8,128]{3,2,1,0:T(8,128)S(1)}, f32[6,8,8,128]{3,2,1,0:T(8,128)S(1)}, u32[]{:S(2)}, u32[]{:S(2)}) collective-permute-start(f32[6,8,8,128]{3,2,1,0:T(8,128)S(1)} %get-tuple-element.61), channel_id=1, source_target_pairs={{0,7},{1,0},{2,1},{3,2},{4,3},{5,4},{6,5},{7,6},{8,15},{9,8},{10,9... | collective-permute-start | bytes 589832 | tf_op jit(solution)/shard_map/ppermute | solution.py:481
  135.1 16.7 %collective-permute-start.17 = (f32[6,8,8,128]{3,2,1,0:T(8,128)S(1)}, f32[6,8,8,128]{3,2,1,0:T(8,128)S(1)}, u32[]{:S(2)}, u32[]{:S(2)}) collective-permute-start(f32[6,8,8,128]{3,2,1,0:T(8,128)S(1)} %get-tuple-element.66), channel_id=1, source_target_pairs={{0,1},{1,2},{2,3},{3,4},{4,5},{5,6},{6,7},{7,0},{8,9},{9,10},{10,1... | collective-permute-start | bytes 589832 | tf_op jit(solution)/shard_map/ppermute | solution.py:481
  135.2 16.7 %collective-permute-start.18 = (f32[6,8,8,128]{3,2,1,0:T(8,128)S(1)}, f32[6,8,8,128]{3,2,1,0:T(8,128)S(1)}, u32[]{:S(2)}, u32[]{:S(2)}) collective-permute-start(f32[6,8,8,128]{3,2,1,0:T(8,128)S(1)} %get-tuple-element.67), channel_id=1, source_target_pairs={{0,7},{1,0},{2,1},{3,2},{4,3},{5,4},{6,5},{7,6},{8,15},{9,8},{10,9... | collective-permute-start | bytes 589832 | tf_op jit(solution)/shard_map/ppermute | solution.py:481
  147.1 10.2 %collective-permute-start.15 = (f32[6,8,8,128]{3,2,1,0:T(8,128)S(1)}, f32[6,8,8,128]{3,2,1,0:T(8,128)S(1)}, u32[]{:S(2)}, u32[]{:S(2)}) collective-permute-start(f32[6,8,8,128]{3,2,1,0:T(8,128)S(1)} %get-tuple-element.64), channel_id=1, source_target_pairs={{0,1},{1,2},{2,3},{3,4},{4,5},{5,6},{6,7},{7,0},{8,9},{9,10},{10,1... | collective-permute-start | bytes 589832 | tf_op jit(solution)/shard_map/ppermute | solution.py:481
  147.1 11.9 %collective-permute-start.16 = (f32[6,8,8,128]{3,2,1,0:T(8,128)S(1)}, f32[6,8,8,128]{3,2,1,0:T(8,128)S(1)}, u32[]{:S(2)}, u32[]{:S(2)}) collective-permute-start(f32[6,8,8,128]{3,2,1,0:T(8,128)S(1)} %get-tuple-element.65), channel_id=1, source_target_pairs={{0,7},{1,0},{2,1},{3,2},{4,3},{5,4},{6,5},{7,6},{8,15},{9,8},{10,9... | collective-permute-start | bytes 589832 | tf_op jit(solution)/shard_map/ppermute | solution.py:481

commit v3 on v2

--- a/solution.py
+++ b/solution.py
@@ -35,10 +35,9 @@
     def __init__(self, state, sectors):
         self.fields, self.axial, self.cycle, self.radial = state.shape
         self.sectors = sectors
-        strip = self.axial // 4
-        self.outer = ((0, strip), (self.axial - strip, self.axial))
-        self.inner = ((strip, self.axial - strip),)
+        self.middle = self.axial // 8 * 4
         self.ghost = (2, self.fields, 2, self.cycle, self.radial)
+        self.ends = 8
         self.deep = 8
         self.full = self.cycle * sectors
         self.mine = self.radial // sectors
@@ -46,14 +45,29 @@
         self.packed = self.deep * self.cycle
 
 
-def count(ranges):
-    return sum(high - low for low, high in ranges)
-
-
-def write_edges(plan, value, field, place, low_ref, high_ref):
-    tile, row = place
-    low_ref[field, tile, row : row + 2, :] = value[:2]
-    high_ref[field, tile, row : row + 2, :] = value[plan.cycle - 2 :]
+    def ranges(self, kind, stage):
+        reach = 2 * (stage + 1)
+        if kind == "low":
+            return ((reach, self.middle),)
+        if kind == "high":
+            return ((self.middle, self.axial - reach),)
+        return ((0, reach), (self.axial - reach, self.axial))
+
+    def kept(self, kind):
+        return {"low": self.middle, "high": self.axial - self.middle, "ends": 2 * self.ends}[kind]
+
+    def owner(self, plane, stage):
+        reach = 2 * stage
+        if plane < reach:
+            return "ends", plane
+        if plane >= self.axial - reach:
+            return "ends", plane - self.axial + 2 * self.ends
+        return ("low", plane) if plane < self.middle else ("high", plane - self.middle)
+
+    def place(self, kind, plane):
+        if kind == "ends":
+            return plane if plane < self.middle else plane - self.axial + 2 * self.ends
+        return plane if kind == "low" else plane - self.middle
 
 
 def pack_kernel(plan, state, below, out, planes, tall, sem):
@@ -86,7 +100,8 @@
 
 
 def zone_kernel(plan, place, offsets, speed, swirl, next_swirl, diffusion, coupling, weights, got, *refs):
-    to_here, to_next, base, now, later, spread, matrix, made = refs
+    _, to_here, to_next, token, base, now, later, spread, matrix, made = refs
+    token[...] = jnp.zeros(token.shape, jnp.float32)
     fields, deep, cycle, full, wide = plan.fields, plan.deep, plan.cycle, plan.full, plan.wide
     sections = offsets.shape[0]
     row, sector = place[0], place[1]
@@ -207,15 +222,17 @@
         lax.fori_loop(0, fields, hand_out, 0)
 
 
-def zone(plan, place, offsets, scalars, next_swirl, weights, got):
+def zone(plan, place, offsets, scalars, next_swirl, weights, got, after):
     speed, swirl, diffusion, coupling = scalars
     buffer = held((2, plan.fields, plan.deep + 4, LOW + plan.wide + 8, plan.full))
+    rows = -(-(LOW + plan.wide + 8) // 8) * 8
+    need = (3 * 2 * plan.fields * (plan.deep + 4) + 2 * plan.fields * (plan.fields + 9)) * rows * plan.full * 4
     sent = jax.ShapeDtypeStruct((plan.sectors, plan.fields, plan.mine, plan.packed), jnp.float32)
     return pl.pallas_call(
         functools.partial(zone_kernel, plan),
-        in_specs=[whole(SMEM)] * 7 + [whole(VMEM)] * 2,
-        out_specs=[whole(VMEM)] * 2,
-        out_shape=[sent] * 2,
+        in_specs=[whole(SMEM)] * 7 + [whole(VMEM)] * 3,
+        out_specs=[whole(VMEM)] * 3,
+        out_shape=[sent, sent, held((8, plan.radial))],
         scratch_shapes=[
             buffer,
             buffer,
@@ -224,13 +241,14 @@
             held((plan.full, plan.full)),
             held((2, plan.fields, 2 * offsets.shape[0], plan.mine, plan.full)),
         ],
-        compiler_params=pltpu.CompilerParams(vmem_limit_bytes=48 * 1024 * 1024),
+        compiler_params=pltpu.CompilerParams(vmem_limit_bytes=need + 6 * 1024 * 1024),
         name="step_zone",
-    )(place, offsets, speed, swirl, next_swirl, diffusion, coupling, weights, got)
-
-
-def unpack_kernel(plan, got, *refs):
-    *outs, tall = refs
+    )(place, offsets, speed, swirl, next_swirl, diffusion, coupling, weights, got, near(after[0]))
+
+
+def unpack_kernel(plan, got, _, *refs):
+    *outs, token, tall = refs
+    token[...] = jnp.zeros(token.shape, jnp.float32)
     for side in range(2):
         for field in range(plan.fields):
             for sector in range(plan.sectors):
@@ -242,50 +260,48 @@
                     out[side, field, plane] = flat[start : start + plan.cycle]
 
 
-def unpack(plan, got, sections):
+def unpack(plan, got, sections, after):
     return pl.pallas_call(
         functools.partial(unpack_kernel, plan),
-        in_specs=[whole(VMEM)],
-        out_specs=[whole(VMEM)] * sections,
-        out_shape=[held(plan.ghost)] * sections,
+        in_specs=[whole(VMEM)] * 2,
+        out_specs=[whole(VMEM)] * (sections + 1),
+        out_shape=[held(plan.ghost)] * sections + [held((8, plan.radial))],
         scratch_shapes=[held((plan.radial, plan.packed))],
         compiler_params=params(),
         name="unpack_ghosts",
-    )(got)
-
-
-def first_kernel(plan, state, lo_o, hi_o, lo_i, hi_i):
-    for ranges, low_ref, high_ref in ((plan.outer, lo_o, hi_o), (plan.inner, lo_i, hi_i)):
-        start = 0
-        for low, high in ranges:
-
-            def body(tile, carry, low=low, start=start, low_ref=low_ref, high_ref=high_ref):
-                for field in range(plan.fields):
-                    for step in range(4):
-                        at = low + tile * 4 + step
-                        low_ref[field, start + tile, 2 * step : 2 * step + 2, :] = state[field, at, 0:2, :]
-                        high_ref[field, start + tile, 2 * step : 2 * step + 2, :] = state[
-                            field, at, plan.cycle - 2 : plan.cycle, :
-                        ]
-                return carry
-
-            lax.fori_loop(0, (high - low) // 4, body, 0)
-            start += (high - low) // 4
-
-
-def edge_shape(plan, ranges):
-    return held((plan.fields, count(ranges) // 4, 8, plan.radial))
-
-
-def first(plan, state):
-    return pl.pallas_call(
+    )(got, near(after[0]))
+
+
+def edge_shape(plan, kind):
+    return held((plan.fields, plan.kept(kind) // 4, 8, plan.radial))
+
+
+def first_kernel(plan, state, *refs):
+    for at, (first, low_ref, high_ref) in enumerate(((0, *refs[:2]), (plan.middle, *refs[2:]))):
+
+        def body(tile, carry, first=first, low_ref=low_ref, high_ref=high_ref):
+            for field in range(plan.fields):
+                for step in range(4):
+                    plane = first + tile * 4 + step
+                    rows = slice(2 * step, 2 * step + 2)
+                    low_ref[field, tile, rows, :] = state[field, plane, 0:2, :]
+                    high_ref[field, tile, rows, :] = state[field, plane, plan.cycle - 2 : plan.cycle, :]
+            return carry
+
+        lax.fori_loop(0, low_ref.shape[1], body, 0)
+
+
+def first_edges(plan, state):
+    low, high = edge_shape(plan, "low"), edge_shape(plan, "high")
+    results = pl.pallas_call(
         functools.partial(first_kernel, plan),
         in_specs=[whole(VMEM)],
         out_specs=[whole(VMEM)] * 4,
-        out_shape=[edge_shape(plan, ranges) for ranges in (plan.outer, plan.outer, plan.inner, plan.inner)],
+        out_shape=[low, low, high, high],
         compiler_params=params(),
         name="first_edges",
-    )(state)
+    )(near(state))
+    return results[:2], results[2:]
 
 
 def coefficients(plan, speed, swirl, diffusion, coupling):
@@ -301,29 +317,11 @@
     return table
 
 
-def stage_kernel(plan, stage, outer, speed, swirl, diffusion, coupling, *refs):
-    refs = list(refs)
-    take = lambda number: [refs.pop(0) for _ in range(number)]
-    ranges = plan.outer if outer else plan.inner
-    (state,) = take(1)
-    chunks = {"state": state} if stage == 0 else dict(zip(("outer", "inner"), take(2)))
-    low_in, high_in = take(2)
-    if outer:
-        (ghosts,) = take(1)
-    else:
-        take(1)
-    if stage == 3:
-        older = take(2)
-        if not outer:
-            take(1)
-        (out_any,) = take(1)
-        if outer:
-            (token,) = take(1)
-        out_buf, sem = take(2)
-    else:
-        out, low_out, high_out, token = take(4)
-    work, spread = take(2)
-    cycle, radial = plan.cycle, plan.radial
+def stage_kernel(plan, stage, kind, names, speed, swirl, diffusion, coupling, *refs):
+    ref = dict(zip(names, refs))
+    ranges = plan.ranges(kind, stage)
+    cycle, radial, last = plan.cycle, plan.radial, stage == 3
+    state, work, spread = ref["state"], ref["work"], ref["spread"]
     terms = plan.fields + 9
     for f, (axial, around, d, mix) in enumerate(coefficients(plan, speed, swirl, diffusion, coupling)):
         for number, factor in enumerate((d, *mix, *axial, *around)):
@@ -332,145 +330,149 @@
     not_first = lane > 0
     not_last = lane < radial - 1
 
-    def source(at):
-        if at < 0:
-            return ghosts, 0, at + 2
-        if at >= plan.axial:
-            return ghosts, 1, at - plan.axial
-        if stage == 0:
-            return state, None, at
-        start = 0
-        for low, high in plan.outer:
-            if low <= at < high:
-                return chunks["outer"], None, start + at - low
-            start += high - low
-        return chunks["inner"], None, at - plan.inner[0][0]
-
-    def fill(field, at, to):
-        ref, side, place = source(at)
-        if side is not None:
-            work[field, to, LOW : LOW + cycle, :] = ref[side, field, place]
-        else:
-            work[field, to, LOW : LOW + cycle, :] = ref[field, place]
-
-    begin = 0
-    for low, high in ranges:
+    def cells(plane, level):
+        if plane < 0:
+            return ref["ghosts"][0, :, plane + 2]
+        if plane >= plan.axial:
+            return ref["ghosts"][1, :, plane - plan.axial]
+        if level == 0:
+            return state[:, plane]
+        owner, at = plan.owner(plane, level)
+        return ref["cells", level, owner][:, at]
+
+    copies = []
+    for number, (low, high) in enumerate(ranges):
         size = high - low
-        for field in range(plan.fields):
-            for at, to in ((low - 2, 0), (low - 1, 1), (high, size + 2), (high + 1, size + 3)):
-                fill(field, at, to)
-        ref, _, first_place = source(low)
-
-        def copy(tile, carry, ref=ref, first_place=first_place, begin=begin):
-            for field in range(plan.fields):
-                for step in range(4):
-                    place = tile * 4 + step
-                    work[field, place + 2, LOW : LOW + cycle, :] = ref[field, first_place + place]
-                    work[field, place + 2, LOW - 2 : LOW, :] = low_in[field, begin // 4 + tile, 2 * step : 2 * step + 2, :]
-                    work[field, place + 2, LOW + cycle : LOW + cycle + 2, :] = high_in[
-                        field, begin // 4 + tile, 2 * step : 2 * step + 2, :
-                    ]
-            return carry
-
-        lax.fori_loop(0, size // 4, copy, 0)
-
-        def compute(tile, carry, low=low, begin=begin):
+        for plane in range(low - 2, high + 2):
+            work[:, plane - low + 2, LOW : LOW + cycle, :] = cells(plane, stage)
+        for plane in range(low, high):
+            owner, at = plan.owner(plane, stage)
+            rows = slice(2 * (at % 4), 2 * (at % 4) + 2)
+            work[:, plane - low + 2, LOW - 2 : LOW, :] = ref["low halo", owner][:, at // 4, rows, :]
+            work[:, plane - low + 2, LOW + cycle : LOW + cycle + 2, :] = ref["high halo", owner][:, at // 4, rows, :]
+            if last:
+                ref["earlier"][:, plane - low] = cells(plane, 1) + 2.0 * cells(plane, 2)
+        start = plan.place(kind, low)
+
+        def compute(tile, steps, low=low, start=start, number=number):
             for f in range(plan.fields):
                 factors = [spread[f * terms + number] for number in range(terms)]
                 values = {}
-                for step in range(4):
-                    at = tile * 4 + step + 2
+                for step in steps:
+                    at = tile * 4 + step - start % 4
                     for row in range(0, cycle, 8):
                         here = slice(LOW + row, LOW + row + 8)
-                        center = work[f, at, here, :]
+                        center = work[f, at + 2, here, :]
                         left = jnp.where(not_first, pltpu.roll(center, 1, 1), 0.0)
                         right = jnp.where(not_last, pltpu.roll(center, radial - 1, 1), 0.0)
                         total = factors[0] * (left + right)
                         for e in range(plan.fields):
-                            total += factors[1 + e] * (center if e == f else work[e, at, here, :])
-                        for number, by in enumerate((-2, -1, 1, 2)):
-                            total += factors[1 + plan.fields + number] * work[f, at + by, here, :]
-                            total += factors[5 + plan.fields + number] * work[f, at, LOW + row + by : LOW + row + by + 8, :]
-                        place = begin + tile * 4 + step
-                        base = state[f, low + tile * 4 + step, row : row + 8, :]
-                        if stage == 3:
-                            second, third = older
-                            kept = second[f, place, row : row + 8, :] + 2.0 * third[f, place, row : row + 8, :]
-                            value = (kept + center - base) * (1.0 / 3.0) + (time_step / 6.0) * total
+                            total += factors[1 + e] * (center if e == f else work[e, at + 2, here, :])
+                        for place, by in enumerate((-2, -1, 1, 2)):
+                            total += factors[1 + plan.fields + place] * work[f, at + 2 + by, here, :]
+                            beside = slice(LOW + row + by, LOW + row + by + 8)
+                            total += factors[5 + plan.fields + place] * work[f, at + 2, beside, :]
+                        base = state[f, low + at, row : row + 8, :]
+                        if last:
+                            value = (ref["earlier"][f, at, row : row + 8, :] + center - base) * (1.0 / 3.0)
+                            value += (time_step / 6.0) * total
                         else:
                             value = base + (time_step if stage == 2 else 0.5 * time_step) * total
                         values[step, row] = value
                 for (step, row), value in values.items():
-                    place = begin + tile * 4 + step
-                    if stage == 3:
-                        out_buf[f, place, row : row + 8, :] = value
+                    at = tile * 4 + step - start % 4
+                    if last:
+                        ref["made"][number, f, at, row : row + 8, :] = value
                         continue
-                    out[f, place, row : row + 8, :] = value
+                    ref["out"][f, start + at, row : row + 8, :] = value
+                    rows = slice(2 * step, 2 * step + 2)
                     if row == 0:
-                        low_out[f, begin // 4 + tile, 2 * step : 2 * step + 2, :] = value[:2]
+                        ref["low edge"][f, start // 4 + tile, rows, :] = value[:2]
                     if row == cycle - 8:
-                        high_out[f, begin // 4 + tile, 2 * step : 2 * step + 2, :] = value[6:]
+                        ref["high edge"][f, start // 4 + tile, rows, :] = value[6:]
+
+        head = start % 4
+        tiles = (head + size) // 4
+        if head:
+            compute(0, range(head, min(4, head + size)))
+        first = 1 if head else 0
+
+        def whole_tile(tile, carry, compute=compute):
+            compute(tile, range(4))
             return carry
 
-        lax.fori_loop(0, size // 4, compute, 0)
-        begin += size
-
-    if stage == 3:
-        begin = 0
-        copies = []
-        for number, (low, high) in enumerate(ranges):
+        if tiles > first:
+            lax.fori_loop(first, tiles, whole_tile, 0)
+        tail = (head + size) % 4
+        if tail and tiles >= first:
+            compute(tiles, range(tail))
+        if last:
             copies.append(
                 pltpu.make_async_copy(
-                    out_buf.at[:, begin : begin + high - low], out_any.at[:, low:high], sem.at[number]
+                    ref["made"].at[number, :, 0:size], ref["result"].at[:, low:high], ref["sem"].at[number]
                 )
             )
             copies[-1].start()
-            begin += high - low
-        for item in copies:
-            item.wait()
-    if stage < 3 or outer:
-        token[...] = jnp.zeros(token.shape, jnp.float32)
-
-
-def stage_call(plan, stage, outer, scalars, state, chunks, halos, extra, older=(), whole_out=None):
-    ranges = plan.outer if outer else plan.inner
-    chunk = (plan.fields, count(ranges), plan.cycle, plan.radial)
+    for item in copies:
+        item.wait()
+    ref["token"][...] = jnp.zeros(ref["token"].shape, jnp.float32)
+
+
+def stage_call(plan, stage, kind, scalars, state, levels, halos, ghosts, after, result=None):
+    ranges = plan.ranges(kind, stage)
+    last = stage == 3
     longest = max(high - low for low, high in ranges)
-    operands, specs = list(scalars), [whole(SMEM)] * len(scalars)
-
-    def add(values):
-        operands.extend(map(near, values))
-        specs.extend([whole(VMEM)] * len(values))
-
-    add([state, *(chunks or ()), *halos, extra])
-    scratch = [
-        held((plan.fields, longest + 4, plan.cycle + 16, plan.radial)),
-        held((plan.fields * (plan.fields + 9), 8, plan.radial)),
-    ]
+    operands = {"state": near(state)}
+    specs = [whole(VMEM)]
+
+    def add(name, value):
+        operands[name] = near(value)
+        specs.append(whole(VMEM))
+
+    kinds = {plan.owner(plane, stage)[0] for low, high in ranges for plane in range(low, high)}
+    for owner in sorted(kinds):
+        add(("low halo", owner), halos[owner][0])
+        add(("high halo", owner), halos[owner][1])
+    for level in (1, 2, stage) if last else (stage,) if stage else ():
+        edge = 2 if level == stage else 0
+        planes = [plane for low, high in ranges for plane in range(max(0, low - edge), min(plan.axial, high + edge))]
+        for owner in sorted({plan.owner(plane, level)[0] for plane in planes}):
+            add(("cells", level, owner), levels[level][owner])
+    if kind == "ends":
+        add("ghosts", ghosts)
+    for number, token in enumerate(after):
+        add(("after", number), token)
     aliases = {}
+    if result is not None:
+        aliases = {len(scalars) + len(operands): 0}
+        operands["earlier result"] = result
+        specs.append(whole(pl.ANY))
     token = held((8, plan.radial))
-    if stage == 3:
-        add(older)
-        if whole_out is not None:
-            aliases = {len(operands): 0}
-            operands.append(whole_out)
-            specs.append(whole(pl.ANY))
-        out_shape = [jax.ShapeDtypeStruct(state.shape, jnp.float32)] + [token] * outer
-        out_specs = [whole(pl.ANY)] + [whole(VMEM)] * outer
-        scratch = [held(chunk), pltpu.SemaphoreType.DMA((len(ranges),))] + scratch
+    if last:
+        outs = {"result": jax.ShapeDtypeStruct(state.shape, jnp.float32), "token": token}
     else:
-        out_shape = [held(chunk), edge_shape(plan, ranges), edge_shape(plan, ranges), token]
-        out_specs = [whole(VMEM)] * len(out_shape)
+        edges = edge_shape(plan, kind)
+        cells = held((plan.fields, plan.kept(kind), plan.cycle, plan.radial))
+        outs = {"out": cells, "low edge": edges, "high edge": edges, "token": token}
+    scratch = {
+        "work": held((plan.fields, longest + 4, plan.cycle + 16, plan.radial)),
+        "spread": held((plan.fields * (plan.fields + 9), 8, plan.radial)),
+    }
+    if last:
+        scratch["earlier"] = held((plan.fields, longest, plan.cycle, plan.radial))
+        scratch["made"] = held((len(ranges), plan.fields, longest, plan.cycle, plan.radial))
+        scratch["sem"] = pltpu.SemaphoreType.DMA((len(ranges),))
+    names = (*operands, *outs, *scratch)
     return pl.pallas_call(
-        functools.partial(stage_kernel, plan, stage, outer),
-        in_specs=specs,
-        out_specs=out_specs,
-        out_shape=out_shape,
-        scratch_shapes=scratch,
+        functools.partial(stage_kernel, plan, stage, kind, names),
+        in_specs=[whole(SMEM)] * len(scalars) + specs,
+        out_specs=[whole(pl.ANY if name == "result" else VMEM) for name in outs],
+        out_shape=list(outs.values()),
+        scratch_shapes=list(scratch.values()),
         input_output_aliases=aliases,
         compiler_params=params(),
-        name=f"stage{stage}_{'outer' if outer else 'inner'}",
-    )(*operands)
+        name=f"stage{stage}_{kind}",
+    )(*scalars, *operands.values())
 
 
 def exchange(edges):
@@ -492,30 +494,47 @@
 
     below = lax.ppermute(state[:, : plan.deep], "row", back)
     next_swirl = lax.ppermute(row_swirl, "row", back)
-    got = lax.all_to_all(pack(plan, state, below), "sector", 0, 0, tiled=True)
     weights = jnp.pad(interp_blocks, ((0, 0), (0, 0), (0, plan.full - interp_blocks.shape[2])))
-    downstream, to_next = zone(plan, place, rotor_offset, scalars, next_swirl, weights, got)
+    packed = pack(plan, state, below)
+    got = lax.all_to_all(packed, "sector", 0, 0, tiled=True)
+
+    levels, halos = [None], [{}]
+    edges = dict(zip(("low", "high"), first_edges(plan, state)))
+    halos[0] = {kind: exchange(edges[kind]) for kind in ("low", "high")}
+    token, result, ghosts = (), None, None
+
+    def step(stage, kind):
+        nonlocal token, result
+        ghost = ghosts[stage] if kind == "ends" else None
+        outs = stage_call(plan, stage, kind, scalars, state, levels, halos[stage], ghost, token, result)
+        token = outs[-1:]
+        if stage == sections - 1:
+            result = outs[0]
+            return
+        if len(levels) == stage + 1:
+            levels.append({})
+            halos.append({})
+        levels[stage + 1][kind] = outs[0]
+        halos[stage + 1][kind] = exchange(outs[1:3])
+
+    step(0, "low")
+    step(0, "high")
+    downstream, to_next, *token = zone(plan, place, rotor_offset, scalars, next_swirl, weights, got, token)
     upstream = lax.ppermute(to_next, "row", ahead)
     returned = lax.all_to_all(jnp.concatenate([upstream, downstream], axis=1), "sector", 0, 0, tiled=True)
-    ghosts = unpack(plan, returned, sections)
-
-    lo_o, hi_o, lo_i, hi_i = first(plan, state)
-    outer_edges, inner_edges = (lo_o, hi_o), (lo_i, hi_i)
-    chunks, history = None, []
-    for stage in range(4):
-        outer_halos, inner_halos = exchange(outer_edges), exchange(inner_edges)
-        last = stage == 3
-        older = [(history[0][i], history[1][i]) if last else () for i in range(2)]
-        out_o, *rest = stage_call(plan, stage, True, scalars, state, chunks, outer_halos, ghosts[stage], older[0])
-        token = rest[0] if last else rest[2]
-        out_i, *rest_i = stage_call(
-            plan, stage, False, scalars, state, chunks, inner_halos, token, older[1], out_o if last else None
-        )
-        if last:
-            return out_i
-        outer_edges, inner_edges = rest[:2], rest_i[:2]
-        chunks = (out_o, out_i)
-        history.append(chunks)
+    step(1, "low")
+    step(1, "high")
+    *ghosts, last_token = unpack(plan, returned, sections, token)
+    token = (last_token,)
+    step(0, "ends")
+    step(2, "low")
+    step(1, "ends")
+    step(2, "high")
+    step(2, "ends")
+    step(3, "low")
+    step(3, "high")
+    step(3, "ends")
+    return result
 
 
 def solution(mesh):

time: 166 us -> 189 us (1.14)
  local copies, waits for them, and re-layouts: 2.96 us -> 19.4 us
  starting transfers between devices: 64.8 us -> 72.1 us
  waiting for transfers between devices: 40.3 us -> 35.1 us
  Pallas kernels: 54.2 us -> 58.9 us
    ppermute x8 -> x11, waiting for transfers between devices: 1.62 us -> 22.4 us  [exchange(): lax.ppermute(high_edges, 'sector', ahead)]
    all_to_all x1, waiting for transfers between devices: 20.1 us -> 0.01 us  [on_device(): got = lax.all_to_all(packed, 'sector', 0, 0, tiled=True)]
    unnamed x14 -> x70, local copies, waits for them, and re-layouts: 1.92 us -> 16.8 us
    all_to_all x1, waiting for transfers between devices: 7.17 us -> 0.01 us  [on_device(): lax.all_to_all(jnp.concatenate([upstream, downstream], axis=1), 'sector',...]
    ppermute x8 -> x11, waiting for transfers between devices: 2.04 us -> 9.03 us  [exchange(): lax.ppermute(low_edges, 'sector', back)]
    ppermute x8 -> x11, starting transfers between devices: 28.4 us -> 35.3 us  [exchange(): lax.ppermute(low_edges, 'sector', back)]
    ppermute x8 -> x11, starting transfers between devices: 17.8 us -> 11.5 us  [exchange(): lax.ppermute(high_edges, 'sector', ahead)]
    ppermute x1, waiting for transfers between devices: 5.8 us -> 0.01 us  [on_device(): next_swirl = lax.ppermute(row_swirl, 'row', back)]
  transfers between devices with their start and end apart: 21 -> 27, of which waited for: 9 -> 6; matrix products, arithmetic and copies ran while one was open for 0% -> 1% of each run, Pallas kernels for 21% -> 21%
where the time goes in v3:
time: 189 us; the launch traced here: 188 us
  starting transfers between devices  72.1 us (38%)
  Pallas kernels  58.9 us (31%)
  waiting for transfers between devices  35.1 us (19%)
  local copies, waits for them, and re-layouts  19.4 us (10%)
    pallas_call x12, Pallas kernels, stage_call(): pl.pallas_call(functools.partial(stage_kernel, plan, stage, kind, names),...  41.7 us
    ppermute x11, starting transfers between devices, exchange(): lax.ppermute(low_edges, 'sector', back)  35.3 us
    ppermute x11, waiting for transfers between devices, exchange(): lax.ppermute(high_edges, 'sector', ahead)  22.4 us
    unnamed x70, local copies, waits for them, and re-layouts  16.8 us
    pallas_call x1, Pallas kernels, zone(): pl.pallas_call(functools.partial(zone_kernel, plan), in_specs=[whole(SMEM...  14.1 us
    ppermute x11, starting transfers between devices, exchange(): lax.ppermute(high_edges, 'sector', ahead)  11.5 us
    ppermute x11, waiting for transfers between devices, exchange(): lax.ppermute(low_edges, 'sector', back)  9.03 us
    ppermute x1, starting transfers between devices, on_device(): upstream = lax.ppermute(to_next, 'row', ahead)  7.87 us
  transfers between devices with their start and end apart: 27, of which 6 were waited for; matrix products, arithmetic and copies ran while one was open for 1% of the time, Pallas kernels for 21%

profile of v3, /device:TPU:0, one launch (start us, length us, event | category | flops | bytes accessed | tf_op | source)
XLA Modules:
  0.0 188.2 jit_solution(2946659802336479184)
XLA Ops:
  0.0 1.0 slice.3
  1.0 1.3 collective-permute-start.5
  2.3 2.3 %collective-permute-done.5.below = f32[6,8,16,128]{3,2,1,0:T(8,128)S(1)} collective-permute-done((f32[6,8,16,128]{3,2,1,0:T(8,128)S(1)}, f32[6,8,16,128]{3,2,1,0:T(8,128)S(1)}, u32[]{:S(2)}, u32[]{:S(2)}) %collective-permute-start.5) | collective-permute-done | bytes 393248 | tf_op jit(solution)/shard_map/ppermute | solution.py:495
  4.6 1.9 %copy-done = f32[6,64,16,128]{3,2,1,0:T(8,128)S(1)} copy-done((f32[6,64,16,128]{3,2,1,0:T(8,128)S(1)}, f32[6,64,16,128]{3,2,1,0:T(8,128)}, u32[]{:S(2)}) %copy-start) | copy-done | bytes 3145752
  8.0 7.3 %all-to-all-start = ((f32[8,12,24,128]{3,2,1,0:T(8,128)}), f32[8,12,24,128]{3,2,1,0:T(8,128)}, u32[]{:S(2)}, u32[]{:S(2)}) async-start(f32[8,12,24,128]{3,2,1,0:T(8,128)} %copy-done.12), calls=%async_computation | async-start | bytes 2359296 | tf_op jit(solution)/shard_map/all_to_all | solution.py:499
  15.3 1.2 first_edges.1
  16.6 2.0 %collective-permute-start.2 = (f32[6,8,8,128]{3,2,1,0:T(8,128)}, f32[6,8,8,128]{3,2,1,0:T(8,128)S(1)}, u32[]{:S(2)}, u32[]{:S(2)}) collective-permute-start(f32[6,8,8,128]{3,2,1,0:T(8,128)} %get-tuple-element.60), channel_id=1, source_target_pairs={{0,1},{1,2},{2,3},{3,4},{4,5},{5,6},{6,7},{7,0},{8,9},{9,10},{10,1... | collective-permute-start | bytes 589832 | tf_op jit(solution)/shard_map/ppermute | solution.py:483
  18.6 2.7 %collective-permute-start.3 = (f32[6,8,8,128]{3,2,1,0:T(8,128)}, f32[6,8,8,128]{3,2,1,0:T(8,128)S(1)}, u32[]{:S(2)}, u32[]{:S(2)}) collective-permute-start(f32[6,8,8,128]{3,2,1,0:T(8,128)} %get-tuple-element.61), channel_id=1, source_target_pairs={{0,7},{1,0},{2,1},{3,2},{4,3},{5,4},{6,5},{7,6},{8,15},{9,8},{10,9... | collective-permute-start | bytes 589832 | tf_op jit(solution)/shard_map/ppermute | solution.py:483
  21.3 4.7 %collective-permute-start.1 = (f32[6,8,8,128]{3,2,1,0:T(8,128)}, f32[6,8,8,128]{3,2,1,0:T(8,128)}, u32[]{:S(2)}, u32[]{:S(2)}) collective-permute-start(f32[6,8,8,128]{3,2,1,0:T(8,128)} %get-tuple-element.59), channel_id=1, source_target_pairs={{0,7},{1,0},{2,1},{3,2},{4,3},{5,4},{6,5},{7,6},{8,15},{9,8},{10,9... | collective-permute-start | bytes 589832 | tf_op jit(solution)/shard_map/ppermute | solution.py:483
  26.0 1.3 collective-permute-start.4
  27.9 1.6 pad.4.weights
  30.1 10.9 %collective-permute-done.2.refs_1_.refs_3_ = f32[6,8,8,128]{3,2,1,0:T(8,128)S(1)} collective-permute-done((f32[6,8,8,128]{3,2,1,0:T(8,128)}, f32[6,8,8,128]{3,2,1,0:T(8,128)S(1)}, u32[]{:S(2)}, u32[]{:S(2)}) %collective-permute-start.2) | collective-permute-done | bytes 196640 | tf_op jit(solution)/shard_map/ppermute | solution.py:483
  41.0 3.7 %stage0_low.1 = (f32[6,32,16,128]{3,2,1,0:T(8,128)S(1)}, f32[6,8,8,128]{3,2,1,0:T(8,128)S(1)}, f32[6,8,8,128]{3,2,1,0:T(8,128)S(1)}, f32[8,128]{1,0:T(8,128)S(1)}) custom-call(f32[6]{0:T(128)S(1)} %copy-done.23, f32[1]{0:T(128)S(6)} %copy.12.swirl, f32[6]{0:T(128)S(1)} %copy-done.24, f32[6,6]{1,0:T(8,128)S(1)} %copy-done.21, ...), custom_call_target="tpu_custom_call" | custom-call | tf_op jit(solution)/shard_map/stage0_low/pallas_call | solution.py:466
  44.8 1.1 copy-done.2
  47.3 4.2 %stage0_high.1 = (f32[6,32,16,128]{3,2,1,0:T(8,128)S(1)}, f32[6,8,8,128]{3,2,1,0:T(8,128)S(1)}, f32[6,8,8,128]{3,2,1,0:T(8,128)S(1)}, f32[8,128]{1,0:T(8,128)S(1)}) custom-call(f32[6]{0:T(128)S(1)} %copy-done.23, f32[1]{0:T(128)S(6)} %copy.12.swirl, f32[6]{0:T(128)S(1)} %copy-done.24, f32[6,6]{1,0:T(8,128)S(1)} %copy-done.21, ...), custom_call_target="tpu_custom_call" | custom-call | tf_op jit(solution)/shard_map/stage0_high/pallas_call | solution.py:466
  51.5 1.1 copy-done.5
  56.2 14.1 %step_zone.1 = (f32[8,6,16,128]{3,2,1,0:T(8,128)S(1)}, f32[8,6,16,128]{3,2,1,0:T(8,128)S(1)}, f32[8,128]{1,0:T(8,128)S(1)}) custom-call(s32[2]{0:T(128)S(1)} %copy-done.28, s32[4,3]{1,0:T(4,128)S(1)} %copy-done.27, f32[6]{0:T(128)S(1)} %copy-done.23, f32[1]{0:T(128)S(6)} %copy.12.swirl, f32[1]{0:T(128)} %collective-permute-done.4.next_swirl, ...), custom_call_target="tpu_custom_call" | custom-call | tf_op jit(solution)/shard_map/step_zone/pallas_call | solution.py:231
  70.9 7.9 %collective-permute-start.6 = (f32[8,6,16,128]{3,2,1,0:T(8,128)S(1)}, f32[8,6,16,128]{3,2,1,0:T(8,128)S(1)}, u32[]{:S(2)}, u32[]{:S(2)}) collective-permute-start(f32[8,6,16,128]{3,2,1,0:T(8,128)S(1)} %get-tuple-element.64), channel_id=1, source_target_pairs={{0,8},{8,16},{16,24},{1,9},{9,17},{17,25},{2,10},{10,18},{18,26},{... | collective-permute-start | bytes 1179656 | tf_op jit(solution)/shard_map/ppermute | solution.py:523
  78.8 1.3 collective-permute-done.6
  81.0 7.7 %all-to-all-start.1 = ((f32[8,12,16,128]{3,2,1,0:T(8,128)}), f32[8,12,16,128]{3,2,1,0:T(8,128)}, u32[]{:S(2)}, u32[]{:S(2)}) async-start(f32[8,12,16,128]{3,2,1,0:T(8,128)} %pad_maximum_fusion), calls=%async_computation.1 | async-start | bytes 1572864 | tf_op jit(solution)/shard_map/all_to_all | solution.py:524
  88.7 2.0 %collective-permute-start.9 = (f32[6,8,8,128]{3,2,1,0:T(8,128)}, f32[6,8,8,128]{3,2,1,0:T(8,128)S(1)}, u32[]{:S(2)}, u32[]{:S(2)}) collective-permute-start(f32[6,8,8,128]{3,2,1,0:T(8,128)} %copy-done.34), channel_id=1, source_target_pairs={{0,1},{1,2},{2,3},{3,4},{4,5},{5,6},{6,7},{7,0},{8,9},{9,10},{10,1... | collective-permute-start | bytes 589832 | tf_op jit(solution)/shard_map/ppermute | solution.py:483
  90.7 2.7 %collective-permute-start.10 = (f32[6,8,8,128]{3,2,1,0:T(8,128)}, f32[6,8,8,128]{3,2,1,0:T(8,128)S(1)}, u32[]{:S(2)}, u32[]{:S(2)}) collective-permute-start(f32[6,8,8,128]{3,2,1,0:T(8,128)} %copy-done.33), channel_id=1, source_target_pairs={{0,7},{1,0},{2,1},{3,2},{4,3},{5,4},{6,5},{7,6},{8,15},{9,8},{10,9... | collective-permute-start | bytes 589832 | tf_op jit(solution)/shard_map/ppermute | solution.py:483
  93.4 4.7 %collective-permute-start.8 = (f32[6,8,8,128]{3,2,1,0:T(8,128)}, f32[6,8,8,128]{3,2,1,0:T(8,128)S(1)}, u32[]{:S(2)}, u32[]{:S(2)}) collective-permute-start(f32[6,8,8,128]{3,2,1,0:T(8,128)} %copy-done.31), channel_id=1, source_target_pairs={{0,7},{1,0},{2,1},{3,2},{4,3},{5,4},{6,5},{7,6},{8,15},{9,8},{10,9... | collective-permute-start | bytes 589832 | tf_op jit(solution)/shard_map/ppermute | solution.py:483
  98.2 11.4 %collective-permute-done.9.refs_1_.refs_5_ = f32[6,8,8,128]{3,2,1,0:T(8,128)S(1)} collective-permute-done((f32[6,8,8,128]{3,2,1,0:T(8,128)}, f32[6,8,8,128]{3,2,1,0:T(8,128)S(1)}, u32[]{:S(2)}, u32[]{:S(2)}) %collective-permute-start.9) | collective-permute-done | bytes 196640 | tf_op jit(solution)/shard_map/ppermute | solution.py:483
  109.6 1.5 copy-done.3
  111.2 1.4 copy-done.6
  112.6 4.3 %stage1_low.1 = (f32[6,32,16,128]{3,2,1,0:T(8,128)S(1)}, f32[6,8,8,128]{3,2,1,0:T(8,128)}, f32[6,8,8,128]{3,2,1,0:T(8,128)}, f32[8,128]{1,0:T(8,128)S(1)}) custom-call(f32[6]{0:T(128)S(1)} %copy-done.23, f32[1]{0:T(128)S(6)} %copy.12.swirl, f32[6]{0:T(128)S(1)} %copy-done.24, f32[6,6]{1,0:T(8,128)S(1)} %copy-done.21, f32[6,64,16,128]{3,2,1,0:T(8,128)S(1)} %copy-done.1, ...), custom_call_target="tpu_custom_call" | custom-call | tf_op jit(solution)/shard_map/stage1_low/pallas_call | solution.py:466
  116.9 1.2 copy-done.8
  118.0 4.7 %collective-permute-start.14 = (f32[6,8,8,128]{3,2,1,0:T(8,128)}, f32[6,8,8,128]{3,2,1,0:T(8,128)}, u32[]{:S(2)}, u32[]{:S(2)}) collective-permute-start(f32[6,8,8,128]{3,2,1,0:T(8,128)} %get-tuple-element.82), channel_id=1, source_target_pairs={{0,7},{1,0},{2,1},{3,2},{4,3},{5,4},{6,5},{7,6},{8,15},{9,8},{10,9... | collective-permute-start | bytes 589832 | tf_op jit(solution)/shard_map/ppermute | solution.py:483
  122.8 4.2 %stage1_high.1 = (f32[6,32,16,128]{3,2,1,0:T(8,128)S(1)}, f32[6,8,8,128]{3,2,1,0:T(8,128)S(1)}, f32[6,8,8,128]{3,2,1,0:T(8,128)}, f32[8,128]{1,0:T(8,128)S(1)}) custom-call(f32[6]{0:T(128)S(1)} %copy-done.23, f32[1]{0:T(128)S(6)} %copy.12.swirl, f32[6]{0:T(128)S(1)} %copy-done.24, f32[6,6]{1,0:T(8,128)S(1)} %copy-done.21, f32[6,64,16,128]{3,2,1,0:T(8,128)S(1)} %copy-done.1, ...), custom_call_target="tpu_custom_call" | custom-call | tf_op jit(solution)/shard_map/stage1_high/pallas_call | solution.py:466
  127.0 1.2 copy-done.10
  128.9 1.4 unpack_ghosts.1
  130.3 1.5 stage0_ends.1
  131.9 1.6 collective-permute-start.11
  133.4 3.3 %collective-permute-start.12 = (f32[6,4,8,128]{3,2,1,0:T(8,128)S(1)}, f32[6,4,8,128]{3,2,1,0:T(8,128)S(1)}, u32[]{:S(2)}, u32[]{:S(2)}) collective-permute-start(f32[6,4,8,128]{3,2,1,0:T(8,128)S(1)} %get-tuple-element.78), channel_id=1, source_target_pairs={{0,7},{1,0},{2,1},{3,2},{4,3},{5,4},{6,5},{7,6},{8,15},{9,8},{10,9... | collective-permute-start | bytes 294920 | tf_op jit(solution)/shard_map/ppermute | solution.py:483
  136.7 2.0 %collective-permute-start.18 = (f32[6,8,8,128]{3,2,1,0:T(8,128)S(1)}, f32[6,8,8,128]{3,2,1,0:T(8,128)S(1)}, u32[]{:S(2)}, u32[]{:S(2)}) collective-permute-start(f32[6,8,8,128]{3,2,1,0:T(8,128)S(1)} %copy-done.30), channel_id=1, source_target_pairs={{0,7},{1,0},{2,1},{3,2},{4,3},{5,4},{6,5},{7,6},{8,15},{9,8},{10,9... | collective-permute-start | bytes 589832 | tf_op jit(solution)/shard_map/ppermute | solution.py:483
  138.7 3.9 %stage2_low.1 = (f32[6,32,16,128]{3,2,1,0:T(8,128)S(1)}, f32[6,8,8,128]{3,2,1,0:T(8,128)S(1)}, f32[6,8,8,128]{3,2,1,0:T(8,128)S(1)}, f32[8,128]{1,0:T(8,128)S(1)}) custom-call(f32[6]{0:T(128)S(1)} %copy-done.23, f32[1]{0:T(128)S(6)} %copy.12.swirl, f32[6]{0:T(128)S(1)} %copy-done.24, f32[6,6]{1,0:T(8,128)S(1)} %copy-done.21, ...), custom_call_target="tpu_custom_call" | custom-call | tf_op jit(solution)/shard_map/stage2_low/pallas_call | solution.py:466
  143.7 1.3 stage1_ends.1
  145.0 5.0 %collective-permute-start.23 = (f32[6,8,8,128]{3,2,1,0:T(8,128)S(1)}, f32[6,8,8,128]{3,2,1,0:T(8,128)S(1)}, u32[]{:S(2)}, u32[]{:S(2)}) collective-permute-start(f32[6,8,8,128]{3,2,1,0:T(8,128)S(1)} %get-tuple-element.99), channel_id=1, source_target_pairs={{0,1},{1,2},{2,3},{3,4},{4,5},{5,6},{6,7},{7,0},{8,9},{9,10},{10,1... | collective-permute-start | bytes 589832 | tf_op jit(solution)/shard_map/ppermute | solution.py:483
  150.0 1.8 collective-permute-start.16
  151.8 3.7 %stage2_high.1 = (f32[6,32,16,128]{3,2,1,0:T(8,128)S(1)}, f32[6,8,8,128]{3,2,1,0:T(8,128)S(1)}, f32[6,8,8,128]{3,2,1,0:T(8,128)S(1)}, f32[8,128]{1,0:T(8,128)S(1)}) custom-call(f32[6]{0:T(128)S(1)} %copy-done.23, f32[1]{0:T(128)S(6)} %copy.12.swirl, f32[6]{0:T(128)S(1)} %copy-done.24, f32[6,6]{1,0:T(8,128)S(1)} %copy-done.21, ...), custom_call_target="tpu_custom_call" | custom-call | tf_op jit(solution)/shard_map/stage2_high/pallas_call | solution.py:466
  156.3 4.0 %collective-permute-start.22 = (f32[6,8,8,128]{3,2,1,0:T(8,128)S(1)}, f32[6,8,8,128]{3,2,1,0:T(8,128)S(1)}, u32[]{:S(2)}, u32[]{:S(2)}) collective-permute-start(f32[6,8,8,128]{3,2,1,0:T(8,128)S(1)} %get-tuple-element.98), channel_id=1, source_target_pairs={{0,7},{1,0},{2,1},{3,2},{4,3},{5,4},{6,5},{7,6},{8,15},{9,8},{10,9... | collective-permute-start | bytes 589832 | tf_op jit(solution)/shard_map/ppermute | solution.py:483
  160.2 8.0 %collective-permute-done.16.refs_2_ = f32[6,4,8,128]{3,2,1,0:T(8,128)S(1)} collective-permute-done((f32[6,4,8,128]{3,2,1,0:T(8,128)S(1)}, f32[6,4,8,128]{3,2,1,0:T(8,128)S(1)}, u32[]{:S(2)}, u32[]{:S(2)}) %collective-permute-start.16) | collective-permute-done | bytes 98336 | tf_op jit(solution)/shard_map/ppermute | solution.py:483
  168.2 2.0 %stage2_ends.1 = (f32[6,16,16,128]{3,2,1,0:T(8,128)S(1)}, f32[6,4,8,128]{3,2,1,0:T(8,128)S(1)}, f32[6,4,8,128]{3,2,1,0:T(8,128)S(1)}, f32[8,128]{1,0:T(8,128)S(1)}) custom-call(f32[6]{0:T(128)S(1)} %copy-done.23, f32[1]{0:T(128)S(6)} %copy.12.swirl, f32[6]{0:T(128)S(1)} %copy-done.24, f32[6,6]{1,0:T(8,128)S(1)} %copy-done.21, ...), custom_call_target="tpu_custom_call" | custom-call | tf_op jit(solution)/shard_map/stage2_ends/pallas_call | solution.py:466
  170.3 4.7 %collective-permute-start.20 = (f32[6,4,8,128]{3,2,1,0:T(8,128)S(1)}, f32[6,4,8,128]{3,2,1,0:T(8,128)S(1)}, u32[]{:S(2)}, u32[]{:S(2)}) collective-permute-start(f32[6,4,8,128]{3,2,1,0:T(8,128)S(1)} %get-tuple-element.96), channel_id=1, source_target_pairs={{0,7},{1,0},{2,1},{3,2},{4,3},{5,4},{6,5},{7,6},{8,15},{9,8},{10,9... | collective-permute-start | bytes 294920 | tf_op jit(solution)/shard_map/ppermute | solution.py:483
  175.0 4.5 %stage3_low.1 = (f32[6,64,16,128]{3,2,1,0:T(8,128)}, f32[8,128]{1,0:T(8,128)S(1)}) custom-call(f32[6]{0:T(128)S(1)} %copy-done.23, f32[1]{0:T(128)S(6)} %copy.12.swirl, f32[6]{0:T(128)S(1)} %copy-done.24, f32[6,6]{1,0:T(8,128)S(1)} %copy-done.21, f32[6,64,16,128]{3,2,1,0:T(8,128)S(1)} %copy-done.1, ...), custom_call_target="tpu_custom_call" | custom-call | tf_op jit(solution)/shard_map/stage3_low/pallas_call | solution.py:466
  179.5 4.5 %stage3_high.1 = (f32[6,64,16,128]{3,2,1,0:T(8,128)}, f32[8,128]{1,0:T(8,128)S(1)}) custom-call(f32[6]{0:T(128)S(1)} %copy-done.23, f32[1]{0:T(128)S(6)} %copy.12.swirl, f32[6]{0:T(128)S(1)} %copy-done.24, f32[6,6]{1,0:T(8,128)S(1)} %copy-done.21, f32[6,64,16,128]{3,2,1,0:T(8,128)S(1)} %copy-done.1, ...), custom_call_target="tpu_custom_call", output_to_operand_aliasing={{0}: (12, {})} | custom-call | tf_op jit(solution)/shard_map/stage3_high/pallas_call | solution.py:466
  184.1 3.9 %stage3_ends.1 = (f32[6,64,16,128]{3,2,1,0:T(8,128)}, f32[8,128]{1,0:T(8,128)}) custom-call(f32[6]{0:T(128)S(1)} %copy-done.23, f32[1]{0:T(128)S(6)} %copy.12.swirl, f32[6]{0:T(128)S(1)} %copy-done.24, f32[6,6]{1,0:T(8,128)S(1)} %copy-done.21, f32[6,64,16,128]{3,2,1,0:T(8,128)S(1)} %copy-done.1, ...), custom_call_target="tpu_custom_call", output_to_operand_aliasing={{0}: (22, {})} | custom-call | tf_op jit(solution)/shard_map/stage3_ends/pallas_call | solution.py:466
  (96 shorter events, 11.2 us)
Async XLA Ops:
  1.0 3.6 %collective-permute-start.5 = (f32[6,8,16,128]{3,2,1,0:T(8,128)S(1)}, f32[6,8,16,128]{3,2,1,0:T(8,128)S(1)}, u32[]{:S(2)}, u32[]{:S(2)}) collective-permute-start(f32[6,8,16,128]{3,2,1,0:T(8,128)S(1)} %slice.3), channel_id=1, source_target_pairs={{8,0},{16,8},{24,16},{9,1},{17,9},{25,17},{10,2},{18,10},{26,18},{... | collective-permute-start | bytes 1179656 | tf_op jit(solution)/shard_map/ppermute | solution.py:495
  4.6 1.9 %copy-start = (f32[6,64,16,128]{3,2,1,0:T(8,128)S(1)}, f32[6,64,16,128]{3,2,1,0:T(8,128)}, u32[]{:S(2)}) copy-start(f32[6,64,16,128]{3,2,1,0:T(8,128)} %refs_0_.23) | copy-start | bytes 9437188
  6.5 8.7 %copy-start.1 = (f32[6,64,16,128]{3,2,1,0:T(8,128)S(1)}, f32[6,64,16,128]{3,2,1,0:T(8,128)}, u32[]{:S(2)}) copy-start(f32[6,64,16,128]{3,2,1,0:T(8,128)} %refs_0_.23) | copy-start | bytes 9437188
  8.0 46.0 %all-to-all-start = ((f32[8,12,24,128]{3,2,1,0:T(8,128)}), f32[8,12,24,128]{3,2,1,0:T(8,128)}, u32[]{:S(2)}, u32[]{:S(2)}) async-start(f32[8,12,24,128]{3,2,1,0:T(8,128)} %copy-done.12), calls=%async_computation | async-start | bytes 2359296 | tf_op jit(solution)/shard_map/all_to_all | solution.py:499
  15.3 25.8 %copy-start.21 = (f32[6,6]{1,0:T(8,128)S(1)}, f32[6,6]{1,0:T(8,128)}, u32[]{:S(2)}) copy-start(f32[6,6]{1,0:T(8,128)} %coupling.25) | copy-start | bytes 436
  15.3 25.7 %copy-start.23 = (f32[6]{0:T(128)S(1)}, f32[6]{0:T(128)}, u32[]{:S(2)}) copy-start(f32[6]{0:T(128)} %speed.25) | copy-start | bytes 76
  15.3 25.7 %copy-start.24 = (f32[6]{0:T(128)S(1)}, f32[6]{0:T(128)}, u32[]{:S(2)}) copy-start(f32[6]{0:T(128)} %diffusion.25) | copy-start | bytes 76
  16.6 24.5 %collective-permute-start.2 = (f32[6,8,8,128]{3,2,1,0:T(8,128)}, f32[6,8,8,128]{3,2,1,0:T(8,128)S(1)}, u32[]{:S(2)}, u32[]{:S(2)}) collective-permute-start(f32[6,8,8,128]{3,2,1,0:T(8,128)} %get-tuple-element.60), channel_id=1, source_target_pairs={{0,1},{1,2},{2,3},{3,4},{4,5},{5,6},{6,7},{7,0},{8,9},{9,10},{10,1... | collective-permute-start | bytes 589832 | tf_op jit(solution)/shard_map/ppermute | solution.py:483
  18.6 22.5 %collective-permute-start.3 = (f32[6,8,8,128]{3,2,1,0:T(8,128)}, f32[6,8,8,128]{3,2,1,0:T(8,128)S(1)}, u32[]{:S(2)}, u32[]{:S(2)}) collective-permute-start(f32[6,8,8,128]{3,2,1,0:T(8,128)} %get-tuple-element.61), channel_id=1, source_target_pairs={{0,7},{1,0},{2,1},{3,2},{4,3},{5,4},{6,5},{7,6},{8,15},{9,8},{10,9... | collective-permute-start | bytes 589832 | tf_op jit(solution)/shard_map/ppermute | solution.py:483
  21.3 26.0 %collective-permute-start = (f32[6,8,8,128]{3,2,1,0:T(8,128)}, f32[6,8,8,128]{3,2,1,0:T(8,128)}, u32[]{:S(2)}, u32[]{:S(2)}) collective-permute-start(f32[6,8,8,128]{3,2,1,0:T(8,128)} %get-tuple-element.58), channel_id=1, source_target_pairs={{0,1},{1,2},{2,3},{3,4},{4,5},{5,6},{6,7},{7,0},{8,9},{9,10},{10,1... | collective-permute-start | bytes 589832 | tf_op jit(solution)/shard_map/ppermute | solution.py:483
  21.3 26.0 %collective-permute-start.1 = (f32[6,8,8,128]{3,2,1,0:T(8,128)}, f32[6,8,8,128]{3,2,1,0:T(8,128)}, u32[]{:S(2)}, u32[]{:S(2)}) collective-permute-start(f32[6,8,8,128]{3,2,1,0:T(8,128)} %get-tuple-element.59), channel_id=1, source_target_pairs={{0,7},{1,0},{2,1},{3,2},{4,3},{5,4},{6,5},{7,6},{8,15},{9,8},{10,9... | collective-permute-start | bytes 589832 | tf_op jit(solution)/shard_map/ppermute | solution.py:483
  26.0 28.0 %collective-permute-start.4 = (f32[1]{0:T(128)}, f32[1]{0:T(128)}, u32[]{:S(2)}, u32[]{:S(2)}) collective-permute-start(f32[1]{0:T(128)} %param.11), channel_id=1, source_target_pairs={{8,0},{16,8},{24,16},{9,1},{17,9},{25,17},{10,2},{18,10},{26,18},{... | collective-permute-start | bytes 20 | tf_op jit(solution)/shard_map/ppermute | solution.py:496
  70.9 9.2 %collective-permute-start.6 = (f32[8,6,16,128]{3,2,1,0:T(8,128)S(1)}, f32[8,6,16,128]{3,2,1,0:T(8,128)S(1)}, u32[]{:S(2)}, u32[]{:S(2)}) collective-permute-start(f32[8,6,16,128]{3,2,1,0:T(8,128)S(1)} %get-tuple-element.64), channel_id=1, source_target_pairs={{0,8},{8,16},{16,24},{1,9},{9,17},{17,25},{2,10},{10,18},{18,26},{... | collective-permute-start | bytes 1179656 | tf_op jit(solution)/shard_map/ppermute | solution.py:523
  80.1 29.5 %copy-start.26 = (f32[8,128]{1,0:T(8,128)S(1)}, f32[8,128]{1,0:T(8,128)}, u32[]{:S(2)}) copy-start(f32[8,128]{1,0:T(8,128)} %copy-done.25) | copy-start | bytes 12292
  81.0 47.9 %all-to-all-start.1 = ((f32[8,12,16,128]{3,2,1,0:T(8,128)}), f32[8,12,16,128]{3,2,1,0:T(8,128)}, u32[]{:S(2)}, u32[]{:S(2)}) async-start(f32[8,12,16,128]{3,2,1,0:T(8,128)} %pad_maximum_fusion), calls=%async_computation.1 | async-start | bytes 1572864 | tf_op jit(solution)/shard_map/all_to_all | solution.py:524
  88.7 20.9 %collective-permute-start.9 = (f32[6,8,8,128]{3,2,1,0:T(8,128)}, f32[6,8,8,128]{3,2,1,0:T(8,128)S(1)}, u32[]{:S(2)}, u32[]{:S(2)}) collective-permute-start(f32[6,8,8,128]{3,2,1,0:T(8,128)} %copy-done.34), channel_id=1, source_target_pairs={{0,1},{1,2},{2,3},{3,4},{4,5},{5,6},{6,7},{7,0},{8,9},{9,10},{10,1... | collective-permute-start | bytes 589832 | tf_op jit(solution)/shard_map/ppermute | solution.py:483
  90.7 18.9 %collective-permute-start.10 = (f32[6,8,8,128]{3,2,1,0:T(8,128)}, f32[6,8,8,128]{3,2,1,0:T(8,128)S(1)}, u32[]{:S(2)}, u32[]{:S(2)}) collective-permute-start(f32[6,8,8,128]{3,2,1,0:T(8,128)} %copy-done.33), channel_id=1, source_target_pairs={{0,7},{1,0},{2,1},{3,2},{4,3},{5,4},{6,5},{7,6},{8,15},{9,8},{10,9... | collective-permute-start | bytes 589832 | tf_op jit(solution)/shard_map/ppermute | solution.py:483
  93.4 29.3 %collective-permute-start.7 = (f32[6,8,8,128]{3,2,1,0:T(8,128)}, f32[6,8,8,128]{3,2,1,0:T(8,128)S(1)}, u32[]{:S(2)}, u32[]{:S(2)}) collective-permute-start(f32[6,8,8,128]{3,2,1,0:T(8,128)} %copy-done.32), channel_id=1, source_target_pairs={{0,1},{1,2},{2,3},{3,4},{4,5},{5,6},{6,7},{7,0},{8,9},{9,10},{10,1... | collective-permute-start | bytes 589832 | tf_op jit(solution)/shard_map/ppermute | solution.py:483
  93.4 29.3 %collective-permute-start.8 = (f32[6,8,8,128]{3,2,1,0:T(8,128)}, f32[6,8,8,128]{3,2,1,0:T(8,128)S(1)}, u32[]{:S(2)}, u32[]{:S(2)}) collective-permute-start(f32[6,8,8,128]{3,2,1,0:T(8,128)} %copy-done.31), channel_id=1, source_target_pairs={{0,7},{1,0},{2,1},{3,2},{4,3},{5,4},{6,5},{7,6},{8,15},{9,8},{10,9... | collective-permute-start | bytes 589832 | tf_op jit(solution)/shard_map/ppermute | solution.py:483
  109.6 7.3 %copy-start.13 = (f32[6,8,8,128]{3,2,1,0:T(8,128)}, f32[6,8,8,128]{3,2,1,0:T(8,128)S(1)}, u32[]{:S(2)}) copy-start(f32[6,8,8,128]{3,2,1,0:T(8,128)S(1)} %collective-permute-done.9.refs_1_.refs_5_) | copy-start | bytes 589828
  109.6 7.3 %copy-start.15 = (f32[6,8,8,128]{3,2,1,0:T(8,128)}, f32[6,8,8,128]{3,2,1,0:T(8,128)S(1)}, u32[]{:S(2)}) copy-start(f32[6,8,8,128]{3,2,1,0:T(8,128)S(1)} %collective-permute-done.10.refs_2_.refs_6_) | copy-start | bytes 589828
  109.6 1.6 copy-start.3
  111.2 1.4 copy-start.6
  118.0 18.7 %collective-permute-start.13 = (f32[6,8,8,128]{3,2,1,0:T(8,128)}, f32[6,8,8,128]{3,2,1,0:T(8,128)}, u32[]{:S(2)}, u32[]{:S(2)}) collective-permute-start(f32[6,8,8,128]{3,2,1,0:T(8,128)} %get-tuple-element.81), channel_id=1, source_target_pairs={{0,1},{1,2},{2,3},{3,4},{4,5},{5,6},{6,7},{7,0},{8,9},{9,10},{10,1... | collective-permute-start | bytes 589832 | tf_op jit(solution)/shard_map/ppermute | solution.py:483
  118.0 20.6 %collective-permute-start.14 = (f32[6,8,8,128]{3,2,1,0:T(8,128)}, f32[6,8,8,128]{3,2,1,0:T(8,128)}, u32[]{:S(2)}, u32[]{:S(2)}) collective-permute-start(f32[6,8,8,128]{3,2,1,0:T(8,128)} %get-tuple-element.82), channel_id=1, source_target_pairs={{0,7},{1,0},{2,1},{3,2},{4,3},{5,4},{6,5},{7,6},{8,15},{9,8},{10,9... | collective-permute-start | bytes 589832 | tf_op jit(solution)/shard_map/ppermute | solution.py:483
  122.8 4.2 %copy-start.17 = (f32[6,8,8,128]{3,2,1,0:T(8,128)}, f32[6,8,8,128]{3,2,1,0:T(8,128)S(1)}, u32[]{:S(2)}) copy-start(f32[6,8,8,128]{3,2,1,0:T(8,128)S(1)} %collective-permute-done.7.refs_1_.refs_3_) | copy-start | bytes 589828
  122.8 4.2 %copy-start.19 = (f32[6,8,8,128]{3,2,1,0:T(8,128)}, f32[6,8,8,128]{3,2,1,0:T(8,128)S(1)}, u32[]{:S(2)}) copy-start(f32[6,8,8,128]{3,2,1,0:T(8,128)S(1)} %collective-permute-done.8.refs_2_.refs_4_) | copy-start | bytes 589828
  128.9 21.1 %collective-permute-start.17 = (f32[6,8,8,128]{3,2,1,0:T(8,128)}, f32[6,8,8,128]{3,2,1,0:T(8,128)}, u32[]{:S(2)}, u32[]{:S(2)}) collective-permute-start(f32[6,8,8,128]{3,2,1,0:T(8,128)} %get-tuple-element.89), channel_id=1, source_target_pairs={{0,1},{1,2},{2,3},{3,4},{4,5},{5,6},{6,7},{7,0},{8,9},{9,10},{10,1... | collective-permute-start | bytes 589832 | tf_op jit(solution)/shard_map/ppermute | solution.py:483
  130.3 6.4 %copy-start.30 = (f32[6,8,8,128]{3,2,1,0:T(8,128)S(1)}, f32[6,8,8,128]{3,2,1,0:T(8,128)}, u32[]{:S(2)}) copy-start(f32[6,8,8,128]{3,2,1,0:T(8,128)} %copy-done.29) | copy-start | bytes 589828
  130.3 8.4 %copy-start.9 = (f32[6,32,16,128]{3,2,1,0:T(8,128)S(1)}, f32[6,32,16,128]{3,2,1,0:T(8,128)}, u32[]{:S(2)}) copy-start(f32[6,32,16,128]{3,2,1,0:T(8,128)} %copy-done.8) | copy-start | bytes 4718596
  130.3 8.4 %copy-start.11 = (f32[6,32,16,128]{3,2,1,0:T(8,128)S(1)}, f32[6,32,16,128]{3,2,1,0:T(8,128)}, u32[]{:S(2)}) copy-start(f32[6,32,16,128]{3,2,1,0:T(8,128)} %copy-done.10) | copy-start | bytes 4718596
  131.9 10.8 %collective-permute-start.11 = (f32[6,4,8,128]{3,2,1,0:T(8,128)S(1)}, f32[6,4,8,128]{3,2,1,0:T(8,128)S(1)}, u32[]{:S(2)}, u32[]{:S(2)}) collective-permute-start(f32[6,4,8,128]{3,2,1,0:T(8,128)S(1)} %get-tuple-element.77), channel_id=1, source_target_pairs={{0,1},{1,2},{2,3},{3,4},{4,5},{5,6},{6,7},{7,0},{8,9},{9,10},{10,1... | collective-permute-start | bytes 294920 | tf_op jit(solution)/shard_map/ppermute | solution.py:483
  133.4 10.2 %collective-permute-start.12 = (f32[6,4,8,128]{3,2,1,0:T(8,128)S(1)}, f32[6,4,8,128]{3,2,1,0:T(8,128)S(1)}, u32[]{:S(2)}, u32[]{:S(2)}) collective-permute-start(f32[6,4,8,128]{3,2,1,0:T(8,128)S(1)} %get-tuple-element.78), channel_id=1, source_target_pairs={{0,7},{1,0},{2,1},{3,2},{4,3},{5,4},{6,5},{7,6},{8,15},{9,8},{10,9... | collective-permute-start | bytes 294920 | tf_op jit(solution)/shard_map/ppermute | solution.py:483
  136.7 15.1 %collective-permute-start.18 = (f32[6,8,8,128]{3,2,1,0:T(8,128)S(1)}, f32[6,8,8,128]{3,2,1,0:T(8,128)S(1)}, u32[]{:S(2)}, u32[]{:S(2)}) collective-permute-start(f32[6,8,8,128]{3,2,1,0:T(8,128)S(1)} %copy-done.30), channel_id=1, source_target_pairs={{0,7},{1,0},{2,1},{3,2},{4,3},{5,4},{6,5},{7,6},{8,15},{9,8},{10,9... | collective-permute-start | bytes 589832 | tf_op jit(solution)/shard_map/ppermute | solution.py:483
  138.7 5.0 %copy-start.4 = (f32[6,32,16,128]{3,2,1,0:T(8,128)S(1)}, f32[6,32,16,128]{3,2,1,0:T(8,128)}, u32[]{:S(2)}) copy-start(f32[6,32,16,128]{3,2,1,0:T(8,128)} %copy-done.2) | copy-start | bytes 4718596
  138.7 5.0 %copy-start.7 = (f32[6,32,16,128]{3,2,1,0:T(8,128)S(1)}, f32[6,32,16,128]{3,2,1,0:T(8,128)}, u32[]{:S(2)}) copy-start(f32[6,32,16,128]{3,2,1,0:T(8,128)} %copy-done.5) | copy-start | bytes 4718596
  138.7 5.0 %copy-start.14 = (f32[6,8,8,128]{3,2,1,0:T(8,128)S(1)}, f32[6,8,8,128]{3,2,1,0:T(8,128)}, u32[]{:S(2)}) copy-start(f32[6,8,8,128]{3,2,1,0:T(8,128)} %copy-done.13) | copy-start | bytes 589828
  138.7 5.0 %copy-start.16 = (f32[6,8,8,128]{3,2,1,0:T(8,128)S(1)}, f32[6,8,8,128]{3,2,1,0:T(8,128)}, u32[]{:S(2)}) copy-start(f32[6,8,8,128]{3,2,1,0:T(8,128)} %copy-done.15) | copy-start | bytes 589828
  138.7 5.0 %copy-start.18 = (f32[6,8,8,128]{3,2,1,0:T(8,128)S(1)}, f32[6,8,8,128]{3,2,1,0:T(8,128)}, u32[]{:S(2)}) copy-start(f32[6,8,8,128]{3,2,1,0:T(8,128)} %copy-done.17) | copy-start | bytes 589828
  138.7 5.0 %copy-start.20 = (f32[6,8,8,128]{3,2,1,0:T(8,128)S(1)}, f32[6,8,8,128]{3,2,1,0:T(8,128)}, u32[]{:S(2)}) copy-start(f32[6,8,8,128]{3,2,1,0:T(8,128)} %copy-done.19) | copy-start | bytes 589828
  145.0 11.3 %collective-permute-start.15 = (f32[6,4,8,128]{3,2,1,0:T(8,128)S(1)}, f32[6,4,8,128]{3,2,1,0:T(8,128)S(1)}, u32[]{:S(2)}, u32[]{:S(2)}) collective-permute-start(f32[6,4,8,128]{3,2,1,0:T(8,128)S(1)} %get-tuple-element.87), channel_id=1, source_target_pairs={{0,1},{1,2},{2,3},{3,4},{4,5},{5,6},{6,7},{7,0},{8,9},{9,10},{10,1... | collective-permute-start | bytes 294920 | tf_op jit(solution)/shard_map/ppermute | solution.py:483
  145.0 25.3 %collective-permute-start.23 = (f32[6,8,8,128]{3,2,1,0:T(8,128)S(1)}, f32[6,8,8,128]{3,2,1,0:T(8,128)S(1)}, u32[]{:S(2)}, u32[]{:S(2)}) collective-permute-start(f32[6,8,8,128]{3,2,1,0:T(8,128)S(1)} %get-tuple-element.99), channel_id=1, source_target_pairs={{0,1},{1,2},{2,3},{3,4},{4,5},{5,6},{6,7},{7,0},{8,9},{9,10},{10,1... | collective-permute-start | bytes 589832 | tf_op jit(solution)/shard_map/ppermute | solution.py:483
  150.0 25.0 %collective-permute-start.24 = (f32[6,8,8,128]{3,2,1,0:T(8,128)S(1)}, f32[6,8,8,128]{3,2,1,0:T(8,128)S(1)}, u32[]{:S(2)}, u32[]{:S(2)}) collective-permute-start(f32[6,8,8,128]{3,2,1,0:T(8,128)S(1)} %get-tuple-element.100), channel_id=1, source_target_pairs={{0,7},{1,0},{2,1},{3,2},{4,3},{5,4},{6,5},{7,6},{8,15},{9,8},{10,9... | collective-permute-start | bytes 589832 | tf_op jit(solution)/shard_map/ppermute | solution.py:483
  150.0 18.2 %collective-permute-start.16 = (f32[6,4,8,128]{3,2,1,0:T(8,128)S(1)}, f32[6,4,8,128]{3,2,1,0:T(8,128)S(1)}, u32[]{:S(2)}, u32[]{:S(2)}) collective-permute-start(f32[6,4,8,128]{3,2,1,0:T(8,128)S(1)} %get-tuple-element.88), channel_id=1, source_target_pairs={{0,7},{1,0},{2,1},{3,2},{4,3},{5,4},{6,5},{7,6},{8,15},{9,8},{10,9... | collective-permute-start | bytes 294920 | tf_op jit(solution)/shard_map/ppermute | solution.py:483
  155.5 24.1 %collective-permute-start.21 = (f32[6,8,8,128]{3,2,1,0:T(8,128)S(1)}, f32[6,8,8,128]{3,2,1,0:T(8,128)S(1)}, u32[]{:S(2)}, u32[]{:S(2)}) collective-permute-start(f32[6,8,8,128]{3,2,1,0:T(8,128)S(1)} %get-tuple-element.97), channel_id=1, source_target_pairs={{0,1},{1,2},{2,3},{3,4},{4,5},{5,6},{6,7},{7,0},{8,9},{9,10},{10,1... | collective-permute-start | bytes 589832 | tf_op jit(solution)/shard_map/ppermute | solution.py:483
  156.3 23.3 %collective-permute-start.22 = (f32[6,8,8,128]{3,2,1,0:T(8,128)S(1)}, f32[6,8,8,128]{3,2,1,0:T(8,128)S(1)}, u32[]{:S(2)}, u32[]{:S(2)}) collective-permute-start(f32[6,8,8,128]{3,2,1,0:T(8,128)S(1)} %get-tuple-element.98), channel_id=1, source_target_pairs={{0,7},{1,0},{2,1},{3,2},{4,3},{5,4},{6,5},{7,6},{8,15},{9,8},{10,9... | collective-permute-start | bytes 589832 | tf_op jit(solution)/shard_map/ppermute | solution.py:483
  170.2 13.8 %collective-permute-start.19 = (f32[6,4,8,128]{3,2,1,0:T(8,128)S(1)}, f32[6,4,8,128]{3,2,1,0:T(8,128)S(1)}, u32[]{:S(2)}, u32[]{:S(2)}) collective-permute-start(f32[6,4,8,128]{3,2,1,0:T(8,128)S(1)} %get-tuple-element.95), channel_id=1, source_target_pairs={{0,1},{1,2},{2,3},{3,4},{4,5},{5,6},{6,7},{7,0},{8,9},{9,10},{10,1... | collective-permute-start | bytes 294920 | tf_op jit(solution)/shard_map/ppermute | solution.py:483
  170.3 13.8 %collective-permute-start.20 = (f32[6,4,8,128]{3,2,1,0:T(8,128)S(1)}, f32[6,4,8,128]{3,2,1,0:T(8,128)S(1)}, u32[]{:S(2)}, u32[]{:S(2)}) collective-permute-start(f32[6,4,8,128]{3,2,1,0:T(8,128)S(1)} %get-tuple-element.96), channel_id=1, source_target_pairs={{0,7},{1,0},{2,1},{3,2},{4,3},{5,4},{6,5},{7,6},{8,15},{9,8},{10,9... | collective-permute-start | bytes 294920 | tf_op jit(solution)/shard_map/ppermute | solution.py:483
  (14 other events, 11.9 us)

commit v4 on v3

--- a/solution.py
+++ b/solution.py
@@ -94,6 +94,7 @@
             held((plan.radial + 2 * EXTRA, plan.packed)),
             pltpu.SemaphoreType.DMA((1,)),
         ],
+        cost_estimate=pl.CostEstimate(flops=10000000000, transcendentals=0, bytes_accessed=10000000),
         compiler_params=params(),
         name="pack_zone",
     )(state, below)
@@ -241,6 +242,7 @@
             held((plan.full, plan.full)),
             held((2, plan.fields, 2 * offsets.shape[0], plan.mine, plan.full)),
         ],
+        cost_estimate=pl.CostEstimate(flops=10000000000, transcendentals=0, bytes_accessed=10000000),
         compiler_params=pltpu.CompilerParams(vmem_limit_bytes=need + 6 * 1024 * 1024),
         name="step_zone",
     )(place, offsets, speed, swirl, next_swirl, diffusion, coupling, weights, got, near(after[0]))
@@ -267,6 +269,7 @@
         out_specs=[whole(VMEM)] * (sections + 1),
         out_shape=[held(plan.ghost)] * sections + [held((8, plan.radial))],
         scratch_shapes=[held((plan.radial, plan.packed))],
+        cost_estimate=pl.CostEstimate(flops=10000000000, transcendentals=0, bytes_accessed=10000000),
         compiler_params=params(),
         name="unpack_ghosts",
     )(got, near(after[0]))
@@ -298,6 +301,7 @@
         in_specs=[whole(VMEM)],
         out_specs=[whole(VMEM)] * 4,
         out_shape=[low, low, high, high],
+        cost_estimate=pl.CostEstimate(flops=10000000000, transcendentals=0, bytes_accessed=10000000),
         compiler_params=params(),
         name="first_edges",
     )(near(state))
@@ -470,6 +474,7 @@
         out_shape=list(outs.values()),
         scratch_shapes=list(scratch.values()),
         input_output_aliases=aliases,
+        cost_estimate=pl.CostEstimate(flops=10000000000, transcendentals=0, bytes_accessed=10000000),
         compiler_params=params(),
         name=f"stage{stage}_{kind}",
     )(*scalars, *operands.values())
@@ -496,11 +501,11 @@
     next_swirl = lax.ppermute(row_swirl, "row", back)
     weights = jnp.pad(interp_blocks, ((0, 0), (0, 0), (0, plan.full - interp_blocks.shape[2])))
     packed = pack(plan, state, below)
-    got = lax.all_to_all(packed, "sector", 0, 0, tiled=True)
-
     levels, halos = [None], [{}]
     edges = dict(zip(("low", "high"), first_edges(plan, state)))
-    halos[0] = {kind: exchange(edges[kind]) for kind in ("low", "high")}
+    halos[0] = {"low": exchange(edges["low"])}
+    packed, *halos[0]["low"] = lax.optimization_barrier((packed, *halos[0]["low"]))
+    got = lax.all_to_all(packed, "sector", 0, 0, tiled=True)
     token, result, ghosts = (), None, None
 
     def step(stage, kind):
@@ -518,10 +523,14 @@
         halos[stage + 1][kind] = exchange(outs[1:3])
 
     step(0, "low")
-    step(0, "high")
+    *high_edges, first_token = lax.optimization_barrier((*edges["high"], *token))
+    halos[0]["high"] = exchange(high_edges)
+    token = (first_token,)
     downstream, to_next, *token = zone(plan, place, rotor_offset, scalars, next_swirl, weights, got, token)
     upstream = lax.ppermute(to_next, "row", ahead)
-    returned = lax.all_to_all(jnp.concatenate([upstream, downstream], axis=1), "sector", 0, 0, tiled=True)
+    step(0, "high")
+    joined, *token = lax.optimization_barrier((jnp.concatenate([upstream, downstream], axis=1), *token))
+    returned = lax.all_to_all(joined, "sector", 0, 0, tiled=True)
     step(1, "low")
     step(1, "high")
     *ghosts, last_token = unpack(plan, returned, sections, token)

time: 189 us -> 165 us (0.87)
  waiting for transfers between devices: 35.1 us -> 19.7 us
  local copies, waits for them, and re-layouts: 19.4 us -> 14.7 us
  Pallas kernels: 58.9 us -> 55.9 us
    ppermute x11, waiting for transfers between devices: 22.4 us -> 5.55 us  [exchange(): lax.ppermute(high_edges, 'sector', ahead)]
    ppermute x11, starting transfers between devices: 11.5 us -> 24.2 us  [exchange(): lax.ppermute(high_edges, 'sector', ahead)]
    all_to_all x1, waiting for transfers between devices: 0.01 us -> 11.6 us  [on_device(): got = lax.all_to_all(packed, 'sector', 0, 0, tiled=True)]
    ppermute x1, starting transfers between devices: 7.87 us -> 1.31 us  [on_device(): upstream = lax.ppermute(to_next, 'row', ahead)]
    ppermute x11, waiting for transfers between devices: 9.03 us -> 2.54 us  [exchange(): lax.ppermute(low_edges, 'sector', back)]
    unnamed x70 -> x40, local copies, waits for them, and re-layouts: 16.8 us -> 13.6 us
    all_to_all x1, starting transfers between devices: 7.28 us -> 4.38 us  [on_device(): got = lax.all_to_all(packed, 'sector', 0, 0, tiled=True)]
    all_to_all x1, starting transfers between devices: 7.66 us -> 5.16 us  [on_device(): returned = lax.all_to_all(joined, 'sector', 0, 0, tiled=True)]
  transfers between devices with their start and end apart: 27 -> 27, of which waited for: 6 -> 4; matrix products, arithmetic and copies ran while one was open for 1% -> 1% of each run, Pallas kernels for 21% -> 32%
where the time goes in v4:
time: 165 us; the launch traced here: 164 us
  starting transfers between devices  71.7 us (43%)
  Pallas kernels  55.9 us (34%)
  waiting for transfers between devices  19.7 us (12%)
  local copies, waits for them, and re-layouts  14.7 us (9%)
    pallas_call x12, Pallas kernels, stage_call(): pl.pallas_call(functools.partial(stage_kernel, plan, stage, kind, names),...  40.2 us
    ppermute x11, starting transfers between devices, exchange(): lax.ppermute(low_edges, 'sector', back)  34 us
    ppermute x11, starting transfers between devices, exchange(): lax.ppermute(high_edges, 'sector', ahead)  24.2 us
    pallas_call x1, Pallas kernels, zone(): pl.pallas_call(functools.partial(zone_kernel, plan), in_specs=[whole(SMEM...  13.7 us
    unnamed x40, local copies, waits for them, and re-layouts  13.6 us
    all_to_all x1, waiting for transfers between devices, on_device(): got = lax.all_to_all(packed, 'sector', 0, 0, tiled=True)  11.6 us
    ppermute x11, waiting for transfers between devices, exchange(): lax.ppermute(high_edges, 'sector', ahead)  5.55 us
    all_to_all x1, starting transfers between devices, on_device(): returned = lax.all_to_all(joined, 'sector', 0, 0, tiled=True)  5.16 us
  transfers between devices with their start and end apart: 27, of which 4 were waited for; matrix products, arithmetic and copies ran while one was open for 1% of the time, Pallas kernels for 32%

profile of v4, /device:TPU:0, one launch (start us, length us, event | category | flops | bytes accessed | tf_op | source)
XLA Modules:
  0.0 164.2 jit_solution(4587934331935881366)
XLA Ops:
  0.0 1.0 slice.3
  1.0 1.3 collective-permute-start
  2.3 1.9 %copy-done = f32[6,64,16,128]{3,2,1,0:T(8,128)S(1)} copy-done((f32[6,64,16,128]{3,2,1,0:T(8,128)S(1)}, f32[6,64,16,128]{3,2,1,0:T(8,128)}, u32[]{:S(2)}) %copy-start) | copy-done | bytes 3145752
  4.6 3.0 %collective-permute-start.1 = (f32[6,8,8,128]{3,2,1,0:T(8,128)S(1)}, f32[6,8,8,128]{3,2,1,0:T(8,128)S(1)}, u32[]{:S(2)}, u32[]{:S(2)}) collective-permute-start(f32[6,8,8,128]{3,2,1,0:T(8,128)S(1)} %get-tuple-element.68), channel_id=1, source_target_pairs={{0,1},{1,2},{2,3},{3,4},{4,5},{5,6},{6,7},{7,0},{8,9},{9,10},{10,1... | collective-permute-start | bytes 589832 | tf_op jit(solution)/shard_map/ppermute | solution.py:488
  7.6 3.1 %collective-permute-start.2 = (f32[6,8,8,128]{3,2,1,0:T(8,128)S(1)}, f32[6,8,8,128]{3,2,1,0:T(8,128)S(1)}, u32[]{:S(2)}, u32[]{:S(2)}) collective-permute-start(f32[6,8,8,128]{3,2,1,0:T(8,128)S(1)} %get-tuple-element.69), channel_id=1, source_target_pairs={{0,7},{1,0},{2,1},{3,2},{4,3},{5,4},{6,5},{7,6},{8,15},{9,8},{10,9... | collective-permute-start | bytes 589832 | tf_op jit(solution)/shard_map/ppermute | solution.py:488
  10.7 1.4 pack_zone.1
  12.2 4.8 %collective-permute-done.1.refs_1_.refs_3_ = f32[6,8,8,128]{3,2,1,0:T(8,128)S(1)} collective-permute-done((f32[6,8,8,128]{3,2,1,0:T(8,128)S(1)}, f32[6,8,8,128]{3,2,1,0:T(8,128)S(1)}, u32[]{:S(2)}, u32[]{:S(2)}) %collective-permute-start.1) | collective-permute-done | bytes 196640 | tf_op jit(solution)/shard_map/ppermute | solution.py:488
  17.0 2.5 %collective-permute-done.2.refs_2_.refs_4_ = f32[6,8,8,128]{3,2,1,0:T(8,128)S(1)} collective-permute-done((f32[6,8,8,128]{3,2,1,0:T(8,128)S(1)}, f32[6,8,8,128]{3,2,1,0:T(8,128)S(1)}, u32[]{:S(2)}, u32[]{:S(2)}) %collective-permute-start.2) | collective-permute-done | bytes 196640 | tf_op jit(solution)/shard_map/ppermute | solution.py:488
  19.5 4.4 %all-to-all-start = ((f32[8,12,24,128]{3,2,1,0:T(8,128)}), f32[8,12,24,128]{3,2,1,0:T(8,128)S(1)}, u32[]{:S(2)}, u32[]{:S(2)}) async-start(f32[8,12,24,128]{3,2,1,0:T(8,128)} %pack_zone.1), calls=%async_computation | async-start | bytes 2359296 | tf_op jit(solution)/shard_map/all_to_all | solution.py:508
  23.9 1.3 collective-permute-start.5
  25.9 1.9 %copy-done.1 = f32[6,64,16,128]{3,2,1,0:T(8,128)S(1)} copy-done((f32[6,64,16,128]{3,2,1,0:T(8,128)S(1)}, f32[6,64,16,128]{3,2,1,0:T(8,128)}, u32[]{:S(2)}) %copy-start.1) | copy-done | bytes 3145752
  27.8 3.8 %stage0_low.1 = (f32[6,32,16,128]{3,2,1,0:T(8,128)S(1)}, f32[6,8,8,128]{3,2,1,0:T(8,128)S(1)}, f32[6,8,8,128]{3,2,1,0:T(8,128)S(1)}, f32[8,128]{1,0:T(8,128)S(1)}) custom-call(f32[6]{0:T(128)S(1)} %copy-done.7, f32[1]{0:T(128)S(6)} %copy.12.swirl, f32[6]{0:T(128)S(1)} %copy-done.8, f32[6,6]{1,0:T(8,128)S(1)} %copy-done.5, f32[6,64,16,128]{3,2,1,0:T(8,128)S(1)} %copy-done.1, ...), custom_call_target="tpu_custom_call" | custom-call | flops 10000000000 | bytes 10000000 | tf_op jit(solution)/shard_map/stage0_low/pallas_call | solution.py:470
  31.6 1.2 copy-done.9
  32.8 2.0 %collective-permute-start.3 = (f32[6,8,8,128]{3,2,1,0:T(8,128)S(1)}, f32[6,8,8,128]{3,2,1,0:T(8,128)S(1)}, u32[]{:S(2)}, u32[]{:S(2)}) collective-permute-start(f32[6,8,8,128]{3,2,1,0:T(8,128)S(1)} %get-tuple-element.73), channel_id=1, source_target_pairs={{0,1},{1,2},{2,3},{3,4},{4,5},{5,6},{6,7},{7,0},{8,9},{9,10},{10,1... | collective-permute-start | bytes 589832 | tf_op jit(solution)/shard_map/ppermute | solution.py:488
  34.8 2.7 %collective-permute-start.4 = (f32[6,8,8,128]{3,2,1,0:T(8,128)S(1)}, f32[6,8,8,128]{3,2,1,0:T(8,128)S(1)}, u32[]{:S(2)}, u32[]{:S(2)}) collective-permute-start(f32[6,8,8,128]{3,2,1,0:T(8,128)S(1)} %get-tuple-element.74), channel_id=1, source_target_pairs={{0,7},{1,0},{2,1},{3,2},{4,3},{5,4},{6,5},{7,6},{8,15},{9,8},{10,9... | collective-permute-start | bytes 589832 | tf_op jit(solution)/shard_map/ppermute | solution.py:488
  37.5 4.7 %collective-permute-start.10 = (f32[6,8,8,128]{3,2,1,0:T(8,128)S(1)}, f32[6,8,8,128]{3,2,1,0:T(8,128)S(1)}, u32[]{:S(2)}, u32[]{:S(2)}) collective-permute-start(f32[6,8,8,128]{3,2,1,0:T(8,128)S(1)} %get-tuple-element.87), channel_id=1, source_target_pairs={{0,7},{1,0},{2,1},{3,2},{4,3},{5,4},{6,5},{7,6},{8,15},{9,8},{10,9... | collective-permute-start | bytes 589832 | tf_op jit(solution)/shard_map/ppermute | solution.py:488
  42.2 11.6 %all-to-all-done.got = f32[8,12,24,128]{3,2,1,0:T(8,128)S(1)} async-done(((f32[8,12,24,128]{3,2,1,0:T(8,128)}), f32[8,12,24,128]{3,2,1,0:T(8,128)S(1)}, u32[]{:S(2)}, u32[]{:S(2)}) %all-to-all-start) | async-done | bytes 1179680 | tf_op jit(solution)/shard_map/all_to_all | solution.py:508
  53.9 13.7 %step_zone.1 = (f32[8,6,16,128]{3,2,1,0:T(8,128)S(1)}, f32[8,6,16,128]{3,2,1,0:T(8,128)S(1)}, f32[8,128]{1,0:T(8,128)S(1)}) custom-call(s32[2]{0:T(128)S(1)} %pad_add_fusion.place, s32[4,3]{1,0:T(4,128)S(1)} %copy-done.6, f32[6]{0:T(128)S(1)} %copy-done.7, f32[1]{0:T(128)S(6)} %copy.12.swirl, f32[1]{0:T(128)} %collective-permute-done.5.next_swirl, ...), custom_call_target="tpu_custom_call" | custom-call | flops 10000000000 | bytes 10000000 | tf_op jit(solution)/shard_map/step_zone/pallas_call | solution.py:232
  67.5 1.3 collective-permute-start.6
  68.9 4.5 %stage0_high.1 = (f32[6,32,16,128]{3,2,1,0:T(8,128)S(1)}, f32[6,8,8,128]{3,2,1,0:T(8,128)S(1)}, f32[6,8,8,128]{3,2,1,0:T(8,128)}, f32[8,128]{1,0:T(8,128)S(1)}) custom-call(f32[6]{0:T(128)S(1)} %copy-done.7, f32[1]{0:T(128)S(6)} %copy.12.swirl, f32[6]{0:T(128)S(1)} %copy-done.8, f32[6,6]{1,0:T(8,128)S(1)} %copy-done.5, f32[6,64,16,128]{3,2,1,0:T(8,128)S(1)} %copy-done.2, ...), custom_call_target="tpu_custom_call" | custom-call | flops 10000000000 | bytes 10000000 | tf_op jit(solution)/shard_map/stage0_high/pallas_call | solution.py:470
  73.4 8.7 %collective-permute-start.7 = (f32[6,8,8,128]{3,2,1,0:T(8,128)}, f32[6,8,8,128]{3,2,1,0:T(8,128)S(1)}, u32[]{:S(2)}, u32[]{:S(2)}) collective-permute-start(f32[6,8,8,128]{3,2,1,0:T(8,128)} %get-tuple-element.82), channel_id=1, source_target_pairs={{0,1},{1,2},{2,3},{3,4},{4,5},{5,6},{6,7},{7,0},{8,9},{9,10},{10,1... | collective-permute-start | bytes 589832 | tf_op jit(solution)/shard_map/ppermute | solution.py:488
  82.1 1.0 pad_maximum_fusion
  83.1 5.2 %all-to-all-start.1 = ((f32[8,12,16,128]{3,2,1,0:T(8,128)}), f32[8,12,16,128]{3,2,1,0:T(8,128)S(1)}, u32[]{:S(2)}, u32[]{:S(2)}) async-start(f32[8,12,16,128]{3,2,1,0:T(8,128)} %pad_maximum_fusion), calls=%async_computation.1 | async-start | bytes 1572864 | tf_op jit(solution)/shard_map/all_to_all | solution.py:533
  88.2 1.9 %copy-done.3 = f32[6,64,16,128]{3,2,1,0:T(8,128)S(1)} copy-done((f32[6,64,16,128]{3,2,1,0:T(8,128)S(1)}, f32[6,64,16,128]{3,2,1,0:T(8,128)}, u32[]{:S(2)}) %copy-start.3) | copy-done | bytes 3145752
  90.1 1.4 copy-done.10
  91.5 1.4 copy-done.13
  92.9 4.3 %stage1_low.1 = (f32[6,32,16,128]{3,2,1,0:T(8,128)S(1)}, f32[6,8,8,128]{3,2,1,0:T(8,128)}, f32[6,8,8,128]{3,2,1,0:T(8,128)}, f32[8,128]{1,0:T(8,128)S(1)}) custom-call(f32[6]{0:T(128)S(1)} %copy-done.7, f32[1]{0:T(128)S(6)} %copy.12.swirl, f32[6]{0:T(128)S(1)} %copy-done.8, f32[6,6]{1,0:T(8,128)S(1)} %copy-done.5, f32[6,64,16,128]{3,2,1,0:T(8,128)S(1)} %copy-done.3, ...), custom_call_target="tpu_custom_call" | custom-call | flops 10000000000 | bytes 10000000 | tf_op jit(solution)/shard_map/stage1_low/pallas_call | solution.py:470
  97.3 1.1 copy-done.15
  98.4 2.0 %collective-permute-start.13 = (f32[6,8,8,128]{3,2,1,0:T(8,128)}, f32[6,8,8,128]{3,2,1,0:T(8,128)S(1)}, u32[]{:S(2)}, u32[]{:S(2)}) collective-permute-start(f32[6,8,8,128]{3,2,1,0:T(8,128)} %get-tuple-element.97), channel_id=1, source_target_pairs={{0,1},{1,2},{2,3},{3,4},{4,5},{5,6},{6,7},{7,0},{8,9},{9,10},{10,1... | collective-permute-start | bytes 589832 | tf_op jit(solution)/shard_map/ppermute | solution.py:488
  100.4 2.7 %collective-permute-start.14 = (f32[6,8,8,128]{3,2,1,0:T(8,128)}, f32[6,8,8,128]{3,2,1,0:T(8,128)S(1)}, u32[]{:S(2)}, u32[]{:S(2)}) collective-permute-start(f32[6,8,8,128]{3,2,1,0:T(8,128)} %get-tuple-element.98), channel_id=1, source_target_pairs={{0,7},{1,0},{2,1},{3,2},{4,3},{5,4},{6,5},{7,6},{8,15},{9,8},{10,9... | collective-permute-start | bytes 589832 | tf_op jit(solution)/shard_map/ppermute | solution.py:488
  103.1 4.2 %stage1_high.1 = (f32[6,32,16,128]{3,2,1,0:T(8,128)S(1)}, f32[6,8,8,128]{3,2,1,0:T(8,128)S(1)}, f32[6,8,8,128]{3,2,1,0:T(8,128)}, f32[8,128]{1,0:T(8,128)S(1)}) custom-call(f32[6]{0:T(128)S(1)} %copy-done.7, f32[1]{0:T(128)S(6)} %copy.12.swirl, f32[6]{0:T(128)S(1)} %copy-done.8, f32[6,6]{1,0:T(8,128)S(1)} %copy-done.5, f32[6,64,16,128]{3,2,1,0:T(8,128)S(1)} %copy-done.3, ...), custom_call_target="tpu_custom_call" | custom-call | flops 10000000000 | bytes 10000000 | tf_op jit(solution)/shard_map/stage1_high/pallas_call | solution.py:470
  107.3 1.2 copy-done.17
  108.5 4.7 %collective-permute-start.18 = (f32[6,8,8,128]{3,2,1,0:T(8,128)S(1)}, f32[6,8,8,128]{3,2,1,0:T(8,128)S(1)}, u32[]{:S(2)}, u32[]{:S(2)}) collective-permute-start(f32[6,8,8,128]{3,2,1,0:T(8,128)S(1)} %get-tuple-element.106), channel_id=1, source_target_pairs={{0,7},{1,0},{2,1},{3,2},{4,3},{5,4},{6,5},{7,6},{8,15},{9,8},{10,9... | collective-permute-start | bytes 589832 | tf_op jit(solution)/shard_map/ppermute | solution.py:488
  113.5 1.6 copy-done.4
  115.1 1.0 stage0_ends.1
  116.1 6.2 %collective-permute-start.11 = (f32[6,4,8,128]{3,2,1,0:T(8,128)S(1)}, f32[6,4,8,128]{3,2,1,0:T(8,128)S(1)}, u32[]{:S(2)}, u32[]{:S(2)}) collective-permute-start(f32[6,4,8,128]{3,2,1,0:T(8,128)S(1)} %get-tuple-element.93), channel_id=1, source_target_pairs={{0,1},{1,2},{2,3},{3,4},{4,5},{5,6},{6,7},{7,0},{8,9},{9,10},{10,1... | collective-permute-start | bytes 294920 | tf_op jit(solution)/shard_map/ppermute | solution.py:488
  122.4 3.4 %stage2_low.1 = (f32[6,32,16,128]{3,2,1,0:T(8,128)S(1)}, f32[6,8,8,128]{3,2,1,0:T(8,128)S(1)}, f32[6,8,8,128]{3,2,1,0:T(8,128)S(1)}, f32[8,128]{1,0:T(8,128)S(1)}) custom-call(f32[6]{0:T(128)S(1)} %copy-done.7, f32[1]{0:T(128)S(6)} %copy.12.swirl, f32[6]{0:T(128)S(1)} %copy-done.8, f32[6,6]{1,0:T(8,128)S(1)} %copy-done.5, f32[6,64,16,128]{3,2,1,0:T(8,128)S(1)} %copy-done.4, ...), custom_call_target="tpu_custom_call" | custom-call | flops 10000000000 | bytes 10000000 | tf_op jit(solution)/shard_map/stage2_low/pallas_call | solution.py:470
  125.8 2.1 %collective-permute-start.23 = (f32[6,8,8,128]{3,2,1,0:T(8,128)S(1)}, f32[6,8,8,128]{3,2,1,0:T(8,128)S(1)}, u32[]{:S(2)}, u32[]{:S(2)}) collective-permute-start(f32[6,8,8,128]{3,2,1,0:T(8,128)S(1)} %get-tuple-element.115), channel_id=1, source_target_pairs={{0,1},{1,2},{2,3},{3,4},{4,5},{5,6},{6,7},{7,0},{8,9},{9,10},{10,1... | collective-permute-start | bytes 589832 | tf_op jit(solution)/shard_map/ppermute | solution.py:488
  127.8 2.7 %collective-permute-start.24 = (f32[6,8,8,128]{3,2,1,0:T(8,128)S(1)}, f32[6,8,8,128]{3,2,1,0:T(8,128)S(1)}, u32[]{:S(2)}, u32[]{:S(2)}) collective-permute-start(f32[6,8,8,128]{3,2,1,0:T(8,128)S(1)} %get-tuple-element.116), channel_id=1, source_target_pairs={{0,7},{1,0},{2,1},{3,2},{4,3},{5,4},{6,5},{7,6},{8,15},{9,8},{10,9... | collective-permute-start | bytes 589832 | tf_op jit(solution)/shard_map/ppermute | solution.py:488
  130.5 1.3 stage1_ends.1
  131.9 4.7 %collective-permute-start.16 = (f32[6,4,8,128]{3,2,1,0:T(8,128)S(1)}, f32[6,4,8,128]{3,2,1,0:T(8,128)S(1)}, u32[]{:S(2)}, u32[]{:S(2)}) collective-permute-start(f32[6,4,8,128]{3,2,1,0:T(8,128)S(1)} %get-tuple-element.104), channel_id=1, source_target_pairs={{0,7},{1,0},{2,1},{3,2},{4,3},{5,4},{6,5},{7,6},{8,15},{9,8},{10,9... | collective-permute-start | bytes 294920 | tf_op jit(solution)/shard_map/ppermute | solution.py:488
  136.6 3.4 %stage2_high.1 = (f32[6,32,16,128]{3,2,1,0:T(8,128)S(1)}, f32[6,8,8,128]{3,2,1,0:T(8,128)S(1)}, f32[6,8,8,128]{3,2,1,0:T(8,128)S(1)}, f32[8,128]{1,0:T(8,128)S(1)}) custom-call(f32[6]{0:T(128)S(1)} %copy-done.7, f32[1]{0:T(128)S(6)} %copy.12.swirl, f32[6]{0:T(128)S(1)} %copy-done.8, f32[6,6]{1,0:T(8,128)S(1)} %copy-done.5, f32[6,64,16,128]{3,2,1,0:T(8,128)S(1)} %copy-done.4, ...), custom_call_target="tpu_custom_call" | custom-call | flops 10000000000 | bytes 10000000 | tf_op jit(solution)/shard_map/stage2_high/pallas_call | solution.py:470
  140.8 3.9 %collective-permute-start.22 = (f32[6,8,8,128]{3,2,1,0:T(8,128)S(1)}, f32[6,8,8,128]{3,2,1,0:T(8,128)S(1)}, u32[]{:S(2)}, u32[]{:S(2)}) collective-permute-start(f32[6,8,8,128]{3,2,1,0:T(8,128)S(1)} %get-tuple-element.114), channel_id=1, source_target_pairs={{0,7},{1,0},{2,1},{3,2},{4,3},{5,4},{6,5},{7,6},{8,15},{9,8},{10,9... | collective-permute-start | bytes 589832 | tf_op jit(solution)/shard_map/ppermute | solution.py:488
  144.8 1.5 stage2_ends.1
  146.4 4.7 %collective-permute-start.20 = (f32[6,4,8,128]{3,2,1,0:T(8,128)S(1)}, f32[6,4,8,128]{3,2,1,0:T(8,128)S(1)}, u32[]{:S(2)}, u32[]{:S(2)}) collective-permute-start(f32[6,4,8,128]{3,2,1,0:T(8,128)S(1)} %get-tuple-element.112), channel_id=1, source_target_pairs={{0,7},{1,0},{2,1},{3,2},{4,3},{5,4},{6,5},{7,6},{8,15},{9,8},{10,9... | collective-permute-start | bytes 294920 | tf_op jit(solution)/shard_map/ppermute | solution.py:488
  151.1 4.5 %stage3_low.1 = (f32[6,64,16,128]{3,2,1,0:T(8,128)}, f32[8,128]{1,0:T(8,128)S(1)}) custom-call(f32[6]{0:T(128)S(1)} %copy-done.7, f32[1]{0:T(128)S(6)} %copy.12.swirl, f32[6]{0:T(128)S(1)} %copy-done.8, f32[6,6]{1,0:T(8,128)S(1)} %copy-done.5, f32[6,64,16,128]{3,2,1,0:T(8,128)S(1)} %copy-done.4, ...), custom_call_target="tpu_custom_call" | custom-call | flops 10000000000 | bytes 10000000 | tf_op jit(solution)/shard_map/stage3_low/pallas_call | solution.py:470
  155.6 4.5 %stage3_high.1 = (f32[6,64,16,128]{3,2,1,0:T(8,128)}, f32[8,128]{1,0:T(8,128)S(1)}) custom-call(f32[6]{0:T(128)S(1)} %copy-done.7, f32[1]{0:T(128)S(6)} %copy.12.swirl, f32[6]{0:T(128)S(1)} %copy-done.8, f32[6,6]{1,0:T(8,128)S(1)} %copy-done.5, f32[6,64,16,128]{3,2,1,0:T(8,128)S(1)} %copy-done.4, ...), custom_call_target="tpu_custom_call", output_to_operand_aliasing={{0}: (12, {})} | custom-call | flops 10000000000 | bytes 10000000 | tf_op jit(solution)/shard_map/stage3_high/pallas_call | solution.py:470
  160.1 3.9 %stage3_ends.1 = (f32[6,64,16,128]{3,2,1,0:T(8,128)}, f32[8,128]{1,0:T(8,128)}) custom-call(f32[6]{0:T(128)S(1)} %copy-done.7, f32[1]{0:T(128)S(6)} %copy.12.swirl, f32[6]{0:T(128)S(1)} %copy-done.8, f32[6,6]{1,0:T(8,128)S(1)} %copy-done.5, f32[6,64,16,128]{3,2,1,0:T(8,128)S(1)} %copy-done.4, ...), custom_call_target="tpu_custom_call", output_to_operand_aliasing={{0}: (22, {})} | custom-call | flops 10000000000 | bytes 10000000 | tf_op jit(solution)/shard_map/stage3_ends/pallas_call | solution.py:470
  (66 shorter events, 1.8 us)
Async XLA Ops:
  1.0 9.7 %collective-permute-start = (f32[6,8,16,128]{3,2,1,0:T(8,128)S(1)}, f32[6,8,16,128]{3,2,1,0:T(8,128)S(1)}, u32[]{:S(2)}, u32[]{:S(2)}) collective-permute-start(f32[6,8,16,128]{3,2,1,0:T(8,128)S(1)} %slice.3), channel_id=1, source_target_pairs={{8,0},{16,8},{24,16},{9,1},{17,9},{25,17},{10,2},{18,10},{26,18},{... | collective-permute-start | bytes 1179656 | tf_op jit(solution)/shard_map/ppermute | solution.py:500
  2.3 1.9 %copy-start = (f32[6,64,16,128]{3,2,1,0:T(8,128)S(1)}, f32[6,64,16,128]{3,2,1,0:T(8,128)}, u32[]{:S(2)}) copy-start(f32[6,64,16,128]{3,2,1,0:T(8,128)} %refs_0_.23) | copy-start | bytes 9437188
  4.6 12.4 %collective-permute-start.1 = (f32[6,8,8,128]{3,2,1,0:T(8,128)S(1)}, f32[6,8,8,128]{3,2,1,0:T(8,128)S(1)}, u32[]{:S(2)}, u32[]{:S(2)}) collective-permute-start(f32[6,8,8,128]{3,2,1,0:T(8,128)S(1)} %get-tuple-element.68), channel_id=1, source_target_pairs={{0,1},{1,2},{2,3},{3,4},{4,5},{5,6},{6,7},{7,0},{8,9},{9,10},{10,1... | collective-permute-start | bytes 589832 | tf_op jit(solution)/shard_map/ppermute | solution.py:488
  7.6 11.9 %collective-permute-start.2 = (f32[6,8,8,128]{3,2,1,0:T(8,128)S(1)}, f32[6,8,8,128]{3,2,1,0:T(8,128)S(1)}, u32[]{:S(2)}, u32[]{:S(2)}) collective-permute-start(f32[6,8,8,128]{3,2,1,0:T(8,128)S(1)} %get-tuple-element.69), channel_id=1, source_target_pairs={{0,7},{1,0},{2,1},{3,2},{4,3},{5,4},{6,5},{7,6},{8,15},{9,8},{10,9... | collective-permute-start | bytes 589832 | tf_op jit(solution)/shard_map/ppermute | solution.py:488
  12.2 13.6 %copy-start.19 = (f32[16,16,32]{2,1,0:T(8,128)S(1)}, f32[16,16,32]{2,1,0:T(8,128)}, u32[]{:S(2)}) copy-start(f32[16,16,32]{2,1,0:T(8,128)} %param.8) | copy-start | bytes 98308
  12.2 13.7 %copy-start.5 = (f32[6,6]{1,0:T(8,128)S(1)}, f32[6,6]{1,0:T(8,128)}, u32[]{:S(2)}) copy-start(f32[6,6]{1,0:T(8,128)} %coupling.25) | copy-start | bytes 436
  12.2 13.7 %copy-start.7 = (f32[6]{0:T(128)S(1)}, f32[6]{0:T(128)}, u32[]{:S(2)}) copy-start(f32[6]{0:T(128)} %speed.25) | copy-start | bytes 76
  12.2 13.7 %copy-start.8 = (f32[6]{0:T(128)S(1)}, f32[6]{0:T(128)}, u32[]{:S(2)}) copy-start(f32[6]{0:T(128)} %diffusion.25) | copy-start | bytes 76
  19.5 34.4 %all-to-all-start = ((f32[8,12,24,128]{3,2,1,0:T(8,128)}), f32[8,12,24,128]{3,2,1,0:T(8,128)S(1)}, u32[]{:S(2)}, u32[]{:S(2)}) async-start(f32[8,12,24,128]{3,2,1,0:T(8,128)} %pack_zone.1), calls=%async_computation | async-start | bytes 2359296 | tf_op jit(solution)/shard_map/all_to_all | solution.py:508
  23.9 18.4 %collective-permute-start.5 = (f32[1]{0:T(128)}, f32[1]{0:T(128)}, u32[]{:S(2)}, u32[]{:S(2)}) collective-permute-start(f32[1]{0:T(128)} %param.11), channel_id=1, source_target_pairs={{8,0},{16,8},{24,16},{9,1},{17,9},{25,17},{10,2},{18,10},{26,18},{... | collective-permute-start | bytes 20 | tf_op jit(solution)/shard_map/ppermute | solution.py:501
  25.9 1.9 %copy-start.1 = (f32[6,64,16,128]{3,2,1,0:T(8,128)S(1)}, f32[6,64,16,128]{3,2,1,0:T(8,128)}, u32[]{:S(2)}) copy-start(f32[6,64,16,128]{3,2,1,0:T(8,128)} %refs_0_.23) | copy-start | bytes 9437188
  27.8 26.1 %copy-start.6 = (s32[4,3]{1,0:T(4,128)S(1)}, s32[4,3]{1,0:T(4,128)}, u32[]{:S(2)}) copy-start(s32[4,3]{1,0:T(4,128)} %offsets.1) | copy-start | bytes 148
  31.6 1.2 copy-start.9
  32.8 36.1 %collective-permute-start.3 = (f32[6,8,8,128]{3,2,1,0:T(8,128)S(1)}, f32[6,8,8,128]{3,2,1,0:T(8,128)S(1)}, u32[]{:S(2)}, u32[]{:S(2)}) collective-permute-start(f32[6,8,8,128]{3,2,1,0:T(8,128)S(1)} %get-tuple-element.73), channel_id=1, source_target_pairs={{0,1},{1,2},{2,3},{3,4},{4,5},{5,6},{6,7},{7,0},{8,9},{9,10},{10,1... | collective-permute-start | bytes 589832 | tf_op jit(solution)/shard_map/ppermute | solution.py:488
  34.8 34.1 %collective-permute-start.4 = (f32[6,8,8,128]{3,2,1,0:T(8,128)S(1)}, f32[6,8,8,128]{3,2,1,0:T(8,128)S(1)}, u32[]{:S(2)}, u32[]{:S(2)}) collective-permute-start(f32[6,8,8,128]{3,2,1,0:T(8,128)S(1)} %get-tuple-element.74), channel_id=1, source_target_pairs={{0,7},{1,0},{2,1},{3,2},{4,3},{5,4},{6,5},{7,6},{8,15},{9,8},{10,9... | collective-permute-start | bytes 589832 | tf_op jit(solution)/shard_map/ppermute | solution.py:488
  37.5 50.7 %collective-permute-start.9 = (f32[6,8,8,128]{3,2,1,0:T(8,128)S(1)}, f32[6,8,8,128]{3,2,1,0:T(8,128)S(1)}, u32[]{:S(2)}, u32[]{:S(2)}) collective-permute-start(f32[6,8,8,128]{3,2,1,0:T(8,128)S(1)} %get-tuple-element.86), channel_id=1, source_target_pairs={{0,1},{1,2},{2,3},{3,4},{4,5},{5,6},{6,7},{7,0},{8,9},{9,10},{10,1... | collective-permute-start | bytes 589832 | tf_op jit(solution)/shard_map/ppermute | solution.py:488
  37.5 50.7 %collective-permute-start.10 = (f32[6,8,8,128]{3,2,1,0:T(8,128)S(1)}, f32[6,8,8,128]{3,2,1,0:T(8,128)S(1)}, u32[]{:S(2)}, u32[]{:S(2)}) collective-permute-start(f32[6,8,8,128]{3,2,1,0:T(8,128)S(1)} %get-tuple-element.87), channel_id=1, source_target_pairs={{0,7},{1,0},{2,1},{3,2},{4,3},{5,4},{6,5},{7,6},{8,15},{9,8},{10,9... | collective-permute-start | bytes 589832 | tf_op jit(solution)/shard_map/ppermute | solution.py:488
  53.9 15.0 %copy-start.2 = (f32[6,64,16,128]{3,2,1,0:T(8,128)S(1)}, f32[6,64,16,128]{3,2,1,0:T(8,128)}, u32[]{:S(2)}) copy-start(f32[6,64,16,128]{3,2,1,0:T(8,128)} %refs_0_.23) | copy-start | bytes 9437188
  67.5 14.6 %collective-permute-start.6 = (f32[8,6,16,128]{3,2,1,0:T(8,128)S(1)}, f32[8,6,16,128]{3,2,1,0:T(8,128)S(1)}, u32[]{:S(2)}, u32[]{:S(2)}) collective-permute-start(f32[8,6,16,128]{3,2,1,0:T(8,128)S(1)} %get-tuple-element.77), channel_id=1, source_target_pairs={{0,8},{8,16},{16,24},{1,9},{9,17},{17,25},{2,10},{10,18},{18,26},{... | collective-permute-start | bytes 1179656 | tf_op jit(solution)/shard_map/ppermute | solution.py:530
  73.4 9.7 %copy-start.12 = (f32[6,32,16,128]{3,2,1,0:T(8,128)}, f32[6,32,16,128]{3,2,1,0:T(8,128)S(1)}, u32[]{:S(2)}) copy-start(f32[6,32,16,128]{3,2,1,0:T(8,128)S(1)} %get-tuple-element.84.refs_3_.refs_8_) | copy-start | bytes 4718596
  73.4 29.8 %collective-permute-start.7 = (f32[6,8,8,128]{3,2,1,0:T(8,128)}, f32[6,8,8,128]{3,2,1,0:T(8,128)S(1)}, u32[]{:S(2)}, u32[]{:S(2)}) collective-permute-start(f32[6,8,8,128]{3,2,1,0:T(8,128)} %get-tuple-element.82), channel_id=1, source_target_pairs={{0,1},{1,2},{2,3},{3,4},{4,5},{5,6},{6,7},{7,0},{8,9},{9,10},{10,1... | collective-permute-start | bytes 589832 | tf_op jit(solution)/shard_map/ppermute | solution.py:488
  82.1 21.0 %collective-permute-start.8 = (f32[6,8,8,128]{3,2,1,0:T(8,128)S(1)}, f32[6,8,8,128]{3,2,1,0:T(8,128)S(1)}, u32[]{:S(2)}, u32[]{:S(2)}) collective-permute-start(f32[6,8,8,128]{3,2,1,0:T(8,128)S(1)} %get-tuple-element.83), channel_id=1, source_target_pairs={{0,7},{1,0},{2,1},{3,2},{4,3},{5,4},{6,5},{7,6},{8,15},{9,8},{10,9... | collective-permute-start | bytes 589832 | tf_op jit(solution)/shard_map/ppermute | solution.py:488
  83.1 30.2 %all-to-all-start.1 = ((f32[8,12,16,128]{3,2,1,0:T(8,128)}), f32[8,12,16,128]{3,2,1,0:T(8,128)S(1)}, u32[]{:S(2)}, u32[]{:S(2)}) async-start(f32[8,12,16,128]{3,2,1,0:T(8,128)} %pad_maximum_fusion), calls=%async_computation.1 | async-start | bytes 1572864 | tf_op jit(solution)/shard_map/all_to_all | solution.py:533
  88.2 1.9 %copy-start.3 = (f32[6,64,16,128]{3,2,1,0:T(8,128)S(1)}, f32[6,64,16,128]{3,2,1,0:T(8,128)}, u32[]{:S(2)}) copy-start(f32[6,64,16,128]{3,2,1,0:T(8,128)} %refs_0_.23) | copy-start | bytes 9437188
  90.1 1.4 copy-start.10
  91.5 1.4 copy-start.13
  97.3 1.1 copy-start.15
  98.4 23.9 %collective-permute-start.13 = (f32[6,8,8,128]{3,2,1,0:T(8,128)}, f32[6,8,8,128]{3,2,1,0:T(8,128)S(1)}, u32[]{:S(2)}, u32[]{:S(2)}) collective-permute-start(f32[6,8,8,128]{3,2,1,0:T(8,128)} %get-tuple-element.97), channel_id=1, source_target_pairs={{0,1},{1,2},{2,3},{3,4},{4,5},{5,6},{6,7},{7,0},{8,9},{9,10},{10,1... | collective-permute-start | bytes 589832 | tf_op jit(solution)/shard_map/ppermute | solution.py:488
  100.4 21.9 %collective-permute-start.14 = (f32[6,8,8,128]{3,2,1,0:T(8,128)}, f32[6,8,8,128]{3,2,1,0:T(8,128)S(1)}, u32[]{:S(2)}, u32[]{:S(2)}) collective-permute-start(f32[6,8,8,128]{3,2,1,0:T(8,128)} %get-tuple-element.98), channel_id=1, source_target_pairs={{0,7},{1,0},{2,1},{3,2},{4,3},{5,4},{6,5},{7,6},{8,15},{9,8},{10,9... | collective-permute-start | bytes 589832 | tf_op jit(solution)/shard_map/ppermute | solution.py:488
  107.3 1.2 copy-start.17
  108.5 23.4 %collective-permute-start.17 = (f32[6,8,8,128]{3,2,1,0:T(8,128)}, f32[6,8,8,128]{3,2,1,0:T(8,128)S(1)}, u32[]{:S(2)}, u32[]{:S(2)}) collective-permute-start(f32[6,8,8,128]{3,2,1,0:T(8,128)} %get-tuple-element.105), channel_id=1, source_target_pairs={{0,1},{1,2},{2,3},{3,4},{4,5},{5,6},{6,7},{7,0},{8,9},{9,10},{10,1... | collective-permute-start | bytes 589832 | tf_op jit(solution)/shard_map/ppermute | solution.py:488
  108.5 28.1 %collective-permute-start.18 = (f32[6,8,8,128]{3,2,1,0:T(8,128)S(1)}, f32[6,8,8,128]{3,2,1,0:T(8,128)S(1)}, u32[]{:S(2)}, u32[]{:S(2)}) collective-permute-start(f32[6,8,8,128]{3,2,1,0:T(8,128)S(1)} %get-tuple-element.106), channel_id=1, source_target_pairs={{0,7},{1,0},{2,1},{3,2},{4,3},{5,4},{6,5},{7,6},{8,15},{9,8},{10,9... | collective-permute-start | bytes 589832 | tf_op jit(solution)/shard_map/ppermute | solution.py:488
  113.2 1.9 %copy-start.4 = (f32[6,64,16,128]{3,2,1,0:T(8,128)S(1)}, f32[6,64,16,128]{3,2,1,0:T(8,128)}, u32[]{:S(2)}) copy-start(f32[6,64,16,128]{3,2,1,0:T(8,128)} %refs_0_.23) | copy-start | bytes 9437188
  115.1 7.2 %copy-start.16 = (f32[6,32,16,128]{3,2,1,0:T(8,128)S(1)}, f32[6,32,16,128]{3,2,1,0:T(8,128)}, u32[]{:S(2)}) copy-start(f32[6,32,16,128]{3,2,1,0:T(8,128)} %copy-done.15) | copy-start | bytes 4718596
  115.1 7.2 %copy-start.18 = (f32[6,32,16,128]{3,2,1,0:T(8,128)S(1)}, f32[6,32,16,128]{3,2,1,0:T(8,128)}, u32[]{:S(2)}) copy-start(f32[6,32,16,128]{3,2,1,0:T(8,128)} %copy-done.17) | copy-start | bytes 4718596
  116.1 11.7 %collective-permute-start.11 = (f32[6,4,8,128]{3,2,1,0:T(8,128)S(1)}, f32[6,4,8,128]{3,2,1,0:T(8,128)S(1)}, u32[]{:S(2)}, u32[]{:S(2)}) collective-permute-start(f32[6,4,8,128]{3,2,1,0:T(8,128)S(1)} %get-tuple-element.93), channel_id=1, source_target_pairs={{0,1},{1,2},{2,3},{3,4},{4,5},{5,6},{6,7},{7,0},{8,9},{9,10},{10,1... | collective-permute-start | bytes 294920 | tf_op jit(solution)/shard_map/ppermute | solution.py:488
  122.3 8.2 %collective-permute-start.12 = (f32[6,4,8,128]{3,2,1,0:T(8,128)S(1)}, f32[6,4,8,128]{3,2,1,0:T(8,128)S(1)}, u32[]{:S(2)}, u32[]{:S(2)}) collective-permute-start(f32[6,4,8,128]{3,2,1,0:T(8,128)S(1)} %get-tuple-element.94), channel_id=1, source_target_pairs={{0,7},{1,0},{2,1},{3,2},{4,3},{5,4},{6,5},{7,6},{8,15},{9,8},{10,9... | collective-permute-start | bytes 294920 | tf_op jit(solution)/shard_map/ppermute | solution.py:488
  122.4 8.2 %copy-start.11 = (f32[6,32,16,128]{3,2,1,0:T(8,128)S(1)}, f32[6,32,16,128]{3,2,1,0:T(8,128)}, u32[]{:S(2)}) copy-start(f32[6,32,16,128]{3,2,1,0:T(8,128)} %copy-done.9) | copy-start | bytes 4718596
  122.4 8.2 %copy-start.14 = (f32[6,32,16,128]{3,2,1,0:T(8,128)S(1)}, f32[6,32,16,128]{3,2,1,0:T(8,128)}, u32[]{:S(2)}) copy-start(f32[6,32,16,128]{3,2,1,0:T(8,128)} %copy-done.12) | copy-start | bytes 4718596
  125.8 20.6 %collective-permute-start.23 = (f32[6,8,8,128]{3,2,1,0:T(8,128)S(1)}, f32[6,8,8,128]{3,2,1,0:T(8,128)S(1)}, u32[]{:S(2)}, u32[]{:S(2)}) collective-permute-start(f32[6,8,8,128]{3,2,1,0:T(8,128)S(1)} %get-tuple-element.115), channel_id=1, source_target_pairs={{0,1},{1,2},{2,3},{3,4},{4,5},{5,6},{6,7},{7,0},{8,9},{9,10},{10,1... | collective-permute-start | bytes 589832 | tf_op jit(solution)/shard_map/ppermute | solution.py:488
  127.8 23.2 %collective-permute-start.24 = (f32[6,8,8,128]{3,2,1,0:T(8,128)S(1)}, f32[6,8,8,128]{3,2,1,0:T(8,128)S(1)}, u32[]{:S(2)}, u32[]{:S(2)}) collective-permute-start(f32[6,8,8,128]{3,2,1,0:T(8,128)S(1)} %get-tuple-element.116), channel_id=1, source_target_pairs={{0,7},{1,0},{2,1},{3,2},{4,3},{5,4},{6,5},{7,6},{8,15},{9,8},{10,9... | collective-permute-start | bytes 589832 | tf_op jit(solution)/shard_map/ppermute | solution.py:488
  131.8 9.0 %collective-permute-start.15 = (f32[6,4,8,128]{3,2,1,0:T(8,128)S(1)}, f32[6,4,8,128]{3,2,1,0:T(8,128)S(1)}, u32[]{:S(2)}, u32[]{:S(2)}) collective-permute-start(f32[6,4,8,128]{3,2,1,0:T(8,128)S(1)} %get-tuple-element.103), channel_id=1, source_target_pairs={{0,1},{1,2},{2,3},{3,4},{4,5},{5,6},{6,7},{7,0},{8,9},{9,10},{10,1... | collective-permute-start | bytes 294920 | tf_op jit(solution)/shard_map/ppermute | solution.py:488
  131.9 12.9 %collective-permute-start.16 = (f32[6,4,8,128]{3,2,1,0:T(8,128)S(1)}, f32[6,4,8,128]{3,2,1,0:T(8,128)S(1)}, u32[]{:S(2)}, u32[]{:S(2)}) collective-permute-start(f32[6,4,8,128]{3,2,1,0:T(8,128)S(1)} %get-tuple-element.104), channel_id=1, source_target_pairs={{0,7},{1,0},{2,1},{3,2},{4,3},{5,4},{6,5},{7,6},{8,15},{9,8},{10,9... | collective-permute-start | bytes 294920 | tf_op jit(solution)/shard_map/ppermute | solution.py:488
  140.0 15.6 %collective-permute-start.21 = (f32[6,8,8,128]{3,2,1,0:T(8,128)S(1)}, f32[6,8,8,128]{3,2,1,0:T(8,128)S(1)}, u32[]{:S(2)}, u32[]{:S(2)}) collective-permute-start(f32[6,8,8,128]{3,2,1,0:T(8,128)S(1)} %get-tuple-element.113), channel_id=1, source_target_pairs={{0,1},{1,2},{2,3},{3,4},{4,5},{5,6},{6,7},{7,0},{8,9},{9,10},{10,1... | collective-permute-start | bytes 589832 | tf_op jit(solution)/shard_map/ppermute | solution.py:488
  140.8 14.8 %collective-permute-start.22 = (f32[6,8,8,128]{3,2,1,0:T(8,128)S(1)}, f32[6,8,8,128]{3,2,1,0:T(8,128)S(1)}, u32[]{:S(2)}, u32[]{:S(2)}) collective-permute-start(f32[6,8,8,128]{3,2,1,0:T(8,128)S(1)} %get-tuple-element.114), channel_id=1, source_target_pairs={{0,7},{1,0},{2,1},{3,2},{4,3},{5,4},{6,5},{7,6},{8,15},{9,8},{10,9... | collective-permute-start | bytes 589832 | tf_op jit(solution)/shard_map/ppermute | solution.py:488
  146.3 13.8 %collective-permute-start.19 = (f32[6,4,8,128]{3,2,1,0:T(8,128)S(1)}, f32[6,4,8,128]{3,2,1,0:T(8,128)S(1)}, u32[]{:S(2)}, u32[]{:S(2)}) collective-permute-start(f32[6,4,8,128]{3,2,1,0:T(8,128)S(1)} %get-tuple-element.111), channel_id=1, source_target_pairs={{0,1},{1,2},{2,3},{3,4},{4,5},{5,6},{6,7},{7,0},{8,9},{9,10},{10,1... | collective-permute-start | bytes 294920 | tf_op jit(solution)/shard_map/ppermute | solution.py:488
  146.4 13.8 %collective-permute-start.20 = (f32[6,4,8,128]{3,2,1,0:T(8,128)S(1)}, f32[6,4,8,128]{3,2,1,0:T(8,128)S(1)}, u32[]{:S(2)}, u32[]{:S(2)}) collective-permute-start(f32[6,4,8,128]{3,2,1,0:T(8,128)S(1)} %get-tuple-element.112), channel_id=1, source_target_pairs={{0,7},{1,0},{2,1},{3,2},{4,3},{5,4},{6,5},{7,6},{8,15},{9,8},{10,9... | collective-permute-start | bytes 294920 | tf_op jit(solution)/shard_map/ppermute | solution.py:488
